TPU v7x, 512 devices: a whole 4x8x8 slice. The times are simulated.
512 devices in a mesh: ctx: 32 (over z, x), head: 16 (over y, core).
Axes of the slice: x: 4, y: 8, z: 8, core: 2. Of those that a mesh axis runs over, the one named last changes fastest.
Arguments:
- queries: bfloat16 [16384, 4096], P('ctx', 'head'), may hold values from -6 to 6
- keys: bfloat16 [2, 16384, 4096], P(None, 'ctx', 'head'), may hold values from -6 to 6
- values: bfloat16 [2, 16384, 4096], P(None, 'ctx', 'head'), may hold values from -6 to 6
- betas: float32 [32, 2, 16384], P('head', None, 'ctx'), may hold values from 1.9 to 2
- gate: bfloat16 [16384, 4096], P('ctx', 'head'), may hold values from -6 to 6
- out_weight: bfloat16 [4096, 4096], P('head'), may hold values from -0.125 to 0.125
Outputs:
- mixed: bfloat16 [16384, 4096], P('ctx', 'head')
All inputs are finite; a program needn't handle non-finite values.
Results may differ from a plain program's by a relative error of at most 0.02.
Values may be sent and summed in bfloat16 or wider, within the bound.
No kernel may reach another device: no remote copies, remote signals or barrier semaphores. Data moves between devices by JAX's collectives and lax.ppermute only.
A program may use at most 64 MiB of HBM per device.

v0:
```python
import functools
import jax
import jax.numpy as jnp
from jax import lax
from jax.experimental import pallas as pl
from jax.experimental.pallas import tpu as pltpu
from jax.sharding import Mesh
from jax.sharding import PartitionSpec as P

F32 = jnp.float32
BF16 = jnp.bfloat16
HD = 128
SPAN = 64
CTX = ("ctx_0", "ctx_1")


def dot(a, b):
    return jnp.dot(a, b, preferred_element_type=F32)


def dot_nt(a, b):
    return lax.dot_general(a, b, (((1,), (1,)), ((), ())), preferred_element_type=F32)


def split(x):
    hi = x.astype(BF16)
    return hi, (x - hi.astype(F32)).astype(BF16)


def wide(x):
    return jnp.concatenate(split(x), axis=1)


def square(pair):
    return jnp.concatenate([pair, pair], axis=0)


def halves(x):
    n = x.shape[1] // 2
    return x[:, :n] + x[:, n:]


def local_kernel(group, q_ref, k_ref, v_ref, b_ref, ab_ref, l_ref, m_ref, lev_ref, p_ref):
    heads = q_ref.shape[1] // HD
    blocks = q_ref.shape[0] // SPAN
    sub = 2 * SPAN
    place_r = lax.broadcasted_iota(jnp.int32, (sub, sub), 0)
    place_c = lax.broadcasted_iota(jnp.int32, (sub, sub), 1)

    def order(p):
        return (p & ~31) + 2 * (p & 15) + ((p >> 4) & 1)

    s_r, s_c = order(place_r), order(place_c)
    apart = s_r ^ s_c
    level = jnp.zeros((sub, sub), jnp.int32)
    for bit in range(1, 7):
        level = level + (apart >= 2**bit).astype(jnp.int32)
    lev_ref[...] = jnp.where(s_r > s_c, level, -1)
    eye = (place_r == place_c).astype(F32)
    seen = (order(lax.broadcasted_iota(jnp.int32, (SPAN, sub), 1)) >> 1) <= lax.broadcasted_iota(
        jnp.int32, (SPAN, sub), 0
    )
    for h in range(heads):
        p_ref[h] = jnp.concatenate([eye, jnp.zeros((HD, HD), F32)], axis=1)

    def body(step, carry):
        probs = [(step * group + i, h) for i in range(group) for h in range(heads)]
        kb, vb, qb, sq, n, e, N, X = [], [], [], [], [], [], [], []
        for blk, h in probs:
            rows = [
                (j, pl.ds(pl.multiple_of(blk * SPAN + 16 * g, 16), 16))
                for g in range(SPAN // 16)
                for j in range(2)
            ]
            cols = slice(h * HD, (h + 1) * HD)
            kb.append(jnp.concatenate([k_ref[j, r, cols] for j, r in rows], axis=0))
            vb.append(jnp.concatenate([v_ref[j, r, cols] for j, r in rows], axis=0))
            qb.append(q_ref[pl.ds(pl.multiple_of(blk * SPAN, SPAN), SPAN), cols])
        num = range(len(probs))
        for i in num:
            blk, h = probs[i]
            both = dot_nt(jnp.concatenate([kb[i], qb[i]], axis=0), kb[i])
            gram = both[:sub]
            n2 = jnp.sum(gram * eye, axis=0, keepdims=True) + 1e-6
            beta = b_ref[pl.ds(h * blocks + blk, 1), :]
            e.append(beta / n2)
            n.append(jnp.sqrt(n2))
            sq.append((jnp.where(seen, both[sub:], 0.0) * e[i]).astype(BF16))
            N.append(jnp.where(lev_ref[...] >= 0, gram * e[i], 0.0))
            X.append(eye - jnp.where(lev_ref[...] == 0, N[i], 0.0))
        for lev in range(1, 7):
            xw = [wide(x) for x in X]
            Z = []
            for i in num:
                C = jnp.where(lev_ref[...] == lev, N[i], 0.0)
                Z.append(halves(dot(wide(C), square(xw[i]))))
            for i in num:
                X[i] = X[i] - halves(dot(xw[i], square(wide(Z[i]))))
        A, B, carry_q, loc = [], [], [], []
        for i in num:
            xw = wide(X[i])
            ke = wide(kb[i].T.astype(F32) * e[i])
            y = halves(dot(ke, square(xw)))
            A.append(eye - dot(wide(y), square(kb[i])))
            B.append(dot(wide(y * n[i]), square(vb[i])))
            zq = dot(sq[i], xw[:, :sub])
            carry_q.append((qb[i].astype(F32) - dot(zq.astype(BF16), kb[i])).astype(BF16))
            loc.append(dot((zq * n[i]).astype(BF16), vb[i]))
        for i in num:
            blk, h = probs[i]
            p = p_ref[h]
            ph, plo = split(p)
            lm = dot(carry_q[i], ph)
            rows = pl.ds(pl.multiple_of(blk * SPAN, SPAN), SPAN)
            cols = slice(h * HD, (h + 1) * HD)
            m_ref[rows, cols] = lm[:, :HD].astype(BF16)
            l_ref[rows, cols] = loc[i] + lm[:, HD:]
            aw = wide(A[i])
            new = dot(aw, square(ph)) + dot(aw[:, :HD], plo)
            p_ref[h] = new + jnp.concatenate([jnp.zeros((HD, HD), F32), B[i]], axis=1)
        return carry

    lax.fori_loop(0, blocks // group, body, 0)
    for h in range(heads):
        ab_ref[h] = p_ref[h].astype(BF16)


def local_maps(q, k, v, b_rows, group=2):
    tok, cols = q.shape
    heads = cols // HD
    return pl.pallas_call(
        functools.partial(local_kernel, group),
        out_shape=(
            jax.ShapeDtypeStruct((heads, HD, 2 * HD), BF16),
            jax.ShapeDtypeStruct((tok, cols), F32),
            jax.ShapeDtypeStruct((tok, cols), BF16),
        ),
        in_specs=[pl.BlockSpec(memory_space=pltpu.VMEM)] * 4,
        out_specs=[pl.BlockSpec(memory_space=pltpu.VMEM)] * 3,
        scratch_shapes=[
            pltpu.VMEM((2 * SPAN, 2 * SPAN), jnp.int32),
            pltpu.VMEM((heads, HD, 2 * HD), F32),
        ],
        compiler_params=pltpu.CompilerParams(vmem_limit_bytes=32 * 1024 * 1024),
    )(q, k, v, b_rows)


def beta_rows(betas):
    heads, _, tok = betas.shape
    blocks = tok // SPAN
    return (
        betas.reshape(heads, 2, blocks, SPAN // 16, 16)
        .transpose(0, 2, 3, 1, 4)
        .reshape(heads * blocks, 2 * SPAN)
    )


def affine(a, b):
    return jnp.concatenate([a, b], axis=1)


def fold_kernel(x_ref, m_ref, send_ref, tot_ref, in_ref):
    peers, heads = m_ref.shape[:2]
    x = x_ref[0]
    r = lax.broadcasted_iota(jnp.int32, (HD, 2 * HD), 0)
    c = lax.broadcasted_iota(jnp.int32, (HD, 2 * HD), 1)
    zero = jnp.zeros((HD, HD), F32)
    total = [m_ref[0, h].astype(F32) for h in range(heads)]
    inside = [(r == c).astype(F32)] * heads
    for k in range(1, peers):
        for h in range(heads):
            inside[h] = jnp.where(x == k, total[h], inside[h])
            later = m_ref[k, h]
            prod = halves(dot(later[:, :HD], jnp.concatenate(split(total[h]), axis=1)))
            total[h] = prod + affine(zero, later[:, HD:].astype(F32))
    for h in range(heads):
        send_ref[h] = total[h].astype(BF16)
        tot_ref[h] = total[h]
        in_ref[h] = inside[h]


def join_kernel(later_ref, earlier_ref, send_ref, out_ref):
    zero = jnp.zeros((HD, HD), F32)
    for h in range(later_ref.shape[0]):
        later = later_ref[h]
        out = dot(wide(later[:, :HD]), square(earlier_ref[h])) + affine(zero, later[:, HD:])
        send_ref[h] = out.astype(BF16)
        out_ref[h] = out


def carry_kernel(later_ref, earlier_ref, send_ref):
    for h in range(later_ref.shape[0]):
        later = later_ref[h]
        state = dot(wide(later[:, :HD]), square(earlier_ref[h][:, HD:])) + later[:, HD:]
        send_ref[h] = state.astype(BF16)


def entry_kernel(in_ref, near_ref, far_ref, out_ref):
    zero = jnp.zeros((HD, HD), F32)
    for h in range(in_ref.shape[0]):
        near = near_ref[h]
        both = dot(near[:, :HD], far_ref[h]) + affine(zero, near[:, HD:].astype(F32))
        inner = in_ref[h]
        bh, bl = split(both)
        lhs = wide(inner[:, :HD])
        out = dot(lhs, square(bh)) + dot(lhs[:, :HD], bl)
        out_ref[h] = out + affine(zero, inner[:, HD:])


def mix_kernel(entry_ref, state_ref, l_ref, m_ref, q_ref, g_ref, o_ref):
    for h in range(entry_ref.shape[0]):
        entry = entry_ref[h]
        start = dot(wide(entry[:, :HD]), square(state_ref[h])) + entry[:, HD:]
        cols = slice(h * HD, (h + 1) * HD)
        raw = l_ref[:, cols] + dot(m_ref[:, cols], start.astype(BF16))
        q = q_ref[:, cols].astype(F32)
        unit = lax.rsqrt(jnp.sum(q * q, axis=1, keepdims=True) + 1e-6)
        mean = jnp.mean(raw * raw, axis=1, keepdims=True) * (unit * unit)
        gate = g_ref[:, cols].astype(F32)
        silu = gate / (1.0 + jnp.exp(-gate))
        o_ref[:, cols] = (raw * (unit * lax.rsqrt(mean + 1e-6)) * silu).astype(BF16)


VM = pl.BlockSpec(memory_space=pltpu.VMEM)
SM = pl.BlockSpec(memory_space=pltpu.SMEM)


def small(kernel, outs, *args, specs=None):
    return pl.pallas_call(
        kernel,
        out_shape=outs,
        in_specs=specs or [VM] * len(args),
        out_specs=jax.tree.map(lambda _: VM, outs),
        compiler_params=pltpu.CompilerParams(vmem_limit_bytes=32 * 1024 * 1024),
    )(*args)


def project_kernel(own_at, mate_at, a_ref, b_ref, w_ref, x_ref, o_ref):
    o_ref[0] = (dot(a_ref[...], w_ref[...]) + dot(b_ref[...], x_ref[...])).astype(o_ref.dtype)


def project(own, mate, weight, mate_weight, own_at, mate_at):
    tok, cols = own.shape
    count = own_at.shape[0]
    full = pl.BlockSpec((tok, cols), lambda i, a, b: (0, 0))
    return pl.pallas_call(
        project_kernel,
        out_shape=jax.ShapeDtypeStruct((count, tok, cols), BF16),
        grid_spec=pltpu.PrefetchScalarGridSpec(
            num_scalar_prefetch=2,
            grid=(count,),
            in_specs=[
                full,
                full,
                pl.BlockSpec((cols, cols), lambda i, a, b: (0, a[i])),
                pl.BlockSpec((cols, cols), lambda i, a, b: (0, b[i])),
            ],
            out_specs=pl.BlockSpec((1, tok, cols), lambda i, a, b: (i, 0, 0)),
        ),
        compiler_params=pltpu.CompilerParams(vmem_limit_bytes=32 * 1024 * 1024),
    )(own_at, mate_at, own, mate, weight, mate_weight)


def per_device(queries, keys, values, betas, gate, out_weight):
    tok, cols = queries.shape
    heads = cols // HD
    devices = lax.axis_size("head")
    chips = devices // 2
    me = lax.axis_index("head")
    chip, core = me // 2, me % 2

    def shift(a, by):
        return lax.ppermute(a, "head", [(i, (i + 2 * by) % devices) for i in range(devices)])

    def mate(a):
        return lax.ppermute(a, "head", [(i, i ^ 1) for i in range(devices)])

    def later_z(a, by):
        groups = lax.axis_size("ctx_0")
        return lax.ppermute(a, "ctx_0", [(i, i + by) for i in range(groups - by)])

    maps, local, carry = local_maps(queries, keys, values, beta_rows(betas), 8)
    to_mate = lax.dynamic_index_in_dim(
        out_weight.reshape(cols, chips, 2, cols), 1 - core, 2, keepdims=False
    ).reshape(cols, chips * cols)
    mate_weight = mate(to_mate)

    wide_map = jax.ShapeDtypeStruct((heads, HD, 2 * HD), F32)
    wide_send = jax.ShapeDtypeStruct((heads, HD, 2 * HD), BF16)
    state_send = jax.ShapeDtypeStruct((heads, HD, HD), BF16)
    gathered = lax.all_gather(maps, "ctx_1")
    x = lax.axis_index("ctx_1").astype(jnp.int32).reshape(1)
    send, total, inside = small(
        fold_kernel, (wide_send, wide_map, wide_map), x, gathered, specs=[SM, VM]
    )
    near = later_z(send, 1)
    send, pair = small(join_kernel, (wide_send, wide_map), total, near)
    far = later_z(send, 2)
    send = small(carry_kernel, state_send, pair, far)
    state = later_z(send, 4)
    entry = small(entry_kernel, wide_map, inside, near, far)
    mixed_in = small(
        mix_kernel,
        jax.ShapeDtypeStruct((tok, cols), BF16),
        entry,
        state,
        local,
        carry,
        queries,
        gate,
    )
    mate_in = mate(mixed_in)

    half = chips // 2
    order = [half] + [s for k in range(half - 1, 0, -1) for s in (k, chips - k)] + [0]
    dest = (chip + jnp.array(order, jnp.int32)) % chips
    own_at, mate_at = 2 * dest + core, dest
    first = project(mixed_in, mate_in, out_weight, mate_weight, own_at[:1], mate_at[:1])[0]
    rest = project(mixed_in, mate_in, out_weight, mate_weight, own_at[1:], mate_at[1:])
    cut = tok // 2
    up = shift(first[:cut], 1)
    down = shift(first[cut:], -1)

    def add(*terms):
        return sum(t.astype(F32) for t in terms).astype(BF16)

    up = jnp.concatenate([add(rest[0, :cut], up), rest[0, cut:]], axis=0)
    down = jnp.concatenate([rest[1, :cut], add(rest[1, cut:], down)], axis=0)
    for k in range(1, half):
        up, down = shift(up, 1), shift(down, -1)
        if k < half - 1:
            up, down = add(rest[2 * k], up), add(rest[2 * k + 1], down)
    return add(rest[2 * half - 2], up, down)


def solution(mesh):
    z = mesh.shape["ctx"] // 4
    finer = Mesh(mesh.devices.reshape(z, 4, mesh.shape["head"]), ("ctx_0", "ctx_1", "head"))
    in_specs = (
        P(CTX, "head"),
        P(None, CTX, "head"),
        P(None, CTX, "head"),
        P("head", None, CTX),
        P(CTX, "head"),
        P("head", None),
    )
    return jax.shard_map(
        per_device, mesh=finer, in_specs=in_specs, out_specs=P(CTX, "head"), check_vma=False
    )
```

profile of v0, /device:TPU:6, one launch (start us, length us, event | category | flops | bytes accessed | tf_op | source)
XLA Modules:
  0.0 123.2 jit_solution(2129212235592049924)
XLA Ops:
  0.0 3.3 %reshape.35 = bf16[256,8,2,256]{3,2,1,0:T(2,128)(2,1)S(1)} reshape(bf16[256,4096]{1,0:T(8,128)(2,1)} %w_ref.3) | data formatting | bytes 4194304 | tf_op jit(solution)/shard_map/reshape | solution.py:284
  3.3 6.1 %dynamic-slice_reduce_fusion = bf16[256,8,256]{2,1,0:T(8,128)(2,1)S(1)} fusion(bf16[256,8,2,256]{3,2,1,0:T(2,128)(2,1)S(1)} %reshape.35, s32[]{:T(128)S(6)} %select_n.24), kind=kLoop, calls=%fused_computation | loop fusion | bytes 2097156 | tf_op jit(solution)/shard_map/jit(dynamic_index_in_dim)/dynamic_slice | solution.py:283
  9.5 0.0 copy-start.6
  9.5 0.0 copy-start.1
  9.5 0.0 copy-start.3
  9.5 0.0 copy-start.4
  9.5 1.3 %copy.13 = bf16[32,8,8,256]{3,1,2,0:T(8,128)(2,1)} copy(bf16[32,8,8,256]{3,2,1,0:T(8,128)(2,1)S(1)} %bitcast.55) | data formatting | bytes 2097152
  10.8 2.1 %collective-permute-start.4 = (bf16[256,2048]{1,0:T(8,128)(2,1)}, bf16[256,2048]{1,0:T(8,128)(2,1)S(1)}, u32[]{:S(2)}, u32[]{:S(2)}) collective-permute-start(bf16[256,2048]{1,0:T(8,128)(2,1)} %bitcast.22), channel_id=1, source_target_pairs={{0,1},{1,0},{2,3},{3,2},{4,5},{5,4},{6,7},{7,6},{8,9},{9,8},{10,11... | collective-permute-start | bytes 3145736 | tf_op jit(solution)/shard_map/ppermute | solution.py:276
  12.9 0.0 copy-done.6
  12.9 0.1 reshape.33
  13.1 0.1 copy.15
  13.1 0.1 reshape.34.b_ref
  13.2 0.0 copy-done.1
  13.2 0.0 copy-done.3
  13.3 0.0 copy-done.4
  13.3 0.0 copy-start.2
  13.3 0.0 copy-start.5
  13.3 9.2 %shard_map.73 = (bf16[2,128,256]{2,1,0:T(8,128)(2,1)S(1)}, f32[512,256]{1,0:T(8,128)S(1)}, bf16[512,256]{1,0:T(8,128)(2,1)S(1)}) custom-call(bf16[512,256]{1,0:T(8,128)(2,1)S(1)} %copy-done.1, bf16[2,512,256]{2,1,0:T(8,128)(2,1)S(1)} %copy-done.3, bf16[2,512,256]{2,1,0:T(8,128)(2,1)S(1)} %copy-done.4, f32[16,128]{1,0:T(8,128)S(1)} %reshape.34.b_ref), custom_call_target="tpu_custom_call" | custom-call | tf_op jit(solution)/shard_map/pallas_call | solution.py:131
  22.5 15.9 %all-gather = bf16[8,128,256]{2,1,0:T(8,128)(2,1)S(1)} all-gather(bf16[2,128,256]{2,1,0:T(8,128)(2,1)S(1)} %get-tuple-element.13), channel_id=2, replica_groups=mesh['ctx_0'=8,'ctx_1'=4,'head'=16] {'ctx_1'}, dimensions={0}, use_global_device_ids=true | all-gather | bytes 655360 | tf_op jit(solution)/shard_map/all_gather | solution.py:291
  38.4 0.6 shard_map.74
  39.1 0.0 copy-start.7
  39.1 0.0 copy-start
  39.1 1.9 %collective-permute-start = (bf16[2,128,256]{2,1,0:T(8,128)(2,1)S(1)}, bf16[2,128,256]{2,1,0:T(8,128)(2,1)S(1)}, u32[]{:S(2)}, u32[]{:S(2)}) collective-permute-start(bf16[2,128,256]{2,1,0:T(8,128)(2,1)S(1)} %get-tuple-element.15), channel_id=1, source_target_pairs={{0,64},{64,128},{128,192},{192,256},{256,320},{320,384},{384,448},... | collective-permute-start | bytes 393224 | tf_op jit(solution)/shard_map/ppermute | solution.py:280
  41.0 2.5 %collective-permute-done.earlier_ref.near_ref = bf16[2,128,256]{2,1,0:T(8,128)(2,1)S(1)} collective-permute-done((bf16[2,128,256]{2,1,0:T(8,128)(2,1)S(1)}, bf16[2,128,256]{2,1,0:T(8,128)(2,1)S(1)}, u32[]{:S(2)}, u32[]{:S(2)}) %collective-permute-start) | collective-permute-done | bytes 131104 | tf_op jit(solution)/shard_map/ppermute | solution.py:280
  43.5 0.2 shard_map.75
  43.7 6.2 %collective-permute-start.1 = (bf16[2,128,256]{2,1,0:T(8,128)(2,1)S(1)}, bf16[2,128,256]{2,1,0:T(8,128)(2,1)S(1)}, u32[]{:S(2)}, u32[]{:S(2)}) collective-permute-start(bf16[2,128,256]{2,1,0:T(8,128)(2,1)S(1)} %get-tuple-element.17), channel_id=1, source_target_pairs={{0,128},{64,192},{128,256},{192,320},{256,384},{320,448},{1,129},{... | collective-permute-start | bytes 393224 | tf_op jit(solution)/shard_map/ppermute | solution.py:280
  49.9 2.5 %collective-permute-done.1.far_ref.earlier_ref = bf16[2,128,256]{2,1,0:T(8,128)(2,1)S(1)} collective-permute-done((bf16[2,128,256]{2,1,0:T(8,128)(2,1)S(1)}, bf16[2,128,256]{2,1,0:T(8,128)(2,1)S(1)}, u32[]{:S(2)}, u32[]{:S(2)}) %collective-permute-start.1) | collective-permute-done | bytes 131104 | tf_op jit(solution)/shard_map/ppermute | solution.py:280
  52.4 0.2 shard_map.77
  52.6 12.6 %collective-permute-start.2 = (bf16[2,128,128]{2,1,0:T(8,128)(2,1)S(1)}, bf16[2,128,128]{2,1,0:T(8,128)(2,1)S(1)}, u32[]{:S(2)}, u32[]{:S(2)}) collective-permute-start(bf16[2,128,128]{2,1,0:T(8,128)(2,1)S(1)} %shard_map.77), channel_id=1, source_target_pairs={{0,256},{64,320},{128,384},{192,448},{1,257},{65,321},{129,385},{1... | collective-permute-start | bytes 196616 | tf_op jit(solution)/shard_map/ppermute | solution.py:280
  65.2 0.4 shard_map.76.entry_ref
  65.6 1.5 %collective-permute-done.2.state_ref = bf16[2,128,128]{2,1,0:T(8,128)(2,1)S(1)} collective-permute-done((bf16[2,128,128]{2,1,0:T(8,128)(2,1)S(1)}, bf16[2,128,128]{2,1,0:T(8,128)(2,1)S(1)}, u32[]{:S(2)}, u32[]{:S(2)}) %collective-permute-start.2) | collective-permute-done | bytes 65568 | tf_op jit(solution)/shard_map/ppermute | solution.py:280
  67.1 0.0 copy-done.2
  67.1 0.0 copy-done.5
  67.1 0.6 shard_map.78.a_ref
  67.7 1.9 %collective-permute-start.3 = (bf16[512,256]{1,0:T(8,128)(2,1)S(1)}, bf16[512,256]{1,0:T(8,128)(2,1)}, u32[]{:S(2)}, u32[]{:S(2)}) collective-permute-start(bf16[512,256]{1,0:T(8,128)(2,1)S(1)} %shard_map.78.a_ref), channel_id=1, source_target_pairs={{0,1},{1,0},{2,3},{3,2},{4,5},{5,4},{6,7},{7,6},{8,9},{9,8},{10,11... | collective-permute-start | bytes 786440 | tf_op jit(solution)/shard_map/ppermute | solution.py:276
  69.7 0.0 copy-done.7
  69.7 0.1 slice.51.own_at
  69.8 0.1 slice.52.mate_at
  69.9 1.4 %collective-permute-done.3.b_ref = bf16[512,256]{1,0:T(8,128)(2,1)} collective-permute-done((bf16[512,256]{1,0:T(8,128)(2,1)S(1)}, bf16[512,256]{1,0:T(8,128)(2,1)}, u32[]{:S(2)}, u32[]{:S(2)}) %collective-permute-start.3) | collective-permute-done | bytes 262176 | tf_op jit(solution)/shard_map/ppermute | solution.py:276
  71.3 0.0 collective-permute-done.4.x_ref
  71.3 0.0 copy-done
  71.3 1.3 %shard_map.80 = bf16[1,512,256]{2,1,0:T(8,128)(2,1)S(1)} custom-call(s32[1]{0:T(128)S(1)} %bitcast.53, s32[1]{0:T(128)S(1)} %bitcast.54, bf16[512,256]{1,0:T(8,128)(2,1)S(1)} %shard_map.78.a_ref, bf16[512,256]{1,0:T(8,128)(2,1)} %collective-permute-done.3.b_ref, bf16[256,4096]{1,0:T(8,128)(2,1)S(1)} %copy-done, ...), custom_call_target="tpu_custom_call" | custom-call | tf_op jit(solution)/shard_map/pallas_call | solution.py:246
  72.6 3.5 %collective-permute-start.5 = (bf16[256,256]{1,0:T(8,128)(2,1)S(1)}, bf16[256,256]{1,0:T(8,128)(2,1)S(1)}, u32[]{:S(2)}, u32[]{:S(2)}) collective-permute-start(bf16[256,256]{1,0:T(8,128)(2,1)S(1)} %get-tuple-element.29), channel_id=1, source_target_pairs={{0,2},{1,3},{2,4},{3,5},{4,6},{5,7},{6,8},{7,9},{8,10},{9,11},{10,... | collective-permute-start | bytes 393224 | tf_op jit(solution)/shard_map/ppermute | solution.py:273
  76.1 3.8 %collective-permute-start.9 = (bf16[256,256]{1,0:T(8,128)(2,1)S(1)}, bf16[256,256]{1,0:T(8,128)(2,1)S(1)}, u32[]{:S(2)}, u32[]{:S(2)}) collective-permute-start(bf16[256,256]{1,0:T(8,128)(2,1)S(1)} %get-tuple-element.30), channel_id=1, source_target_pairs={{0,14},{1,15},{2,0},{3,1},{4,2},{5,3},{6,4},{7,5},{8,6},{9,7},{10,... | collective-permute-start | bytes 393224 | tf_op jit(solution)/shard_map/ppermute | solution.py:273
  79.9 4.0 %shard_map.79 = bf16[7,512,256]{2,1,0:T(8,128)(2,1)S(1)} custom-call(s32[7]{0:T(128)S(1)} %slice.51.own_at, s32[7]{0:T(128)S(1)} %slice.52.mate_at, bf16[512,256]{1,0:T(8,128)(2,1)S(1)} %shard_map.78.a_ref, bf16[512,256]{1,0:T(8,128)(2,1)} %collective-permute-done.3.b_ref, bf16[256,4096]{1,0:T(8,128)(2,1)S(1)} %copy-done, ...), custom_call_target="tpu_custom_call" | custom-call | tf_op jit(solution)/shard_map/pallas_call | solution.py:246
  83.9 0.0 collective-permute-done.5
  83.9 0.0 collective-permute-done.9
  84.0 0.1 fusion.7
  84.1 2.8 %collective-permute-start.6 = (bf16[512,256]{1,0:T(8,128)(2,1)S(1)}, bf16[512,256]{1,0:T(8,128)(2,1)S(1)}, u32[]{:S(2)}, u32[]{:S(2)}) collective-permute-start(bf16[512,256]{1,0:T(8,128)(2,1)S(1)} %pad_maximum_fusion), channel_id=1, source_target_pairs={{0,2},{1,3},{2,4},{3,5},{4,6},{5,7},{6,8},{7,9},{8,10},{9,11},{10,... | collective-permute-start | bytes 786440 | tf_op jit(solution)/shard_map/ppermute | solution.py:273
  86.9 4.3 %collective-permute-start.10 = (bf16[512,256]{1,0:T(8,128)(2,1)S(1)}, bf16[512,256]{1,0:T(8,128)(2,1)S(1)}, u32[]{:S(2)}, u32[]{:S(2)}) collective-permute-start(bf16[512,256]{1,0:T(8,128)(2,1)S(1)} %pad_maximum_fusion.1), channel_id=1, source_target_pairs={{0,14},{1,15},{2,0},{3,1},{4,2},{5,3},{6,4},{7,5},{8,6},{9,7},{10,... | collective-permute-start | bytes 786440 | tf_op jit(solution)/shard_map/ppermute | solution.py:273
  91.2 4.1 %collective-permute-done.6 = bf16[512,256]{1,0:T(8,128)(2,1)S(1)} collective-permute-done((bf16[512,256]{1,0:T(8,128)(2,1)S(1)}, bf16[512,256]{1,0:T(8,128)(2,1)S(1)}, u32[]{:S(2)}, u32[]{:S(2)}) %collective-permute-start.6) | collective-permute-done | bytes 262176 | tf_op jit(solution)/shard_map/ppermute | solution.py:273
  95.2 0.1 fusion.2
  95.3 1.9 %collective-permute-start.7 = (bf16[512,256]{1,0:T(8,128)(2,1)S(1)}, bf16[512,256]{1,0:T(8,128)(2,1)S(1)}, u32[]{:S(2)}, u32[]{:S(2)}) collective-permute-start(bf16[512,256]{1,0:T(8,128)(2,1)S(1)} %fusion.2), channel_id=1, source_target_pairs={{0,2},{1,3},{2,4},{3,5},{4,6},{5,7},{6,8},{7,9},{8,10},{9,11},{10,... | collective-permute-start | bytes 786440 | tf_op jit(solution)/shard_map/ppermute | solution.py:273
  97.2 0.0 collective-permute-done.10
  97.2 8.4 %collective-permute-done.7 = bf16[512,256]{1,0:T(8,128)(2,1)S(1)} collective-permute-done((bf16[512,256]{1,0:T(8,128)(2,1)S(1)}, bf16[512,256]{1,0:T(8,128)(2,1)S(1)}, u32[]{:S(2)}, u32[]{:S(2)}) %collective-permute-start.7) | collective-permute-done | bytes 262176 | tf_op jit(solution)/shard_map/ppermute | solution.py:273
  105.6 0.1 fusion.3
  105.7 1.9 %collective-permute-start.11 = (bf16[512,256]{1,0:T(8,128)(2,1)S(1)}, bf16[512,256]{1,0:T(8,128)(2,1)S(1)}, u32[]{:S(2)}, u32[]{:S(2)}) collective-permute-start(bf16[512,256]{1,0:T(8,128)(2,1)S(1)} %get-tuple-element.24), channel_id=1, source_target_pairs={{0,14},{1,15},{2,0},{3,1},{4,2},{5,3},{6,4},{7,5},{8,6},{9,7},{10,... | collective-permute-start | bytes 786440 | tf_op jit(solution)/shard_map/ppermute | solution.py:273
  107.7 3.9 %collective-permute-start.8 = (bf16[512,256]{1,0:T(8,128)(2,1)S(1)}, bf16[512,256]{1,0:T(8,128)(2,1)S(1)}, u32[]{:S(2)}, u32[]{:S(2)}) collective-permute-start(bf16[512,256]{1,0:T(8,128)(2,1)S(1)} %get-tuple-element.23), channel_id=1, source_target_pairs={{0,2},{1,3},{2,4},{3,5},{4,6},{5,7},{6,8},{7,9},{8,10},{9,11},{10,... | collective-permute-start | bytes 786440 | tf_op jit(solution)/shard_map/ppermute | solution.py:273
  111.6 2.4 %collective-permute-done.11 = bf16[512,256]{1,0:T(8,128)(2,1)S(1)} collective-permute-done((bf16[512,256]{1,0:T(8,128)(2,1)S(1)}, bf16[512,256]{1,0:T(8,128)(2,1)S(1)}, u32[]{:S(2)}, u32[]{:S(2)}) %collective-permute-start.11) | collective-permute-done | bytes 262176 | tf_op jit(solution)/shard_map/ppermute | solution.py:273
  114.0 0.1 fusion.1
  114.1 3.3 %collective-permute-start.12 = (bf16[512,256]{1,0:T(8,128)(2,1)S(1)}, bf16[512,256]{1,0:T(8,128)(2,1)S(1)}, u32[]{:S(2)}, u32[]{:S(2)}) collective-permute-start(bf16[512,256]{1,0:T(8,128)(2,1)S(1)} %fusion.1), channel_id=1, source_target_pairs={{0,14},{1,15},{2,0},{3,1},{4,2},{5,3},{6,4},{7,5},{8,6},{9,7},{10,... | collective-permute-start | bytes 786440 | tf_op jit(solution)/shard_map/ppermute | solution.py:273
  117.4 0.0 collective-permute-done.8
  117.4 4.9 %collective-permute-done.12 = bf16[512,256]{1,0:T(8,128)(2,1)S(1)} collective-permute-done((bf16[512,256]{1,0:T(8,128)(2,1)S(1)}, bf16[512,256]{1,0:T(8,128)(2,1)S(1)}, u32[]{:S(2)}, u32[]{:S(2)}) %collective-permute-start.12) | collective-permute-done | bytes 262176 | tf_op jit(solution)/shard_map/ppermute | solution.py:273
  122.3 0.8 fusion.5
  (5 shorter events, 0.1 us)
Async XLA Ops:
  9.5 3.5 %copy-start.6 = (f32[2,2,512]{2,1,0:T(2,128)S(1)}, f32[2,2,512]{2,1,0:T(2,128)}, u32[]{:S(2)}) copy-start(f32[2,2,512]{2,1,0:T(2,128)} %param.10) | copy-start | bytes 24580
  9.5 3.8 %copy-start.1 = (bf16[512,256]{1,0:T(8,128)(2,1)S(1)}, bf16[512,256]{1,0:T(8,128)(2,1)}, u32[]{:S(2)}) copy-start(bf16[512,256]{1,0:T(8,128)(2,1)} %q_ref.3) | copy-start | bytes 786436
  9.5 3.8 %copy-start.3 = (bf16[2,512,256]{2,1,0:T(8,128)(2,1)S(1)}, bf16[2,512,256]{2,1,0:T(8,128)(2,1)}, u32[]{:S(2)}) copy-start(bf16[2,512,256]{2,1,0:T(8,128)(2,1)} %k_ref.1) | copy-start | bytes 1572868
  9.5 3.8 %copy-start.4 = (bf16[2,512,256]{2,1,0:T(8,128)(2,1)S(1)}, bf16[2,512,256]{2,1,0:T(8,128)(2,1)}, u32[]{:S(2)}) copy-start(bf16[2,512,256]{2,1,0:T(8,128)(2,1)} %v_ref.1) | copy-start | bytes 1572868
  10.8 60.5 %collective-permute-start.4 = (bf16[256,2048]{1,0:T(8,128)(2,1)}, bf16[256,2048]{1,0:T(8,128)(2,1)S(1)}, u32[]{:S(2)}, u32[]{:S(2)}) collective-permute-start(bf16[256,2048]{1,0:T(8,128)(2,1)} %bitcast.22), channel_id=1, source_target_pairs={{0,1},{1,0},{2,3},{3,2},{4,5},{5,4},{6,7},{7,6},{8,9},{9,8},{10,11... | collective-permute-start | bytes 3145736 | tf_op jit(solution)/shard_map/ppermute | solution.py:276
  13.3 53.8 %copy-start.2 = (bf16[512,256]{1,0:T(8,128)(2,1)S(1)}, bf16[512,256]{1,0:T(8,128)(2,1)}, u32[]{:S(2)}) copy-start(bf16[512,256]{1,0:T(8,128)(2,1)} %q_ref.3) | copy-start | bytes 786436
  13.3 53.8 %copy-start.5 = (bf16[512,256]{1,0:T(8,128)(2,1)S(1)}, bf16[512,256]{1,0:T(8,128)(2,1)}, u32[]{:S(2)}) copy-start(bf16[512,256]{1,0:T(8,128)(2,1)} %g_ref.1) | copy-start | bytes 786436
  39.1 30.6 %copy-start.7 = (s32[8]{0:T(128)S(1)}, s32[8]{0:T(128)}, u32[]{:S(2)}) copy-start(s32[8]{0:T(128)} %constant.57.clone) | copy-start | bytes 100
  39.1 32.2 %copy-start = (bf16[256,4096]{1,0:T(8,128)(2,1)S(1)}, bf16[256,4096]{1,0:T(8,128)(2,1)}, u32[]{:S(2)}) copy-start(bf16[256,4096]{1,0:T(8,128)(2,1)} %w_ref.3) | copy-start | bytes 6291460
  39.1 4.4 %collective-permute-start = (bf16[2,128,256]{2,1,0:T(8,128)(2,1)S(1)}, bf16[2,128,256]{2,1,0:T(8,128)(2,1)S(1)}, u32[]{:S(2)}, u32[]{:S(2)}) collective-permute-start(bf16[2,128,256]{2,1,0:T(8,128)(2,1)S(1)} %get-tuple-element.15), channel_id=1, source_target_pairs={{0,64},{64,128},{128,192},{192,256},{256,320},{320,384},{384,448},... | collective-permute-start | bytes 393224 | tf_op jit(solution)/shard_map/ppermute | solution.py:280
  43.7 8.7 %collective-permute-start.1 = (bf16[2,128,256]{2,1,0:T(8,128)(2,1)S(1)}, bf16[2,128,256]{2,1,0:T(8,128)(2,1)S(1)}, u32[]{:S(2)}, u32[]{:S(2)}) collective-permute-start(bf16[2,128,256]{2,1,0:T(8,128)(2,1)S(1)} %get-tuple-element.17), channel_id=1, source_target_pairs={{0,128},{64,192},{128,256},{192,320},{256,384},{320,448},{1,129},{... | collective-permute-start | bytes 393224 | tf_op jit(solution)/shard_map/ppermute | solution.py:280
  52.6 14.5 %collective-permute-start.2 = (bf16[2,128,128]{2,1,0:T(8,128)(2,1)S(1)}, bf16[2,128,128]{2,1,0:T(8,128)(2,1)S(1)}, u32[]{:S(2)}, u32[]{:S(2)}) collective-permute-start(bf16[2,128,128]{2,1,0:T(8,128)(2,1)S(1)} %shard_map.77), channel_id=1, source_target_pairs={{0,256},{64,320},{128,384},{192,448},{1,257},{65,321},{129,385},{1... | collective-permute-start | bytes 196616 | tf_op jit(solution)/shard_map/ppermute | solution.py:280
  67.7 3.6 %collective-permute-start.3 = (bf16[512,256]{1,0:T(8,128)(2,1)S(1)}, bf16[512,256]{1,0:T(8,128)(2,1)}, u32[]{:S(2)}, u32[]{:S(2)}) collective-permute-start(bf16[512,256]{1,0:T(8,128)(2,1)S(1)} %shard_map.78.a_ref), channel_id=1, source_target_pairs={{0,1},{1,0},{2,3},{3,2},{4,5},{5,4},{6,7},{7,6},{8,9},{9,8},{10,11... | collective-permute-start | bytes 786440 | tf_op jit(solution)/shard_map/ppermute | solution.py:276
  72.6 11.3 %collective-permute-start.5 = (bf16[256,256]{1,0:T(8,128)(2,1)S(1)}, bf16[256,256]{1,0:T(8,128)(2,1)S(1)}, u32[]{:S(2)}, u32[]{:S(2)}) collective-permute-start(bf16[256,256]{1,0:T(8,128)(2,1)S(1)} %get-tuple-element.29), channel_id=1, source_target_pairs={{0,2},{1,3},{2,4},{3,5},{4,6},{5,7},{6,8},{7,9},{8,10},{9,11},{10,... | collective-permute-start | bytes 393224 | tf_op jit(solution)/shard_map/ppermute | solution.py:273
  76.1 7.8 %collective-permute-start.9 = (bf16[256,256]{1,0:T(8,128)(2,1)S(1)}, bf16[256,256]{1,0:T(8,128)(2,1)S(1)}, u32[]{:S(2)}, u32[]{:S(2)}) collective-permute-start(bf16[256,256]{1,0:T(8,128)(2,1)S(1)} %get-tuple-element.30), channel_id=1, source_target_pairs={{0,14},{1,15},{2,0},{3,1},{4,2},{5,3},{6,4},{7,5},{8,6},{9,7},{10,... | collective-permute-start | bytes 393224 | tf_op jit(solution)/shard_map/ppermute | solution.py:273
  84.1 11.2 %collective-permute-start.6 = (bf16[512,256]{1,0:T(8,128)(2,1)S(1)}, bf16[512,256]{1,0:T(8,128)(2,1)S(1)}, u32[]{:S(2)}, u32[]{:S(2)}) collective-permute-start(bf16[512,256]{1,0:T(8,128)(2,1)S(1)} %pad_maximum_fusion), channel_id=1, source_target_pairs={{0,2},{1,3},{2,4},{3,5},{4,6},{5,7},{6,8},{7,9},{8,10},{9,11},{10,... | collective-permute-start | bytes 786440 | tf_op jit(solution)/shard_map/ppermute | solution.py:273
  86.9 10.4 %collective-permute-start.10 = (bf16[512,256]{1,0:T(8,128)(2,1)S(1)}, bf16[512,256]{1,0:T(8,128)(2,1)S(1)}, u32[]{:S(2)}, u32[]{:S(2)}) collective-permute-start(bf16[512,256]{1,0:T(8,128)(2,1)S(1)} %pad_maximum_fusion.1), channel_id=1, source_target_pairs={{0,14},{1,15},{2,0},{3,1},{4,2},{5,3},{6,4},{7,5},{8,6},{9,7},{10,... | collective-permute-start | bytes 786440 | tf_op jit(solution)/shard_map/ppermute | solution.py:273
  95.3 10.3 %collective-permute-start.7 = (bf16[512,256]{1,0:T(8,128)(2,1)S(1)}, bf16[512,256]{1,0:T(8,128)(2,1)S(1)}, u32[]{:S(2)}, u32[]{:S(2)}) collective-permute-start(bf16[512,256]{1,0:T(8,128)(2,1)S(1)} %fusion.2), channel_id=1, source_target_pairs={{0,2},{1,3},{2,4},{3,5},{4,6},{5,7},{6,8},{7,9},{8,10},{9,11},{10,... | collective-permute-start | bytes 786440 | tf_op jit(solution)/shard_map/ppermute | solution.py:273
  105.7 8.3 %collective-permute-start.11 = (bf16[512,256]{1,0:T(8,128)(2,1)S(1)}, bf16[512,256]{1,0:T(8,128)(2,1)S(1)}, u32[]{:S(2)}, u32[]{:S(2)}) collective-permute-start(bf16[512,256]{1,0:T(8,128)(2,1)S(1)} %get-tuple-element.24), channel_id=1, source_target_pairs={{0,14},{1,15},{2,0},{3,1},{4,2},{5,3},{6,4},{7,5},{8,6},{9,7},{10,... | collective-permute-start | bytes 786440 | tf_op jit(solution)/shard_map/ppermute | solution.py:273
  107.7 9.7 %collective-permute-start.8 = (bf16[512,256]{1,0:T(8,128)(2,1)S(1)}, bf16[512,256]{1,0:T(8,128)(2,1)S(1)}, u32[]{:S(2)}, u32[]{:S(2)}) collective-permute-start(bf16[512,256]{1,0:T(8,128)(2,1)S(1)} %get-tuple-element.23), channel_id=1, source_target_pairs={{0,2},{1,3},{2,4},{3,5},{4,6},{5,7},{6,8},{7,9},{8,10},{9,11},{10,... | collective-permute-start | bytes 786440 | tf_op jit(solution)/shard_map/ppermute | solution.py:273
  114.1 8.3 %collective-permute-start.12 = (bf16[512,256]{1,0:T(8,128)(2,1)S(1)}, bf16[512,256]{1,0:T(8,128)(2,1)S(1)}, u32[]{:S(2)}, u32[]{:S(2)}) collective-permute-start(bf16[512,256]{1,0:T(8,128)(2,1)S(1)} %fusion.1), channel_id=1, source_target_pairs={{0,14},{1,15},{2,0},{3,1},{4,2},{5,3},{6,4},{7,5},{8,6},{9,7},{10,... | collective-permute-start | bytes 786440 | tf_op jit(solution)/shard_map/ppermute | solution.py:273
where the time goes:
time: 125 us; the launch traced here: 123 us
  starting transfers between devices  50.1 us (40%)
  waiting for transfers between devices  27.7 us (22%)
  Pallas kernels  16.5 us (13%)
  blocking collectives  15.9 us (13%)
  local copies, waits for them, and re-layouts  11.3 us (9%)
    ppermute x8, starting transfers between devices, shift(): lax.ppermute(a, 'head', [(i, (i + 2 * by) % devices) for i in range(devic...  25.4 us
    ppermute x3, starting transfers between devices, later_z(): return lax.ppermute(a, 'ctx_0', [(i, i + by) for i in range(groups - by)])  20.7 us
    ppermute x8, waiting for transfers between devices, shift(): lax.ppermute(a, 'head', [(i, (i + 2 * by) % devices) for i in range(devic...  19.8 us
    all_gather x1, blocking collectives, per_device(): gathered = lax.all_gather(maps, 'ctx_1')  15.9 us
    pallas_call x1, Pallas kernels, local_maps(): pl.pallas_call(functools.partial(local_kernel, group), out_shape=(jax.Sha...  9.22 us
    ppermute x3, waiting for transfers between devices, later_z(): return lax.ppermute(a, 'ctx_0', [(i, i + by) for i in range(groups - by)])  6.49 us
    dynamic_slice x1, local copies, waits for them, and re-layouts, per_device(): lax.dynamic_index_in_dim(out_weight.reshape(cols, chips, 2, cols), 1 - co...  6.15 us
    pallas_call x2, Pallas kernels, project(): pl.pallas_call(project_kernel, out_shape=jax.ShapeDtypeStruct((count, tok...  5.24 us
  transfers between devices with their start and end apart: 13, of which 8 were waited for; matrix products, arithmetic and copies ran while one was open for 1% of the time, Pallas kernels for 12%

commit v1 on v0

v1 whole, which is shorter than its diff:
```python
import functools
import jax
import jax.numpy as jnp
from jax import lax
from jax.experimental import pallas as pl
from jax.experimental.pallas import tpu as pltpu
from jax.sharding import Mesh
from jax.sharding import PartitionSpec as P

F32 = jnp.float32
BF16 = jnp.bfloat16
HD = 128
SPAN = 64
CTX = ("ctx_0", "ctx_1")


def dot(a, b):
    return jnp.dot(a, b, preferred_element_type=F32)


def dot_nt(a, b):
    return lax.dot_general(a, b, (((1,), (1,)), ((), ())), preferred_element_type=F32)


def split(x):
    hi = x.astype(BF16)
    return hi, (x - hi.astype(F32)).astype(BF16)


def wide(x):
    return jnp.concatenate(split(x), axis=1)


def square(pair):
    return jnp.concatenate([pair, pair], axis=0)


def halves(x):
    n = x.shape[1] // 2
    return x[:, :n] + x[:, n:]


def read_block(ref, blk, h):
    rows = [
        (j, pl.ds(pl.multiple_of(blk * SPAN + 16 * g, 16), 16))
        for g in range(SPAN // 16)
        for j in range(2)
    ]
    cols = slice(h * HD, (h + 1) * HD)
    return jnp.concatenate([ref[j, r, cols] for j, r in rows], axis=0)


def order(p):
    return (p & ~31) + 2 * (p & 15) + ((p >> 4) & 1)


def map_kernel(
    group, k_hbm, v_hbm, b_ref, ab_ref, x_ref, e_ref, pre_ref, k_ref, v_ref, lev_ref, p_ref, sems
):
    get_k = pltpu.make_async_copy(k_hbm, k_ref, sems.at[0])
    get_v = pltpu.make_async_copy(v_hbm, v_ref, sems.at[1])
    get_k.start()
    get_v.start()
    heads = k_ref.shape[2] // HD
    blocks = k_ref.shape[1] // SPAN
    sub = 2 * SPAN
    place_r = lax.broadcasted_iota(jnp.int32, (sub, sub), 0)
    place_c = lax.broadcasted_iota(jnp.int32, (sub, sub), 1)
    s_r, s_c = order(place_r), order(place_c)
    apart = s_r ^ s_c
    level = jnp.zeros((sub, sub), jnp.int32)
    for bit in range(1, 7):
        level = level + (apart >= 2**bit).astype(jnp.int32)
    lev_ref[...] = jnp.where(s_r > s_c, level, -1)
    eye = (place_r == place_c).astype(F32)
    for h in range(heads):
        p_ref[h] = jnp.concatenate([eye, jnp.zeros((HD, HD), F32)], axis=1)
    get_k.wait()
    get_v.wait()

    def body(step, carry):
        probs = [(step * group + i, h) for i in range(group) for h in range(heads)]
        kb = [read_block(k_ref, blk, h) for blk, h in probs]
        num = range(len(probs))
        n, e, N, X = [], [], [], []
        for i in num:
            blk, h = probs[i]
            gram = dot_nt(kb[i], kb[i])
            n2 = jnp.sum(gram * eye, axis=0, keepdims=True) + 1e-6
            e.append(b_ref[pl.ds(h * blocks + blk, 1), :] / n2)
            n.append(jnp.sqrt(n2))
            e_ref[h * blocks + blk] = jnp.concatenate([e[i], n[i]], axis=0)
            N.append(jnp.where(lev_ref[...] >= 0, gram * e[i], 0.0))
            X.append(eye - jnp.where(lev_ref[...] == 0, N[i], 0.0))
        for lev in range(1, 7):
            xw = [wide(x) for x in X]
            Z = []
            for i in num:
                C = jnp.where(lev_ref[...] == lev, N[i], 0.0)
                Z.append(halves(dot(wide(C), square(xw[i]))))
            for i in num:
                X[i] = X[i] - halves(dot(xw[i], square(wide(Z[i]))))
        A, B = [], []
        for i in num:
            blk, h = probs[i]
            xw = wide(X[i])
            x_ref[h * blocks + blk] = xw
            ke = wide(kb[i].T.astype(F32) * e[i])
            y = halves(dot(ke, square(xw)))
            A.append(wide(eye - dot(wide(y), square(kb[i]))))
            B.append(dot(wide(y * n[i]), square(read_block(v_ref, blk, h))))
        for i in num:
            blk, h = probs[i]
            p = p_ref[h]
            ph, plo = split(p)
            pre_ref[h * blocks + blk] = ph
            new = dot(A[i], square(ph)) + dot(A[i][:, :HD], plo)
            p_ref[h] = new + jnp.concatenate([jnp.zeros((HD, HD), F32), B[i]], axis=1)
        return carry

    lax.fori_loop(0, blocks // group, body, 0)
    for h in range(heads):
        ab_ref[h] = p_ref[h].astype(BF16)


def local_maps(k, v, b_rows, group):
    _, tok, cols = k.shape
    heads = cols // HD
    count = heads * tok // SPAN
    return pl.pallas_call(
        functools.partial(map_kernel, group),
        out_shape=(
            jax.ShapeDtypeStruct((heads, HD, 2 * HD), BF16),
            jax.ShapeDtypeStruct((count, 2 * SPAN, 4 * SPAN), BF16),
            jax.ShapeDtypeStruct((count, 2, 2 * SPAN), F32),
            jax.ShapeDtypeStruct((count, HD, 2 * HD), BF16),
        ),
        in_specs=[pl.BlockSpec(memory_space=pltpu.HBM)] * 2 + [pl.BlockSpec(memory_space=pltpu.VMEM)],
        out_specs=[pl.BlockSpec(memory_space=pltpu.VMEM)] * 4,
        scratch_shapes=[
            pltpu.VMEM(k.shape, k.dtype),
            pltpu.VMEM(v.shape, v.dtype),
            pltpu.VMEM((2 * SPAN, 2 * SPAN), jnp.int32),
            pltpu.VMEM((heads, HD, 2 * HD), F32),
            pltpu.SemaphoreType.DMA((2,)),
        ],
        compiler_params=pltpu.CompilerParams(vmem_limit_bytes=32 * 1024 * 1024),
    )(k, v, b_rows)


def local_kernel(q_ref, k_ref, v_ref, g_ref, x_ref, e_ref, pre_ref, l_ref, m_ref, s_ref):
    heads = q_ref.shape[1] // HD
    blocks = q_ref.shape[0] // SPAN
    sub = 2 * SPAN
    seen = (order(lax.broadcasted_iota(jnp.int32, (SPAN, sub), 1)) >> 1) <= lax.broadcasted_iota(
        jnp.int32, (SPAN, sub), 0
    )
    spots = [
        (h * blocks + blk, slice(blk * SPAN, (blk + 1) * SPAN), slice(h * HD, (h + 1) * HD))
        for blk in range(blocks)
        for h in range(heads)
    ]
    num = range(len(spots))
    kb = [read_block(k_ref, i // heads, i % heads) for i in num]
    scores = [
        wide(jnp.where(seen, dot_nt(q_ref[rows, cols], kb[i]), 0.0) * e_ref[at, :1])
        for i, (at, rows, cols) in enumerate(spots)
    ]
    zq = [halves(dot(scores[i], square(x_ref[spots[i][0]]))) for i in num]
    carry = [
        (q_ref[rows, cols].astype(F32) - dot(wide(zq[i]), square(kb[i]))).astype(BF16)
        for i, (_, rows, cols) in enumerate(spots)
    ]
    loc = [
        dot(wide(zq[i] * e_ref[spots[i][0], 1:]), square(read_block(v_ref, i // heads, i % heads)))
        for i in num
    ]
    prod = [dot(carry[i], pre_ref[spots[i][0]]) for i in num]
    for i, (_, rows, cols) in enumerate(spots):
        qf = q_ref[rows, cols].astype(F32)
        unit = lax.rsqrt(jnp.sum(qf * qf, axis=1, keepdims=True) + 1e-6)
        m_ref[rows, cols] = (prod[i][:, :HD] * unit).astype(BF16)
        l_ref[rows, cols] = (loc[i] + prod[i][:, HD:]) * unit
        gate = g_ref[rows, cols].astype(F32)
        s_ref[rows, cols] = gate / (1.0 + jnp.exp(-gate))


def beta_rows(betas):
    heads, _, tok = betas.shape
    blocks = tok // SPAN
    return (
        betas.reshape(heads, 2, blocks, SPAN // 16, 16)
        .transpose(0, 2, 3, 1, 4)
        .reshape(heads * blocks, 2 * SPAN)
    )


def affine(a, b):
    return jnp.concatenate([a, b], axis=1)


def fold_kernel(x_ref, m_ref, send_ref, tot_ref, in_ref):
    peers, heads = m_ref.shape[:2]
    x = x_ref[0]
    r = lax.broadcasted_iota(jnp.int32, (HD, 2 * HD), 0)
    c = lax.broadcasted_iota(jnp.int32, (HD, 2 * HD), 1)
    zero = jnp.zeros((HD, HD), F32)
    total = [m_ref[0, h].astype(F32) for h in range(heads)]
    inside = [(r == c).astype(F32)] * heads
    for k in range(1, peers):
        for h in range(heads):
            inside[h] = jnp.where(x == k, total[h], inside[h])
            later = m_ref[k, h]
            prod = halves(dot(later[:, :HD], jnp.concatenate(split(total[h]), axis=1)))
            total[h] = prod + affine(zero, later[:, HD:].astype(F32))
    for h in range(heads):
        send_ref[h] = total[h].astype(BF16)
        tot_ref[h] = total[h]
        in_ref[h] = inside[h]


def join_kernel(later_ref, earlier_ref, send_ref, out_ref):
    zero = jnp.zeros((HD, HD), F32)
    for h in range(later_ref.shape[0]):
        later = later_ref[h]
        out = dot(wide(later[:, :HD]), square(earlier_ref[h])) + affine(zero, later[:, HD:])
        send_ref[h] = out.astype(BF16)
        out_ref[h] = out


def carry_kernel(later_ref, earlier_ref, send_ref):
    for h in range(later_ref.shape[0]):
        later = later_ref[h]
        state = dot(wide(later[:, :HD]), square(earlier_ref[h][:, HD:])) + later[:, HD:]
        send_ref[h] = state.astype(BF16)


def entry_kernel(in_ref, near_ref, far_ref, out_ref):
    zero = jnp.zeros((HD, HD), F32)
    for h in range(in_ref.shape[0]):
        near = near_ref[h]
        both = dot(near[:, :HD], far_ref[h]) + affine(zero, near[:, HD:].astype(F32))
        inner = in_ref[h]
        bh, bl = split(both)
        lhs = wide(inner[:, :HD])
        out = dot(lhs, square(bh)) + dot(lhs[:, :HD], bl)
        out_ref[h] = out + affine(zero, inner[:, HD:])


def mix_kernel(entry_ref, state_ref, l_ref, m_ref, s_ref, o_ref):
    for h in range(entry_ref.shape[0]):
        entry = entry_ref[h]
        start = dot(wide(entry[:, :HD]), square(state_ref[h])) + entry[:, HD:]
        cols = slice(h * HD, (h + 1) * HD)
        att = l_ref[:, cols] + dot(m_ref[:, cols], start.astype(BF16))
        scale = lax.rsqrt(jnp.mean(att * att, axis=1, keepdims=True) + 1e-6)
        o_ref[:, cols] = (att * scale * s_ref[:, cols]).astype(BF16)


VM = pl.BlockSpec(memory_space=pltpu.VMEM)
SM = pl.BlockSpec(memory_space=pltpu.SMEM)


def small(kernel, outs, *args, specs=None):
    return pl.pallas_call(
        kernel,
        out_shape=outs,
        in_specs=specs or [VM] * len(args),
        out_specs=jax.tree.map(lambda _: VM, outs),
        compiler_params=pltpu.CompilerParams(vmem_limit_bytes=32 * 1024 * 1024),
    )(*args)


def term(at, a_ref, b_ref, w_ref, x_ref):
    width = a_ref.shape[1]
    cols = pl.ds(pl.multiple_of(at * width, width), width)
    return dot(a_ref[...], w_ref[:, cols]) + dot(b_ref[...], x_ref[:, cols])


def far_kernel(at_ref, a_ref, b_ref, w_ref, x_ref, up_ref, down_ref):
    out = term(at_ref[0], a_ref, b_ref, w_ref, x_ref).astype(BF16)
    up_ref[...] = out[: up_ref.shape[0]]
    down_ref[...] = out[up_ref.shape[0] :]


def terms_kernel(at_ref, a_ref, b_ref, w_ref, x_ref, o_ref):
    for i in range(o_ref.shape[0]):
        o_ref[i] = term(at_ref[i], a_ref, b_ref, w_ref, x_ref)


def first_add_kernel(at, rows, terms_ref, got_ref, o_ref):
    o_ref[...] = terms_ref[at].astype(BF16)
    o_ref[rows] = (terms_ref[at, rows] + got_ref[...].astype(F32)).astype(BF16)


def add_kernel(at, terms_ref, got_ref, o_ref):
    o_ref[...] = (terms_ref[at] + got_ref[...].astype(F32)).astype(o_ref.dtype)


def last_add_kernel(a_ref, b_ref, o_ref):
    o_ref[...] = (a_ref[...] + b_ref[...].astype(F32)).astype(BF16)


def per_device(queries, keys, values, betas, gate, out_weight):
    tok, cols = queries.shape
    heads = cols // HD
    devices = lax.axis_size("head")
    chips = devices // 2
    me = lax.axis_index("head")
    chip, core = me // 2, me % 2

    def shift(a, by):
        return lax.ppermute(a, "head", [(i, (i + 2 * by) % devices) for i in range(devices)])

    def mate(a):
        return lax.ppermute(a, "head", [(i, i ^ 1) for i in range(devices)])

    def later_z(a, by):
        groups = lax.axis_size("ctx_0")
        return lax.ppermute(a, "ctx_0", [(i, i + by) for i in range(groups - by)])

    mate_weight = mate(out_weight)
    maps, inverse, scales, prefixes = local_maps(keys, values, beta_rows(betas), 8)

    wide_map = jax.ShapeDtypeStruct((heads, HD, 2 * HD), F32)
    wide_send = jax.ShapeDtypeStruct((heads, HD, 2 * HD), BF16)
    state_send = jax.ShapeDtypeStruct((heads, HD, HD), BF16)
    gathered = lax.all_gather(maps, "ctx_1")
    x = lax.axis_index("ctx_1").astype(jnp.int32).reshape(1)
    send, total, inside = small(
        fold_kernel, (wide_send, wide_map, wide_map), x, gathered, specs=[SM, VM]
    )
    near = later_z(send, 1)
    send, pair = small(join_kernel, (wide_send, wide_map), total, near)
    far = later_z(send, 2)
    tokens = jax.ShapeDtypeStruct((tok, cols), F32)
    local, carry, silu = small(
        local_kernel,
        (tokens, jax.ShapeDtypeStruct((tok, cols), BF16), tokens),
        queries,
        keys,
        values,
        gate,
        inverse,
        scales,
        lax.optimization_barrier((prefixes, near))[0],
    )
    send = small(carry_kernel, state_send, pair, far)
    state = later_z(send, 4)
    entry = small(entry_kernel, wide_map, inside, near, far)
    mixed_in = small(
        mix_kernel,
        jax.ShapeDtypeStruct((tok, cols), BF16),
        entry,
        state,
        local,
        carry,
        silu,
    )
    mate_in = mate(mixed_in)

    half = chips // 2
    sides = [s for k in range(half - 1, 0, -1) for s in (k, chips - k)] + [0]
    at = [2 * ((chip + jnp.array(o, jnp.int32)) % chips) + core for o in ([half], sides)]

    weights = (mixed_in, mate_in, out_weight, mate_weight)
    specs = [SM] + [VM] * 4
    cut = tok // 2
    part = jax.ShapeDtypeStruct((cut, cols), BF16)
    up, down = small(far_kernel, (part, part), at[0], *weights, specs=specs)
    up, down = shift(up, 1), shift(down, -1)
    several = jax.ShapeDtypeStruct((len(sides), tok, cols), F32)
    terms = small(terms_kernel, several, at[1], *weights, specs=specs)
    sent = jax.ShapeDtypeStruct((tok, cols), BF16)
    down_sum = None
    for k in range(half - 1):
        adders = [functools.partial(add_kernel, 2 * k + i) for i in range(2)]
        if k == 0:
            adders = [
                functools.partial(first_add_kernel, i, r)
                for i, r in enumerate((slice(0, cut), slice(cut, tok)))
            ]
        else:
            up = lax.optimization_barrier((up, down_sum))[0]
        up_sum = small(adders[0], sent, terms, up)
        down = lax.optimization_barrier((down, up_sum))[0]
        down_sum = small(adders[1], sent, terms, down)
        up, down = shift(up_sum, 1), shift(down_sum, -1)
    last = functools.partial(add_kernel, 2 * half - 2)
    up = lax.optimization_barrier((up, down_sum))[0]
    total = small(last, tokens, terms, up)
    return small(last_add_kernel, sent, total, down)


def solution(mesh):
    z = mesh.shape["ctx"] // 4
    finer = Mesh(mesh.devices.reshape(z, 4, mesh.shape["head"]), ("ctx_0", "ctx_1", "head"))
    in_specs = (
        P(CTX, "head"),
        P(None, CTX, "head"),
        P(None, CTX, "head"),
        P("head", None, CTX),
        P(CTX, "head"),
        P("head", None),
    )
    return jax.shard_map(
        per_device, mesh=finer, in_specs=in_specs, out_specs=P(CTX, "head"), check_vma=False
    )
```

time: 125 us -> 111 us (0.89)
  the two profiles are of different devices: /device:TPU:6 before, /device:TPU:26 now
where the time goes in v1:
time: 111 us
  starting transfers between devices  55.7 us (50%)
  waiting for transfers between devices  19.7 us (18%)
  Pallas kernels  18.2 us (16%)
  blocking collectives  13.5 us (12%)
  local copies, waits for them, and re-layouts  3.1 us (3%)
    ppermute x8, starting transfers between devices, shift(): lax.ppermute(a, 'head', [(i, (i + 2 * by) % devices) for i in range(devic...  28.7 us
    ppermute x3, starting transfers between devices, later_z(): return lax.ppermute(a, 'ctx_0', [(i, i + by) for i in range(groups - by)])  23.1 us
    all_gather x1, blocking collectives, per_device(): gathered = lax.all_gather(maps, 'ctx_1')  13.5 us
    ppermute x8, waiting for transfers between devices, shift(): lax.ppermute(a, 'head', [(i, (i + 2 * by) % devices) for i in range(devic...  13.2 us
    pallas_call x1, Pallas kernels, local_maps(): pl.pallas_call(functools.partial(map_kernel, group), out_shape=(jax.Shape...  9.11 us
    pallas_call x16, Pallas kernels, small(): pl.pallas_call(kernel, out_shape=outs, in_specs=specs or [VM] * len(args)...  9.04 us
    ppermute x3, waiting for transfers between devices, later_z(): return lax.ppermute(a, 'ctx_0', [(i, i + by) for i in range(groups - by)])  5.07 us
    ppermute x2, starting transfers between devices, mate(): return lax.ppermute(a, 'head', [(i, i ^ 1) for i in range(devices)])  3.96 us
  transfers between devices with their start and end apart: 13, of which 8 were waited for; matrix products, arithmetic and copies ran while one was open for 1% of the time, Pallas kernels for 14%

profile of v1, /device:TPU:26, one launch (start us, length us, event | category | flops | bytes accessed | tf_op | source)
XLA Modules:
  0.0 110.5 jit_solution(15349564454244109988)
XLA Ops:
  0.0 0.0 copy-start.5
  0.0 2.0 %collective-permute-start.4 = (bf16[256,4096]{1,0:T(8,128)(2,1)}, bf16[256,4096]{1,0:T(8,128)(2,1)}, u32[]{:S(2)}, u32[]{:S(2)}) collective-permute-start(bf16[256,4096]{1,0:T(8,128)(2,1)} %w_ref.3), channel_id=1, source_target_pairs={{0,1},{1,0},{2,3},{3,2},{4,5},{5,4},{6,7},{7,6},{8,9},{9,8},{10,11... | collective-permute-start | bytes 6291464 | tf_op jit(solution)/shard_map/ppermute | solution.py:316
  2.1 0.8 reshape.12
  2.9 0.1 copy.12
  2.9 0.1 reshape.13.b_ref
  3.1 0.0 copy-start.1
  3.1 1.0 copy-done.1
  4.1 0.0 copy-start.3
  4.1 1.0 copy-done.3
  5.1 0.0 copy-start.2
  5.1 0.0 copy-start.4
  5.1 0.0 copy-start.6
  5.2 9.1 %shard_map.82 = (bf16[2,128,256]{2,1,0:T(8,128)(2,1)S(1)}, bf16[16,128,256]{2,1,0:T(8,128)(2,1)S(1)}, f32[16,2,128]{2,1,0:T(2,128)S(1)}, bf16[16,128,256]{2,1,0:T(8,128)(2,1)S(1)}) custom-call(bf16[2,512,256]{2,1,0:T(8,128)(2,1)S(1)} %copy-done.1, bf16[2,512,256]{2,1,0:T(8,128)(2,1)S(1)} %copy-done.3, f32[16,128]{1,0:T(8,128)S(1)} %reshape.13.b_ref), custom_call_target="tpu_custom_call" | custom-call | tf_op jit(solution)/shard_map/pallas_call | solution.py:130
  14.3 13.5 %all-gather = bf16[8,128,256]{2,1,0:T(8,128)(2,1)S(1)} all-gather(bf16[2,128,256]{2,1,0:T(8,128)(2,1)S(1)} %get-tuple-element.26), channel_id=2, replica_groups=mesh['ctx_0'=8,'ctx_1'=4,'head'=16] {'ctx_1'}, dimensions={0}, use_global_device_ids=true | all-gather | bytes 655360 | tf_op jit(solution)/shard_map/all_gather | solution.py:328
  27.8 0.6 shard_map.83
  28.4 4.3 %collective-permute-start = (bf16[2,128,256]{2,1,0:T(8,128)(2,1)S(1)}, bf16[2,128,256]{2,1,0:T(8,128)(2,1)S(1)}, u32[]{:S(2)}, u32[]{:S(2)}) collective-permute-start(bf16[2,128,256]{2,1,0:T(8,128)(2,1)S(1)} %get-tuple-element.28), channel_id=1, source_target_pairs={{0,64},{64,128},{128,192},{192,256},{256,320},{320,384},{384,448},... | collective-permute-start | bytes 393224 | tf_op jit(solution)/shard_map/ppermute | solution.py:320
  32.7 2.5 %collective-permute-done.earlier_ref.near_ref = bf16[2,128,256]{2,1,0:T(8,128)(2,1)S(1)} collective-permute-done((bf16[2,128,256]{2,1,0:T(8,128)(2,1)S(1)}, bf16[2,128,256]{2,1,0:T(8,128)(2,1)S(1)}, u32[]{:S(2)}, u32[]{:S(2)}) %collective-permute-start) | collective-permute-done | bytes 131104 | tf_op jit(solution)/shard_map/ppermute | solution.py:320
  35.2 0.2 shard_map.84
  35.4 6.2 %collective-permute-start.1 = (bf16[2,128,256]{2,1,0:T(8,128)(2,1)S(1)}, bf16[2,128,256]{2,1,0:T(8,128)(2,1)S(1)}, u32[]{:S(2)}, u32[]{:S(2)}) collective-permute-start(bf16[2,128,256]{2,1,0:T(8,128)(2,1)S(1)} %get-tuple-element.30), channel_id=1, source_target_pairs={{0,128},{64,192},{128,256},{192,320},{256,384},{320,448},{1,129},{... | collective-permute-start | bytes 393224 | tf_op jit(solution)/shard_map/ppermute | solution.py:320
  41.6 2.5 %collective-permute-done.1.far_ref.earlier_ref = bf16[2,128,256]{2,1,0:T(8,128)(2,1)S(1)} collective-permute-done((bf16[2,128,256]{2,1,0:T(8,128)(2,1)S(1)}, bf16[2,128,256]{2,1,0:T(8,128)(2,1)S(1)}, u32[]{:S(2)}, u32[]{:S(2)}) %collective-permute-start.1) | collective-permute-done | bytes 131104 | tf_op jit(solution)/shard_map/ppermute | solution.py:320
  44.1 0.2 shard_map.86
  44.2 12.6 %collective-permute-start.2 = (bf16[2,128,128]{2,1,0:T(8,128)(2,1)S(1)}, bf16[2,128,128]{2,1,0:T(8,128)(2,1)S(1)}, u32[]{:S(2)}, u32[]{:S(2)}) collective-permute-start(bf16[2,128,128]{2,1,0:T(8,128)(2,1)S(1)} %shard_map.86), channel_id=1, source_target_pairs={{0,256},{64,320},{128,384},{192,448},{1,257},{65,321},{129,385},{1... | collective-permute-start | bytes 196616 | tf_op jit(solution)/shard_map/ppermute | solution.py:320
  56.9 0.0 copy-done.5
  56.9 0.0 copy-done.2
  56.9 0.0 copy-done.4
  56.9 0.0 copy-done.6
  56.9 1.4 %shard_map.87 = (f32[512,256]{1,0:T(8,128)S(1)}, bf16[512,256]{1,0:T(8,128)(2,1)S(1)}, f32[512,256]{1,0:T(8,128)S(1)}) custom-call(bf16[512,256]{1,0:T(8,128)(2,1)S(1)} %copy-done.5, bf16[2,512,256]{2,1,0:T(8,128)(2,1)S(1)} %copy-done.2, bf16[2,512,256]{2,1,0:T(8,128)(2,1)S(1)} %copy-done.4, bf16[512,256]{1,0:T(8,128)(2,1)S(1)} %copy-done.6, ...), custom_call_target="tpu_custom_call" | custom-call | tf_op jit(solution)/shard_map/pallas_call | solution.py:265
  58.3 0.0 copy-start
  58.3 0.4 shard_map.85.entry_ref
  58.7 0.1 collective-permute-done.2.state_ref
  58.7 0.5 shard_map.88.a_ref
  59.3 1.9 %collective-permute-start.3 = (bf16[512,256]{1,0:T(8,128)(2,1)S(1)}, bf16[512,256]{1,0:T(8,128)(2,1)S(1)}, u32[]{:S(2)}, u32[]{:S(2)}) collective-permute-start(bf16[512,256]{1,0:T(8,128)(2,1)S(1)} %shard_map.88.a_ref), channel_id=1, source_target_pairs={{0,1},{1,0},{2,3},{3,2},{4,5},{5,4},{6,7},{7,6},{8,9},{9,8},{10,11... | collective-permute-start | bytes 786440 | tf_op jit(solution)/shard_map/ppermute | solution.py:316
  61.2 0.0 copy-start.7
  61.2 1.5 %collective-permute-done.3.b_ref = bf16[512,256]{1,0:T(8,128)(2,1)S(1)} collective-permute-done((bf16[512,256]{1,0:T(8,128)(2,1)S(1)}, bf16[512,256]{1,0:T(8,128)(2,1)S(1)}, u32[]{:S(2)}, u32[]{:S(2)}) %collective-permute-start.3) | collective-permute-done | bytes 262176 | tf_op jit(solution)/shard_map/ppermute | solution.py:316
  62.7 0.0 collective-permute-done.4.x_ref
  62.7 0.0 copy-done
  62.7 1.9 %shard_map.90 = (bf16[256,256]{1,0:T(8,128)(2,1)S(1)}, bf16[256,256]{1,0:T(8,128)(2,1)S(1)}) custom-call(s32[1]{0:T(128)S(6)} %add.51.at_ref, bf16[512,256]{1,0:T(8,128)(2,1)S(1)} %shard_map.88.a_ref, bf16[512,256]{1,0:T(8,128)(2,1)S(1)} %collective-permute-done.3.b_ref, bf16[256,4096]{1,0:T(8,128)(2,1)S(1)} %copy-done, ...), custom_call_target="tpu_custom_call" | custom-call | tf_op jit(solution)/shard_map/pallas_call | solution.py:265
  64.6 4.7 %collective-permute-start.5 = (bf16[256,256]{1,0:T(8,128)(2,1)S(1)}, bf16[256,256]{1,0:T(8,128)(2,1)S(1)}, u32[]{:S(2)}, u32[]{:S(2)}) collective-permute-start(bf16[256,256]{1,0:T(8,128)(2,1)S(1)} %get-tuple-element.39), channel_id=1, source_target_pairs={{0,2},{1,3},{2,4},{3,5},{4,6},{5,7},{6,8},{7,9},{8,10},{9,11},{10,... | collective-permute-start | bytes 393224 | tf_op jit(solution)/shard_map/ppermute | solution.py:313
  69.3 1.9 %collective-permute-start.7 = (bf16[256,256]{1,0:T(8,128)(2,1)S(1)}, bf16[256,256]{1,0:T(8,128)(2,1)S(1)}, u32[]{:S(2)}, u32[]{:S(2)}) collective-permute-start(bf16[256,256]{1,0:T(8,128)(2,1)S(1)} %get-tuple-element.40), channel_id=1, source_target_pairs={{0,14},{1,15},{2,0},{3,1},{4,2},{5,3},{6,4},{7,5},{8,6},{9,7},{10,... | collective-permute-start | bytes 393224 | tf_op jit(solution)/shard_map/ppermute | solution.py:313
  71.2 0.0 copy-done.7
  71.3 2.7 %shard_map.89.terms_ref = f32[7,512,256]{2,1,0:T(8,128)S(1)} custom-call(s32[7]{0:T(128)S(1)} %fusion.2.at_ref, bf16[512,256]{1,0:T(8,128)(2,1)S(1)} %shard_map.88.a_ref, bf16[512,256]{1,0:T(8,128)(2,1)S(1)} %collective-permute-done.3.b_ref, bf16[256,4096]{1,0:T(8,128)(2,1)S(1)} %copy-done, bf16[256,4096]{1,0:T(8,128)(2,1)} %collective-permute-done.4.x_ref), custom_call_target="tpu_custom_call" | custom-call | tf_op jit(solution)/shard_map/pallas_call | solution.py:265
  74.0 0.0 collective-permute-done.5.got_ref
  74.1 5.1 %collective-permute-start.6 = (bf16[512,256]{1,0:T(8,128)(2,1)S(1)}, bf16[512,256]{1,0:T(8,128)(2,1)S(1)}, u32[]{:S(2)}, u32[]{:S(2)}) collective-permute-start(bf16[512,256]{1,0:T(8,128)(2,1)S(1)} %shard_map.91), channel_id=1, source_target_pairs={{0,2},{1,3},{2,4},{3,5},{4,6},{5,7},{6,8},{7,9},{8,10},{9,11},{10,... | collective-permute-start | bytes 786440 | tf_op jit(solution)/shard_map/ppermute | solution.py:313
  79.2 0.0 collective-permute-done.7.got_ref
  79.3 1.9 %collective-permute-start.9 = (bf16[512,256]{1,0:T(8,128)(2,1)S(1)}, bf16[512,256]{1,0:T(8,128)(2,1)S(1)}, u32[]{:S(2)}, u32[]{:S(2)}) collective-permute-start(bf16[512,256]{1,0:T(8,128)(2,1)S(1)} %shard_map.92), channel_id=1, source_target_pairs={{0,14},{1,15},{2,0},{3,1},{4,2},{5,3},{6,4},{7,5},{8,6},{9,7},{10,... | collective-permute-start | bytes 786440 | tf_op jit(solution)/shard_map/ppermute | solution.py:313
  81.2 3.3 %collective-permute-done.6.got_ref = bf16[512,256]{1,0:T(8,128)(2,1)S(1)} collective-permute-done((bf16[512,256]{1,0:T(8,128)(2,1)S(1)}, bf16[512,256]{1,0:T(8,128)(2,1)S(1)}, u32[]{:S(2)}, u32[]{:S(2)}) %collective-permute-start.6) | collective-permute-done | bytes 262176 | tf_op jit(solution)/shard_map/ppermute | solution.py:313
  84.5 0.1 shard_map.93
  84.6 5.6 %collective-permute-start.8 = (bf16[512,256]{1,0:T(8,128)(2,1)S(1)}, bf16[512,256]{1,0:T(8,128)(2,1)S(1)}, u32[]{:S(2)}, u32[]{:S(2)}) collective-permute-start(bf16[512,256]{1,0:T(8,128)(2,1)S(1)} %shard_map.93), channel_id=1, source_target_pairs={{0,2},{1,3},{2,4},{3,5},{4,6},{5,7},{6,8},{7,9},{8,10},{9,11},{10,... | collective-permute-start | bytes 786440 | tf_op jit(solution)/shard_map/ppermute | solution.py:313
  90.2 0.0 collective-permute-done.9.got_ref
  90.2 0.1 shard_map.94
  90.2 1.9 %collective-permute-start.11 = (bf16[512,256]{1,0:T(8,128)(2,1)S(1)}, bf16[512,256]{1,0:T(8,128)(2,1)S(1)}, u32[]{:S(2)}, u32[]{:S(2)}) collective-permute-start(bf16[512,256]{1,0:T(8,128)(2,1)S(1)} %shard_map.94), channel_id=1, source_target_pairs={{0,14},{1,15},{2,0},{3,1},{4,2},{5,3},{6,4},{7,5},{8,6},{9,7},{10,... | collective-permute-start | bytes 786440 | tf_op jit(solution)/shard_map/ppermute | solution.py:313
  92.2 2.4 %collective-permute-done.8.got_ref = bf16[512,256]{1,0:T(8,128)(2,1)S(1)} collective-permute-done((bf16[512,256]{1,0:T(8,128)(2,1)S(1)}, bf16[512,256]{1,0:T(8,128)(2,1)S(1)}, u32[]{:S(2)}, u32[]{:S(2)}) %collective-permute-start.8) | collective-permute-done | bytes 262176 | tf_op jit(solution)/shard_map/ppermute | solution.py:313
  94.5 0.1 shard_map.95
  94.6 5.6 %collective-permute-start.10 = (bf16[512,256]{1,0:T(8,128)(2,1)S(1)}, bf16[512,256]{1,0:T(8,128)(2,1)S(1)}, u32[]{:S(2)}, u32[]{:S(2)}) collective-permute-start(bf16[512,256]{1,0:T(8,128)(2,1)S(1)} %shard_map.95), channel_id=1, source_target_pairs={{0,2},{1,3},{2,4},{3,5},{4,6},{5,7},{6,8},{7,9},{8,10},{9,11},{10,... | collective-permute-start | bytes 786440 | tf_op jit(solution)/shard_map/ppermute | solution.py:313
  100.2 0.0 collective-permute-done.11.got_ref
  100.2 0.1 shard_map.96
  100.3 1.9 %collective-permute-start.12 = (bf16[512,256]{1,0:T(8,128)(2,1)S(1)}, bf16[512,256]{1,0:T(8,128)(2,1)S(1)}, u32[]{:S(2)}, u32[]{:S(2)}) collective-permute-start(bf16[512,256]{1,0:T(8,128)(2,1)S(1)} %shard_map.96), channel_id=1, source_target_pairs={{0,14},{1,15},{2,0},{3,1},{4,2},{5,3},{6,4},{7,5},{8,6},{9,7},{10,... | collective-permute-start | bytes 786440 | tf_op jit(solution)/shard_map/ppermute | solution.py:313
  102.2 1.9 %collective-permute-done.10.got_ref = bf16[512,256]{1,0:T(8,128)(2,1)S(1)} collective-permute-done((bf16[512,256]{1,0:T(8,128)(2,1)S(1)}, bf16[512,256]{1,0:T(8,128)(2,1)S(1)}, u32[]{:S(2)}, u32[]{:S(2)}) %collective-permute-start.10) | collective-permute-done | bytes 262176 | tf_op jit(solution)/shard_map/ppermute | solution.py:313
  104.1 0.1 shard_map.97.a_ref
  104.1 5.6 %collective-permute-done.12.b_ref = bf16[512,256]{1,0:T(8,128)(2,1)S(1)} collective-permute-done((bf16[512,256]{1,0:T(8,128)(2,1)S(1)}, bf16[512,256]{1,0:T(8,128)(2,1)S(1)}, u32[]{:S(2)}, u32[]{:S(2)}) %collective-permute-start.12) | collective-permute-done | bytes 262176 | tf_op jit(solution)/shard_map/ppermute | solution.py:313
  109.8 0.7 shard_map.98
  (3 shorter events, 0.1 us)
Async XLA Ops:
  0.0 56.9 %copy-start.5 = (bf16[512,256]{1,0:T(8,128)(2,1)S(1)}, bf16[512,256]{1,0:T(8,128)(2,1)}, u32[]{:S(2)}) copy-start(bf16[512,256]{1,0:T(8,128)(2,1)} %q_ref.1) | copy-start | bytes 786436
  0.0 62.7 %collective-permute-start.4 = (bf16[256,4096]{1,0:T(8,128)(2,1)}, bf16[256,4096]{1,0:T(8,128)(2,1)}, u32[]{:S(2)}, u32[]{:S(2)}) collective-permute-start(bf16[256,4096]{1,0:T(8,128)(2,1)} %w_ref.3), channel_id=1, source_target_pairs={{0,1},{1,0},{2,3},{3,2},{4,5},{5,4},{6,7},{7,6},{8,9},{9,8},{10,11... | collective-permute-start | bytes 6291464 | tf_op jit(solution)/shard_map/ppermute | solution.py:316
  3.1 1.0 copy-start.1
  4.1 1.0 copy-start.3
  5.1 51.7 %copy-start.2 = (bf16[2,512,256]{2,1,0:T(8,128)(2,1)S(1)}, bf16[2,512,256]{2,1,0:T(8,128)(2,1)}, u32[]{:S(2)}) copy-start(bf16[2,512,256]{2,1,0:T(8,128)(2,1)} %k_ref.1) | copy-start | bytes 1572868
  5.1 51.7 %copy-start.4 = (bf16[2,512,256]{2,1,0:T(8,128)(2,1)S(1)}, bf16[2,512,256]{2,1,0:T(8,128)(2,1)}, u32[]{:S(2)}) copy-start(bf16[2,512,256]{2,1,0:T(8,128)(2,1)} %v_ref.1) | copy-start | bytes 1572868
  5.1 51.7 %copy-start.6 = (bf16[512,256]{1,0:T(8,128)(2,1)S(1)}, bf16[512,256]{1,0:T(8,128)(2,1)}, u32[]{:S(2)}) copy-start(bf16[512,256]{1,0:T(8,128)(2,1)} %g_ref.1) | copy-start | bytes 786436
  28.4 6.8 %collective-permute-start = (bf16[2,128,256]{2,1,0:T(8,128)(2,1)S(1)}, bf16[2,128,256]{2,1,0:T(8,128)(2,1)S(1)}, u32[]{:S(2)}, u32[]{:S(2)}) collective-permute-start(bf16[2,128,256]{2,1,0:T(8,128)(2,1)S(1)} %get-tuple-element.28), channel_id=1, source_target_pairs={{0,64},{64,128},{128,192},{192,256},{256,320},{320,384},{384,448},... | collective-permute-start | bytes 393224 | tf_op jit(solution)/shard_map/ppermute | solution.py:320
  35.4 8.7 %collective-permute-start.1 = (bf16[2,128,256]{2,1,0:T(8,128)(2,1)S(1)}, bf16[2,128,256]{2,1,0:T(8,128)(2,1)S(1)}, u32[]{:S(2)}, u32[]{:S(2)}) collective-permute-start(bf16[2,128,256]{2,1,0:T(8,128)(2,1)S(1)} %get-tuple-element.30), channel_id=1, source_target_pairs={{0,128},{64,192},{128,256},{192,320},{256,384},{320,448},{1,129},{... | collective-permute-start | bytes 393224 | tf_op jit(solution)/shard_map/ppermute | solution.py:320
  44.2 14.5 %collective-permute-start.2 = (bf16[2,128,128]{2,1,0:T(8,128)(2,1)S(1)}, bf16[2,128,128]{2,1,0:T(8,128)(2,1)S(1)}, u32[]{:S(2)}, u32[]{:S(2)}) collective-permute-start(bf16[2,128,128]{2,1,0:T(8,128)(2,1)S(1)} %shard_map.86), channel_id=1, source_target_pairs={{0,256},{64,320},{128,384},{192,448},{1,257},{65,321},{129,385},{1... | collective-permute-start | bytes 196616 | tf_op jit(solution)/shard_map/ppermute | solution.py:320
  58.3 4.4 %copy-start = (bf16[256,4096]{1,0:T(8,128)(2,1)S(1)}, bf16[256,4096]{1,0:T(8,128)(2,1)}, u32[]{:S(2)}) copy-start(bf16[256,4096]{1,0:T(8,128)(2,1)} %w_ref.3) | copy-start | bytes 6291460
  59.3 3.4 %collective-permute-start.3 = (bf16[512,256]{1,0:T(8,128)(2,1)S(1)}, bf16[512,256]{1,0:T(8,128)(2,1)S(1)}, u32[]{:S(2)}, u32[]{:S(2)}) collective-permute-start(bf16[512,256]{1,0:T(8,128)(2,1)S(1)} %shard_map.88.a_ref), channel_id=1, source_target_pairs={{0,1},{1,0},{2,3},{3,2},{4,5},{5,4},{6,7},{7,6},{8,9},{9,8},{10,11... | collective-permute-start | bytes 786440 | tf_op jit(solution)/shard_map/ppermute | solution.py:316
  61.2 10.0 %copy-start.7 = (s32[7]{0:T(128)S(1)}, s32[7]{0:T(128)}, u32[]{:S(2)}) copy-start(s32[7]{0:T(128)} %constant.70.clone) | copy-start | bytes 88
  64.6 9.4 %collective-permute-start.5 = (bf16[256,256]{1,0:T(8,128)(2,1)S(1)}, bf16[256,256]{1,0:T(8,128)(2,1)S(1)}, u32[]{:S(2)}, u32[]{:S(2)}) collective-permute-start(bf16[256,256]{1,0:T(8,128)(2,1)S(1)} %get-tuple-element.39), channel_id=1, source_target_pairs={{0,2},{1,3},{2,4},{3,5},{4,6},{5,7},{6,8},{7,9},{8,10},{9,11},{10,... | collective-permute-start | bytes 393224 | tf_op jit(solution)/shard_map/ppermute | solution.py:313
  69.3 9.9 %collective-permute-start.7 = (bf16[256,256]{1,0:T(8,128)(2,1)S(1)}, bf16[256,256]{1,0:T(8,128)(2,1)S(1)}, u32[]{:S(2)}, u32[]{:S(2)}) collective-permute-start(bf16[256,256]{1,0:T(8,128)(2,1)S(1)} %get-tuple-element.40), channel_id=1, source_target_pairs={{0,14},{1,15},{2,0},{3,1},{4,2},{5,3},{6,4},{7,5},{8,6},{9,7},{10,... | collective-permute-start | bytes 393224 | tf_op jit(solution)/shard_map/ppermute | solution.py:313
  74.1 10.4 %collective-permute-start.6 = (bf16[512,256]{1,0:T(8,128)(2,1)S(1)}, bf16[512,256]{1,0:T(8,128)(2,1)S(1)}, u32[]{:S(2)}, u32[]{:S(2)}) collective-permute-start(bf16[512,256]{1,0:T(8,128)(2,1)S(1)} %shard_map.91), channel_id=1, source_target_pairs={{0,2},{1,3},{2,4},{3,5},{4,6},{5,7},{6,8},{7,9},{8,10},{9,11},{10,... | collective-permute-start | bytes 786440 | tf_op jit(solution)/shard_map/ppermute | solution.py:313
  79.3 10.9 %collective-permute-start.9 = (bf16[512,256]{1,0:T(8,128)(2,1)S(1)}, bf16[512,256]{1,0:T(8,128)(2,1)S(1)}, u32[]{:S(2)}, u32[]{:S(2)}) collective-permute-start(bf16[512,256]{1,0:T(8,128)(2,1)S(1)} %shard_map.92), channel_id=1, source_target_pairs={{0,14},{1,15},{2,0},{3,1},{4,2},{5,3},{6,4},{7,5},{8,6},{9,7},{10,... | collective-permute-start | bytes 786440 | tf_op jit(solution)/shard_map/ppermute | solution.py:313
  84.6 10.0 %collective-permute-start.8 = (bf16[512,256]{1,0:T(8,128)(2,1)S(1)}, bf16[512,256]{1,0:T(8,128)(2,1)S(1)}, u32[]{:S(2)}, u32[]{:S(2)}) collective-permute-start(bf16[512,256]{1,0:T(8,128)(2,1)S(1)} %shard_map.93), channel_id=1, source_target_pairs={{0,2},{1,3},{2,4},{3,5},{4,6},{5,7},{6,8},{7,9},{8,10},{9,11},{10,... | collective-permute-start | bytes 786440 | tf_op jit(solution)/shard_map/ppermute | solution.py:313
  90.2 10.0 %collective-permute-start.11 = (bf16[512,256]{1,0:T(8,128)(2,1)S(1)}, bf16[512,256]{1,0:T(8,128)(2,1)S(1)}, u32[]{:S(2)}, u32[]{:S(2)}) collective-permute-start(bf16[512,256]{1,0:T(8,128)(2,1)S(1)} %shard_map.94), channel_id=1, source_target_pairs={{0,14},{1,15},{2,0},{3,1},{4,2},{5,3},{6,4},{7,5},{8,6},{9,7},{10,... | collective-permute-start | bytes 786440 | tf_op jit(solution)/shard_map/ppermute | solution.py:313
  94.6 9.5 %collective-permute-start.10 = (bf16[512,256]{1,0:T(8,128)(2,1)S(1)}, bf16[512,256]{1,0:T(8,128)(2,1)S(1)}, u32[]{:S(2)}, u32[]{:S(2)}) collective-permute-start(bf16[512,256]{1,0:T(8,128)(2,1)S(1)} %shard_map.95), channel_id=1, source_target_pairs={{0,2},{1,3},{2,4},{3,5},{4,6},{5,7},{6,8},{7,9},{8,10},{9,11},{10,... | collective-permute-start | bytes 786440 | tf_op jit(solution)/shard_map/ppermute | solution.py:313
  100.3 9.5 %collective-permute-start.12 = (bf16[512,256]{1,0:T(8,128)(2,1)S(1)}, bf16[512,256]{1,0:T(8,128)(2,1)S(1)}, u32[]{:S(2)}, u32[]{:S(2)}) collective-permute-start(bf16[512,256]{1,0:T(8,128)(2,1)S(1)} %shard_map.96), channel_id=1, source_target_pairs={{0,14},{1,15},{2,0},{3,1},{4,2},{5,3},{6,4},{7,5},{8,6},{9,7},{10,... | collective-permute-start | bytes 786440 | tf_op jit(solution)/shard_map/ppermute | solution.py:313

commit v2 on v1

--- a/solution.py
+++ b/solution.py
@@ -145,7 +145,7 @@
             pltpu.SemaphoreType.DMA((2,)),
         ],
         compiler_params=pltpu.CompilerParams(vmem_limit_bytes=32 * 1024 * 1024),
-    )(k, v, b_rows)
+    )(*(pltpu.with_memory_space_constraint(a, pltpu.HBM) for a in (k, v)), b_rows)
 
 
 def local_kernel(q_ref, k_ref, v_ref, g_ref, x_ref, e_ref, pre_ref, l_ref, m_ref, s_ref):
@@ -277,10 +277,12 @@
     return dot(a_ref[...], w_ref[:, cols]) + dot(b_ref[...], x_ref[:, cols])
 
 
-def far_kernel(at_ref, a_ref, b_ref, w_ref, x_ref, up_ref, down_ref):
+def far_kernel(at_ref, a_ref, b_ref, w_ref, x_ref, ahead_ref, back_ref):
     out = term(at_ref[0], a_ref, b_ref, w_ref, x_ref).astype(BF16)
-    up_ref[...] = out[: up_ref.shape[0]]
-    down_ref[...] = out[up_ref.shape[0] :]
+    cut = ahead_ref.shape[0]
+    flip = at_ref[1] != 0
+    ahead_ref[...] = jnp.where(flip, out[cut:], out[:cut])
+    back_ref[...] = jnp.where(flip, out[:cut], out[cut:])
 
 
 def terms_kernel(at_ref, a_ref, b_ref, w_ref, x_ref, o_ref):
@@ -288,9 +290,14 @@
         o_ref[i] = term(at_ref[i], a_ref, b_ref, w_ref, x_ref)
 
 
-def first_add_kernel(at, rows, terms_ref, got_ref, o_ref):
-    o_ref[...] = terms_ref[at].astype(BF16)
-    o_ref[rows] = (terms_ref[at, rows] + got_ref[...].astype(F32)).astype(BF16)
+def first_add_kernel(at, odd_ref, terms_ref, got_ref, o_ref):
+    cut = got_ref.shape[0]
+    low = odd_ref[0] == at
+    for i in range(2):
+        rows = slice(i * cut, (i + 1) * cut)
+        mine = low if i == 0 else jnp.logical_not(low)
+        got = jnp.where(mine, got_ref[...].astype(F32), 0.0)
+        o_ref[rows] = (terms_ref[at, rows] + got).astype(BF16)
 
 
 def add_kernel(at, terms_ref, got_ref, o_ref):
@@ -309,8 +316,10 @@
     me = lax.axis_index("head")
     chip, core = me // 2, me % 2
 
-    def shift(a, by):
-        return lax.ppermute(a, "head", [(i, (i + 2 * by) % devices) for i in range(devices)])
+    def across(a, odd):
+        pairs = [(c, (c + 1) % chips) for c in range(odd, chips, 2)]
+        both = pairs + [(d, c) for c, d in pairs]
+        return lax.ppermute(a, "head", [(2 * c + i, 2 * d + i) for c, d in both for i in range(2)])
 
     def mate(a):
         return lax.ppermute(a, "head", [(i, i ^ 1) for i in range(devices)])
@@ -346,6 +355,7 @@
         lax.optimization_barrier((prefixes, near))[0],
     )
     send = small(carry_kernel, state_send, pair, far)
+    mate_weight, far = lax.optimization_barrier((mate_weight, far))
     state = later_z(send, 4)
     entry = small(entry_kernel, wide_map, inside, near, far)
     mixed_in = small(
@@ -360,36 +370,39 @@
     mate_in = mate(mixed_in)
 
     half = chips // 2
-    sides = [s for k in range(half - 1, 0, -1) for s in (k, chips - k)] + [0]
-    at = [2 * ((chip + jnp.array(o, jnp.int32)) % chips) + core for o in ([half], sides)]
+    odd = chip % 2
+    sign = 1 - 2 * odd
+    sides = [s for k in range(half - 1, 0, -1) for s in (k, -k)] + [0]
+    at = 2 * ((chip + chips + sign * jnp.array(sides, jnp.int32)) % chips) + core
+    far_at = jnp.stack([2 * ((chip + half) % chips) + core, odd]).astype(jnp.int32)
+    odd = odd.astype(jnp.int32).reshape(1)
 
     weights = (mixed_in, mate_in, out_weight, mate_weight)
     specs = [SM] + [VM] * 4
-    cut = tok // 2
-    part = jax.ShapeDtypeStruct((cut, cols), BF16)
-    up, down = small(far_kernel, (part, part), at[0], *weights, specs=specs)
-    up, down = shift(up, 1), shift(down, -1)
+    part = jax.ShapeDtypeStruct((tok // 2, cols), BF16)
+    ahead, back = small(far_kernel, (part, part), far_at, *weights, specs=specs)
+    back, ahead = across(ahead, 0), across(back, 1)
     several = jax.ShapeDtypeStruct((len(sides), tok, cols), F32)
-    terms = small(terms_kernel, several, at[1], *weights, specs=specs)
+    terms = small(terms_kernel, several, at, *weights, specs=specs)
     sent = jax.ShapeDtypeStruct((tok, cols), BF16)
-    down_sum = None
-    for k in range(half - 1):
-        adders = [functools.partial(add_kernel, 2 * k + i) for i in range(2)]
-        if k == 0:
-            adders = [
-                functools.partial(first_add_kernel, i, r)
-                for i, r in enumerate((slice(0, cut), slice(cut, tok)))
-            ]
-        else:
-            up = lax.optimization_barrier((up, down_sum))[0]
-        up_sum = small(adders[0], sent, terms, up)
-        down = lax.optimization_barrier((down, up_sum))[0]
-        down_sum = small(adders[1], sent, terms, down)
-        up, down = shift(up_sum, 1), shift(down_sum, -1)
-    last = functools.partial(add_kernel, 2 * half - 2)
-    up = lax.optimization_barrier((up, down_sum))[0]
-    total = small(last, tokens, terms, up)
-    return small(last_add_kernel, sent, total, down)
+    arrived, prior = {0: ahead, 1: back}, None
+    for k in range(half):
+        sums = {}
+        for i in (1, 0) if k % 2 == 0 else (0, 1):
+            got = arrived[i]
+            if prior is not None:
+                got = lax.optimization_barrier((got, prior))[0]
+            if k == 0:
+                adder = functools.partial(first_add_kernel, i)
+                sums[i] = small(adder, sent, odd, terms, got, specs=[SM, VM, VM])
+            elif k < half - 1:
+                sums[i] = small(functools.partial(add_kernel, 2 * k + i), sent, terms, got)
+            elif not sums:
+                sums[i] = small(functools.partial(add_kernel, 2 * k), tokens, terms, got)
+            else:
+                return small(last_add_kernel, sent, prior, got)
+            prior = sums[i]
+        arrived = {0: across(sums[1], 1), 1: across(sums[0], 0)}
 
 
 def solution(mesh):

time: 111 us -> 108 us (0.973)
  the two profiles are of different devices: /device:TPU:26 before, /device:TPU:6 now
where the time goes in v2:
time: 108 us; the launch traced here: 107 us
  starting transfers between devices  48.4 us (45%)
  waiting for transfers between devices  22.1 us (20%)
  Pallas kernels  19.2 us (18%)
  blocking collectives  15.9 us (15%)
    ppermute x8, starting transfers between devices, across(): lax.ppermute(a, 'head', [(2 * c + i, 2 * d + i) for c, d in both for i in...  23.8 us
    ppermute x3, starting transfers between devices, later_z(): return lax.ppermute(a, 'ctx_0', [(i, i + by) for i in range(groups - by)])  20.6 us
    all_gather x1, blocking collectives, per_device(): gathered = lax.all_gather(maps, 'ctx_1')  15.9 us
    ppermute x8, waiting for transfers between devices, across(): lax.ppermute(a, 'head', [(2 * c + i, 2 * d + i) for c, d in both for i in...  15.6 us
    pallas_call x1, Pallas kernels, local_maps(): pl.pallas_call(functools.partial(map_kernel, group), out_shape=(jax.Shape...  10.2 us
    pallas_call x16, Pallas kernels, small(): pl.pallas_call(kernel, out_shape=outs, in_specs=specs or [VM] * len(args)...  9.07 us
    ppermute x3, waiting for transfers between devices, later_z(): return lax.ppermute(a, 'ctx_0', [(i, i + by) for i in range(groups - by)])  5.06 us
    ppermute x2, starting transfers between devices, mate(): return lax.ppermute(a, 'head', [(i, i ^ 1) for i in range(devices)])  3.98 us
  transfers between devices with their start and end apart: 13, of which 9 were waited for; matrix products, arithmetic and copies ran while one was open for 1% of the time, Pallas kernels for 15%

profile of v2, /device:TPU:6, one launch (start us, length us, event | category | flops | bytes accessed | tf_op | source)
XLA Modules:
  0.0 107.1 jit_solution(10251484871659765396)
XLA Ops:
  0.0 0.0 copy-start.2
  0.0 0.0 copy-start.1
  0.0 0.0 copy-start.4
  0.0 0.0 copy-start.3
  0.0 2.1 %collective-permute-start.1 = (bf16[256,4096]{1,0:T(8,128)(2,1)}, bf16[256,4096]{1,0:T(8,128)(2,1)}, u32[]{:S(2)}, u32[]{:S(2)}) collective-permute-start(bf16[256,4096]{1,0:T(8,128)(2,1)} %w_ref.3), channel_id=1, source_target_pairs={{0,1},{1,0},{2,3},{3,2},{4,5},{5,4},{6,7},{7,6},{8,9},{9,8},{10,11... | collective-permute-start | bytes 6291464 | tf_op jit(solution)/shard_map/ppermute | solution.py:325
  2.1 0.8 reshape.13
  2.9 0.1 copy.11
  3.0 0.1 reshape.14.b_ref
  3.1 10.2 %shard_map.73 = (bf16[2,128,256]{2,1,0:T(8,128)(2,1)S(1)}, bf16[16,128,256]{2,1,0:T(8,128)(2,1)S(1)}, f32[16,2,128]{2,1,0:T(2,128)S(1)}, bf16[16,128,256]{2,1,0:T(8,128)(2,1)S(1)}) custom-call(bf16[2,512,256]{2,1,0:T(8,128)(2,1)} %k_ref.1, bf16[2,512,256]{2,1,0:T(8,128)(2,1)} %v_ref.1, f32[16,128]{1,0:T(8,128)S(1)} %reshape.14.b_ref), custom_call_target="tpu_custom_call" | custom-call | tf_op jit(solution)/shard_map/pallas_call | solution.py:130
  13.3 15.9 %all-gather = bf16[8,128,256]{2,1,0:T(8,128)(2,1)S(1)} all-gather(bf16[2,128,256]{2,1,0:T(8,128)(2,1)S(1)} %get-tuple-element.29), channel_id=2, replica_groups=mesh['ctx_0'=8,'ctx_1'=4,'head'=16] {'ctx_1'}, dimensions={0}, use_global_device_ids=true | all-gather | bytes 655360 | tf_op jit(solution)/shard_map/all_gather | solution.py:337
  29.2 0.6 shard_map.74
  29.8 1.8 %collective-permute-start = (bf16[2,128,256]{2,1,0:T(8,128)(2,1)S(1)}, bf16[2,128,256]{2,1,0:T(8,128)(2,1)S(1)}, u32[]{:S(2)}, u32[]{:S(2)}) collective-permute-start(bf16[2,128,256]{2,1,0:T(8,128)(2,1)S(1)} %get-tuple-element.31), channel_id=1, source_target_pairs={{0,64},{64,128},{128,192},{192,256},{256,320},{320,384},{384,448},... | collective-permute-start | bytes 393224 | tf_op jit(solution)/shard_map/ppermute | solution.py:329
  31.6 2.5 %collective-permute-done.earlier_ref.near_ref = bf16[2,128,256]{2,1,0:T(8,128)(2,1)S(1)} collective-permute-done((bf16[2,128,256]{2,1,0:T(8,128)(2,1)S(1)}, bf16[2,128,256]{2,1,0:T(8,128)(2,1)S(1)}, u32[]{:S(2)}, u32[]{:S(2)}) %collective-permute-start) | collective-permute-done | bytes 131104 | tf_op jit(solution)/shard_map/ppermute | solution.py:329
  34.1 0.2 shard_map.75
  34.3 6.2 %collective-permute-start.2 = (bf16[2,128,256]{2,1,0:T(8,128)(2,1)S(1)}, bf16[2,128,256]{2,1,0:T(8,128)(2,1)S(1)}, u32[]{:S(2)}, u32[]{:S(2)}) collective-permute-start(bf16[2,128,256]{2,1,0:T(8,128)(2,1)S(1)} %get-tuple-element.33), channel_id=1, source_target_pairs={{0,128},{64,192},{128,256},{192,320},{256,384},{320,448},{1,129},{... | collective-permute-start | bytes 393224 | tf_op jit(solution)/shard_map/ppermute | solution.py:329
  40.5 2.5 %collective-permute-done.2.far_ref.earlier_ref = bf16[2,128,256]{2,1,0:T(8,128)(2,1)S(1)} collective-permute-done((bf16[2,128,256]{2,1,0:T(8,128)(2,1)S(1)}, bf16[2,128,256]{2,1,0:T(8,128)(2,1)S(1)}, u32[]{:S(2)}, u32[]{:S(2)}) %collective-permute-start.2) | collective-permute-done | bytes 131104 | tf_op jit(solution)/shard_map/ppermute | solution.py:329
  43.0 0.2 shard_map.77
  43.2 12.6 %collective-permute-start.3 = (bf16[2,128,128]{2,1,0:T(8,128)(2,1)S(1)}, bf16[2,128,128]{2,1,0:T(8,128)(2,1)S(1)}, u32[]{:S(2)}, u32[]{:S(2)}) collective-permute-start(bf16[2,128,128]{2,1,0:T(8,128)(2,1)S(1)} %shard_map.77), channel_id=1, source_target_pairs={{0,256},{64,320},{128,384},{192,448},{1,257},{65,321},{129,385},{1... | collective-permute-start | bytes 196616 | tf_op jit(solution)/shard_map/ppermute | solution.py:329
  55.8 0.0 copy-done.2
  55.8 0.0 copy-done.1
  55.8 0.0 copy-done.4
  55.8 0.0 copy-done.3
  55.8 1.4 %shard_map.78 = (f32[512,256]{1,0:T(8,128)S(1)}, bf16[512,256]{1,0:T(8,128)(2,1)S(1)}, f32[512,256]{1,0:T(8,128)S(1)}) custom-call(bf16[512,256]{1,0:T(8,128)(2,1)S(1)} %copy-done.3, bf16[2,512,256]{2,1,0:T(8,128)(2,1)S(1)} %copy-done.1, bf16[2,512,256]{2,1,0:T(8,128)(2,1)S(1)} %copy-done.2, bf16[512,256]{1,0:T(8,128)(2,1)S(1)} %copy-done.4, ...), custom_call_target="tpu_custom_call" | custom-call | tf_op jit(solution)/shard_map/pallas_call | solution.py:265
  57.2 0.0 copy-start
  57.2 0.0 collective-permute-done.1.x_ref
  57.2 0.4 shard_map.76.entry_ref
  57.6 0.1 collective-permute-done.3.state_ref
  57.7 0.5 shard_map.79.a_ref
  58.2 1.9 %collective-permute-start.4 = (bf16[512,256]{1,0:T(8,128)(2,1)S(1)}, bf16[512,256]{1,0:T(8,128)(2,1)S(1)}, u32[]{:S(2)}, u32[]{:S(2)}) collective-permute-start(bf16[512,256]{1,0:T(8,128)(2,1)S(1)} %shard_map.79.a_ref), channel_id=1, source_target_pairs={{0,1},{1,0},{2,3},{3,2},{4,5},{5,4},{6,7},{7,6},{8,9},{9,8},{10,11... | collective-permute-start | bytes 786440 | tf_op jit(solution)/shard_map/ppermute | solution.py:325
  60.2 0.1 pad_add_fusion.at_ref
  60.3 0.0 copy-start.5
  60.3 1.4 %collective-permute-done.4.b_ref = bf16[512,256]{1,0:T(8,128)(2,1)S(1)} collective-permute-done((bf16[512,256]{1,0:T(8,128)(2,1)S(1)}, bf16[512,256]{1,0:T(8,128)(2,1)S(1)}, u32[]{:S(2)}, u32[]{:S(2)}) %collective-permute-start.4) | collective-permute-done | bytes 262176 | tf_op jit(solution)/shard_map/ppermute | solution.py:325
  61.6 0.0 copy-done
  61.6 1.9 %shard_map.81 = (bf16[256,256]{1,0:T(8,128)(2,1)S(1)}, bf16[256,256]{1,0:T(8,128)(2,1)S(1)}) custom-call(s32[2]{0:T(128)S(1)} %pad_add_fusion.at_ref, bf16[512,256]{1,0:T(8,128)(2,1)S(1)} %shard_map.79.a_ref, bf16[512,256]{1,0:T(8,128)(2,1)S(1)} %collective-permute-done.4.b_ref, bf16[256,4096]{1,0:T(8,128)(2,1)S(1)} %copy-done, ...), custom_call_target="tpu_custom_call" | custom-call | tf_op jit(solution)/shard_map/pallas_call | solution.py:265
  63.5 3.5 %collective-permute-start.5 = (bf16[256,256]{1,0:T(8,128)(2,1)S(1)}, bf16[256,256]{1,0:T(8,128)(2,1)S(1)}, u32[]{:S(2)}, u32[]{:S(2)}) collective-permute-start(bf16[256,256]{1,0:T(8,128)(2,1)S(1)} %get-tuple-element.44), channel_id=1, source_target_pairs={{0,2},{1,3},{4,6},{5,7},{8,10},{9,11},{12,14},{13,15},{2,0},{3,1},... | collective-permute-start | bytes 393224 | tf_op jit(solution)/shard_map/ppermute | solution.py:322
  67.1 5.1 %collective-permute-start.7 = (bf16[256,256]{1,0:T(8,128)(2,1)S(1)}, bf16[256,256]{1,0:T(8,128)(2,1)S(1)}, u32[]{:S(2)}, u32[]{:S(2)}) collective-permute-start(bf16[256,256]{1,0:T(8,128)(2,1)S(1)} %get-tuple-element.45), channel_id=1, source_target_pairs={{2,4},{3,5},{6,8},{7,9},{10,12},{11,13},{14,0},{15,1},{4,2},{5,3},... | collective-permute-start | bytes 393224 | tf_op jit(solution)/shard_map/ppermute | solution.py:322
  72.2 0.0 copy-done.5
  72.2 2.7 %shard_map.80.terms_ref = f32[7,512,256]{2,1,0:T(8,128)S(1)} custom-call(s32[7]{0:T(128)S(1)} %fusion.1.at_ref, bf16[512,256]{1,0:T(8,128)(2,1)S(1)} %shard_map.79.a_ref, bf16[512,256]{1,0:T(8,128)(2,1)S(1)} %collective-permute-done.4.b_ref, bf16[256,4096]{1,0:T(8,128)(2,1)S(1)} %copy-done, bf16[256,4096]{1,0:T(8,128)(2,1)} %collective-permute-done.1.x_ref), custom_call_target="tpu_custom_call" | custom-call | tf_op jit(solution)/shard_map/pallas_call | solution.py:265
  75.0 0.0 collective-permute-done.5.got_ref
  75.0 0.1 shard_map.82
  75.1 1.9 %collective-permute-start.6 = (bf16[512,256]{1,0:T(8,128)(2,1)S(1)}, bf16[512,256]{1,0:T(8,128)(2,1)S(1)}, u32[]{:S(2)}, u32[]{:S(2)}) collective-permute-start(bf16[512,256]{1,0:T(8,128)(2,1)S(1)} %shard_map.82), channel_id=1, source_target_pairs={{2,4},{3,5},{6,8},{7,9},{10,12},{11,13},{14,0},{15,1},{4,2},{5,3},... | collective-permute-start | bytes 786440 | tf_op jit(solution)/shard_map/ppermute | solution.py:322
  77.0 0.0 collective-permute-done.7.got_ref
  77.0 0.1 shard_map.83
  77.1 1.9 %collective-permute-start.9 = (bf16[512,256]{1,0:T(8,128)(2,1)S(1)}, bf16[512,256]{1,0:T(8,128)(2,1)S(1)}, u32[]{:S(2)}, u32[]{:S(2)}) collective-permute-start(bf16[512,256]{1,0:T(8,128)(2,1)S(1)} %shard_map.83), channel_id=1, source_target_pairs={{0,2},{1,3},{4,6},{5,7},{8,10},{9,11},{12,14},{13,15},{2,0},{3,1},... | collective-permute-start | bytes 786440 | tf_op jit(solution)/shard_map/ppermute | solution.py:322
  79.0 7.0 %collective-permute-done.6.got_ref = bf16[512,256]{1,0:T(8,128)(2,1)S(1)} collective-permute-done((bf16[512,256]{1,0:T(8,128)(2,1)S(1)}, bf16[512,256]{1,0:T(8,128)(2,1)S(1)}, u32[]{:S(2)}, u32[]{:S(2)}) %collective-permute-start.6) | collective-permute-done | bytes 262176 | tf_op jit(solution)/shard_map/ppermute | solution.py:322
  86.0 1.9 %collective-permute-start.8 = (bf16[512,256]{1,0:T(8,128)(2,1)S(1)}, bf16[512,256]{1,0:T(8,128)(2,1)S(1)}, u32[]{:S(2)}, u32[]{:S(2)}) collective-permute-start(bf16[512,256]{1,0:T(8,128)(2,1)S(1)} %shard_map.84), channel_id=1, source_target_pairs={{0,2},{1,3},{4,6},{5,7},{8,10},{9,11},{12,14},{13,15},{2,0},{3,1},... | collective-permute-start | bytes 786440 | tf_op jit(solution)/shard_map/ppermute | solution.py:322
  87.9 0.0 collective-permute-done.9.got_ref
  87.9 0.1 shard_map.85
  88.0 3.7 %collective-permute-start.11 = (bf16[512,256]{1,0:T(8,128)(2,1)S(1)}, bf16[512,256]{1,0:T(8,128)(2,1)S(1)}, u32[]{:S(2)}, u32[]{:S(2)}) collective-permute-start(bf16[512,256]{1,0:T(8,128)(2,1)S(1)} %shard_map.85), channel_id=1, source_target_pairs={{2,4},{3,5},{6,8},{7,9},{10,12},{11,13},{14,0},{15,1},{4,2},{5,3},... | collective-permute-start | bytes 786440 | tf_op jit(solution)/shard_map/ppermute | solution.py:322
  91.7 3.1 %collective-permute-done.8.got_ref = bf16[512,256]{1,0:T(8,128)(2,1)S(1)} collective-permute-done((bf16[512,256]{1,0:T(8,128)(2,1)S(1)}, bf16[512,256]{1,0:T(8,128)(2,1)S(1)}, u32[]{:S(2)}, u32[]{:S(2)}) %collective-permute-start.8) | collective-permute-done | bytes 262176 | tf_op jit(solution)/shard_map/ppermute | solution.py:322
  94.8 0.1 shard_map.86
  94.8 2.5 %collective-permute-start.10 = (bf16[512,256]{1,0:T(8,128)(2,1)S(1)}, bf16[512,256]{1,0:T(8,128)(2,1)S(1)}, u32[]{:S(2)}, u32[]{:S(2)}) collective-permute-start(bf16[512,256]{1,0:T(8,128)(2,1)S(1)} %shard_map.86), channel_id=1, source_target_pairs={{2,4},{3,5},{6,8},{7,9},{10,12},{11,13},{14,0},{15,1},{4,2},{5,3},... | collective-permute-start | bytes 786440 | tf_op jit(solution)/shard_map/ppermute | solution.py:322
  97.4 0.6 collective-permute-done.11.got_ref
  98.0 0.1 shard_map.87
  98.0 3.2 %collective-permute-start.12 = (bf16[512,256]{1,0:T(8,128)(2,1)S(1)}, bf16[512,256]{1,0:T(8,128)(2,1)S(1)}, u32[]{:S(2)}, u32[]{:S(2)}) collective-permute-start(bf16[512,256]{1,0:T(8,128)(2,1)S(1)} %shard_map.87), channel_id=1, source_target_pairs={{0,2},{1,3},{4,6},{5,7},{8,10},{9,11},{12,14},{13,15},{2,0},{3,1},... | collective-permute-start | bytes 786440 | tf_op jit(solution)/shard_map/ppermute | solution.py:322
  101.3 3.0 %collective-permute-done.10.got_ref = bf16[512,256]{1,0:T(8,128)(2,1)S(1)} collective-permute-done((bf16[512,256]{1,0:T(8,128)(2,1)S(1)}, bf16[512,256]{1,0:T(8,128)(2,1)S(1)}, u32[]{:S(2)}, u32[]{:S(2)}) %collective-permute-start.10) | collective-permute-done | bytes 262176 | tf_op jit(solution)/shard_map/ppermute | solution.py:322
  104.3 0.1 shard_map.88.a_ref
  104.4 1.9 %collective-permute-done.12.b_ref = bf16[512,256]{1,0:T(8,128)(2,1)S(1)} collective-permute-done((bf16[512,256]{1,0:T(8,128)(2,1)S(1)}, bf16[512,256]{1,0:T(8,128)(2,1)S(1)}, u32[]{:S(2)}, u32[]{:S(2)}) %collective-permute-start.12) | collective-permute-done | bytes 262176 | tf_op jit(solution)/shard_map/ppermute | solution.py:322
  106.3 0.7 shard_map.89
  (2 shorter events, 0.1 us)
Async XLA Ops:
  0.0 55.8 %copy-start.2 = (bf16[2,512,256]{2,1,0:T(8,128)(2,1)S(1)}, bf16[2,512,256]{2,1,0:T(8,128)(2,1)}, u32[]{:S(2)}) copy-start(bf16[2,512,256]{2,1,0:T(8,128)(2,1)} %v_ref.1) | copy-start | bytes 1572868
  0.0 55.8 %copy-start.1 = (bf16[2,512,256]{2,1,0:T(8,128)(2,1)S(1)}, bf16[2,512,256]{2,1,0:T(8,128)(2,1)}, u32[]{:S(2)}) copy-start(bf16[2,512,256]{2,1,0:T(8,128)(2,1)} %k_ref.1) | copy-start | bytes 1572868
  0.0 55.8 %copy-start.4 = (bf16[512,256]{1,0:T(8,128)(2,1)S(1)}, bf16[512,256]{1,0:T(8,128)(2,1)}, u32[]{:S(2)}) copy-start(bf16[512,256]{1,0:T(8,128)(2,1)} %g_ref.1) | copy-start | bytes 786436
  0.0 55.8 %copy-start.3 = (bf16[512,256]{1,0:T(8,128)(2,1)S(1)}, bf16[512,256]{1,0:T(8,128)(2,1)}, u32[]{:S(2)}) copy-start(bf16[512,256]{1,0:T(8,128)(2,1)} %q_ref.1) | copy-start | bytes 786436
  0.0 57.2 %collective-permute-start.1 = (bf16[256,4096]{1,0:T(8,128)(2,1)}, bf16[256,4096]{1,0:T(8,128)(2,1)}, u32[]{:S(2)}, u32[]{:S(2)}) collective-permute-start(bf16[256,4096]{1,0:T(8,128)(2,1)} %w_ref.3), channel_id=1, source_target_pairs={{0,1},{1,0},{2,3},{3,2},{4,5},{5,4},{6,7},{7,6},{8,9},{9,8},{10,11... | collective-permute-start | bytes 6291464 | tf_op jit(solution)/shard_map/ppermute | solution.py:325
  29.8 4.3 %collective-permute-start = (bf16[2,128,256]{2,1,0:T(8,128)(2,1)S(1)}, bf16[2,128,256]{2,1,0:T(8,128)(2,1)S(1)}, u32[]{:S(2)}, u32[]{:S(2)}) collective-permute-start(bf16[2,128,256]{2,1,0:T(8,128)(2,1)S(1)} %get-tuple-element.31), channel_id=1, source_target_pairs={{0,64},{64,128},{128,192},{192,256},{256,320},{320,384},{384,448},... | collective-permute-start | bytes 393224 | tf_op jit(solution)/shard_map/ppermute | solution.py:329
  34.3 8.7 %collective-permute-start.2 = (bf16[2,128,256]{2,1,0:T(8,128)(2,1)S(1)}, bf16[2,128,256]{2,1,0:T(8,128)(2,1)S(1)}, u32[]{:S(2)}, u32[]{:S(2)}) collective-permute-start(bf16[2,128,256]{2,1,0:T(8,128)(2,1)S(1)} %get-tuple-element.33), channel_id=1, source_target_pairs={{0,128},{64,192},{128,256},{192,320},{256,384},{320,448},{1,129},{... | collective-permute-start | bytes 393224 | tf_op jit(solution)/shard_map/ppermute | solution.py:329
  43.2 14.5 %collective-permute-start.3 = (bf16[2,128,128]{2,1,0:T(8,128)(2,1)S(1)}, bf16[2,128,128]{2,1,0:T(8,128)(2,1)S(1)}, u32[]{:S(2)}, u32[]{:S(2)}) collective-permute-start(bf16[2,128,128]{2,1,0:T(8,128)(2,1)S(1)} %shard_map.77), channel_id=1, source_target_pairs={{0,256},{64,320},{128,384},{192,448},{1,257},{65,321},{129,385},{1... | collective-permute-start | bytes 196616 | tf_op jit(solution)/shard_map/ppermute | solution.py:329
  57.2 4.4 %copy-start = (bf16[256,4096]{1,0:T(8,128)(2,1)S(1)}, bf16[256,4096]{1,0:T(8,128)(2,1)}, u32[]{:S(2)}) copy-start(bf16[256,4096]{1,0:T(8,128)(2,1)} %w_ref.3) | copy-start | bytes 6291460
  58.2 3.4 %collective-permute-start.4 = (bf16[512,256]{1,0:T(8,128)(2,1)S(1)}, bf16[512,256]{1,0:T(8,128)(2,1)S(1)}, u32[]{:S(2)}, u32[]{:S(2)}) collective-permute-start(bf16[512,256]{1,0:T(8,128)(2,1)S(1)} %shard_map.79.a_ref), channel_id=1, source_target_pairs={{0,1},{1,0},{2,3},{3,2},{4,5},{5,4},{6,7},{7,6},{8,9},{9,8},{10,11... | collective-permute-start | bytes 786440 | tf_op jit(solution)/shard_map/ppermute | solution.py:325
  60.3 11.9 %copy-start.5 = (s32[7]{0:T(128)S(1)}, s32[7]{0:T(128)}, u32[]{:S(2)}) copy-start(s32[7]{0:T(128)} %constant.61.clone) | copy-start | bytes 88
  63.5 11.4 %collective-permute-start.5 = (bf16[256,256]{1,0:T(8,128)(2,1)S(1)}, bf16[256,256]{1,0:T(8,128)(2,1)S(1)}, u32[]{:S(2)}, u32[]{:S(2)}) collective-permute-start(bf16[256,256]{1,0:T(8,128)(2,1)S(1)} %get-tuple-element.44), channel_id=1, source_target_pairs={{0,2},{1,3},{4,6},{5,7},{8,10},{9,11},{12,14},{13,15},{2,0},{3,1},... | collective-permute-start | bytes 393224 | tf_op jit(solution)/shard_map/ppermute | solution.py:322
  67.1 9.9 %collective-permute-start.7 = (bf16[256,256]{1,0:T(8,128)(2,1)S(1)}, bf16[256,256]{1,0:T(8,128)(2,1)S(1)}, u32[]{:S(2)}, u32[]{:S(2)}) collective-permute-start(bf16[256,256]{1,0:T(8,128)(2,1)S(1)} %get-tuple-element.45), channel_id=1, source_target_pairs={{2,4},{3,5},{6,8},{7,9},{10,12},{11,13},{14,0},{15,1},{4,2},{5,3},... | collective-permute-start | bytes 393224 | tf_op jit(solution)/shard_map/ppermute | solution.py:322
  75.1 10.9 %collective-permute-start.6 = (bf16[512,256]{1,0:T(8,128)(2,1)S(1)}, bf16[512,256]{1,0:T(8,128)(2,1)S(1)}, u32[]{:S(2)}, u32[]{:S(2)}) collective-permute-start(bf16[512,256]{1,0:T(8,128)(2,1)S(1)} %shard_map.82), channel_id=1, source_target_pairs={{2,4},{3,5},{6,8},{7,9},{10,12},{11,13},{14,0},{15,1},{4,2},{5,3},... | collective-permute-start | bytes 786440 | tf_op jit(solution)/shard_map/ppermute | solution.py:322
  77.1 10.9 %collective-permute-start.9 = (bf16[512,256]{1,0:T(8,128)(2,1)S(1)}, bf16[512,256]{1,0:T(8,128)(2,1)S(1)}, u32[]{:S(2)}, u32[]{:S(2)}) collective-permute-start(bf16[512,256]{1,0:T(8,128)(2,1)S(1)} %shard_map.83), channel_id=1, source_target_pairs={{0,2},{1,3},{4,6},{5,7},{8,10},{9,11},{12,14},{13,15},{2,0},{3,1},... | collective-permute-start | bytes 786440 | tf_op jit(solution)/shard_map/ppermute | solution.py:322
  86.0 8.8 %collective-permute-start.8 = (bf16[512,256]{1,0:T(8,128)(2,1)S(1)}, bf16[512,256]{1,0:T(8,128)(2,1)S(1)}, u32[]{:S(2)}, u32[]{:S(2)}) collective-permute-start(bf16[512,256]{1,0:T(8,128)(2,1)S(1)} %shard_map.84), channel_id=1, source_target_pairs={{0,2},{1,3},{4,6},{5,7},{8,10},{9,11},{12,14},{13,15},{2,0},{3,1},... | collective-permute-start | bytes 786440 | tf_op jit(solution)/shard_map/ppermute | solution.py:322
  88.0 10.0 %collective-permute-start.11 = (bf16[512,256]{1,0:T(8,128)(2,1)S(1)}, bf16[512,256]{1,0:T(8,128)(2,1)S(1)}, u32[]{:S(2)}, u32[]{:S(2)}) collective-permute-start(bf16[512,256]{1,0:T(8,128)(2,1)S(1)} %shard_map.85), channel_id=1, source_target_pairs={{2,4},{3,5},{6,8},{7,9},{10,12},{11,13},{14,0},{15,1},{4,2},{5,3},... | collective-permute-start | bytes 786440 | tf_op jit(solution)/shard_map/ppermute | solution.py:322
  94.8 9.5 %collective-permute-start.10 = (bf16[512,256]{1,0:T(8,128)(2,1)S(1)}, bf16[512,256]{1,0:T(8,128)(2,1)S(1)}, u32[]{:S(2)}, u32[]{:S(2)}) collective-permute-start(bf16[512,256]{1,0:T(8,128)(2,1)S(1)} %shard_map.86), channel_id=1, source_target_pairs={{2,4},{3,5},{6,8},{7,9},{10,12},{11,13},{14,0},{15,1},{4,2},{5,3},... | collective-permute-start | bytes 786440 | tf_op jit(solution)/shard_map/ppermute | solution.py:322
  98.0 8.3 %collective-permute-start.12 = (bf16[512,256]{1,0:T(8,128)(2,1)S(1)}, bf16[512,256]{1,0:T(8,128)(2,1)S(1)}, u32[]{:S(2)}, u32[]{:S(2)}) collective-permute-start(bf16[512,256]{1,0:T(8,128)(2,1)S(1)} %shard_map.87), channel_id=1, source_target_pairs={{0,2},{1,3},{4,6},{5,7},{8,10},{9,11},{12,14},{13,15},{2,0},{3,1},... | collective-permute-start | bytes 786440 | tf_op jit(solution)/shard_map/ppermute | solution.py:322

commit v3 on v1

--- a/solution.py
+++ b/solution.py
@@ -78,7 +78,7 @@
     get_k.wait()
     get_v.wait()
 
-    def body(step, carry):
+    for step in range(blocks // group):
         probs = [(step * group + i, h) for i in range(group) for h in range(heads)]
         kb = [read_block(k_ref, blk, h) for blk, h in probs]
         num = range(len(probs))
@@ -87,7 +87,16 @@
             blk, h = probs[i]
             gram = dot_nt(kb[i], kb[i])
             n2 = jnp.sum(gram * eye, axis=0, keepdims=True) + 1e-6
-            e.append(b_ref[pl.ds(h * blocks + blk, 1), :] / n2)
+            first = blk * SPAN
+            beta = jnp.concatenate(
+                [
+                    b_ref[h, j : j + 1, first + 16 * g : first + 16 * (g + 1)]
+                    for g in range(SPAN // 16)
+                    for j in range(2)
+                ],
+                axis=1,
+            )
+            e.append(beta / n2)
             n.append(jnp.sqrt(n2))
             e_ref[h * blocks + blk] = jnp.concatenate([e[i], n[i]], axis=0)
             N.append(jnp.where(lev_ref[...] >= 0, gram * e[i], 0.0))
@@ -116,14 +125,11 @@
             pre_ref[h * blocks + blk] = ph
             new = dot(A[i], square(ph)) + dot(A[i][:, :HD], plo)
             p_ref[h] = new + jnp.concatenate([jnp.zeros((HD, HD), F32), B[i]], axis=1)
-        return carry
-
-    lax.fori_loop(0, blocks // group, body, 0)
     for h in range(heads):
         ab_ref[h] = p_ref[h].astype(BF16)
 
 
-def local_maps(k, v, b_rows, group):
+def local_maps(k, v, betas, group):
     _, tok, cols = k.shape
     heads = cols // HD
     count = heads * tok // SPAN
@@ -144,8 +150,8 @@
             pltpu.VMEM((heads, HD, 2 * HD), F32),
             pltpu.SemaphoreType.DMA((2,)),
         ],
-        compiler_params=pltpu.CompilerParams(vmem_limit_bytes=32 * 1024 * 1024),
-    )(k, v, b_rows)
+        compiler_params=pltpu.CompilerParams(vmem_limit_bytes=16 * 1024 * 1024),
+    )(*(pltpu.with_memory_space_constraint(a, pltpu.HBM) for a in (k, v)), betas)
 
 
 def local_kernel(q_ref, k_ref, v_ref, g_ref, x_ref, e_ref, pre_ref, l_ref, m_ref, s_ref):
@@ -185,16 +191,6 @@
         s_ref[rows, cols] = gate / (1.0 + jnp.exp(-gate))
 
 
-def beta_rows(betas):
-    heads, _, tok = betas.shape
-    blocks = tok // SPAN
-    return (
-        betas.reshape(heads, 2, blocks, SPAN // 16, 16)
-        .transpose(0, 2, 3, 1, 4)
-        .reshape(heads * blocks, 2 * SPAN)
-    )
-
-
 def affine(a, b):
     return jnp.concatenate([a, b], axis=1)
 
@@ -202,55 +198,60 @@
 def fold_kernel(x_ref, m_ref, send_ref, tot_ref, in_ref):
     peers, heads = m_ref.shape[:2]
     x = x_ref[0]
+    mine = x % heads
     r = lax.broadcasted_iota(jnp.int32, (HD, 2 * HD), 0)
     c = lax.broadcasted_iota(jnp.int32, (HD, 2 * HD), 1)
     zero = jnp.zeros((HD, HD), F32)
+
+    def after(total, later):
+        prod = halves(dot(later[:, :HD], jnp.concatenate(split(total), axis=1)))
+        return prod + affine(zero, later[:, HD:].astype(F32))
+
     total = [m_ref[0, h].astype(F32) for h in range(heads)]
     inside = [(r == c).astype(F32)] * heads
     for k in range(1, peers):
         for h in range(heads):
             inside[h] = jnp.where(x == k, total[h], inside[h])
-            later = m_ref[k, h]
-            prod = halves(dot(later[:, :HD], jnp.concatenate(split(total[h]), axis=1)))
-            total[h] = prod + affine(zero, later[:, HD:].astype(F32))
+        if k < peers - 1:
+            total = [after(total[h], m_ref[k, h]) for h in range(heads)]
+    own = total[0]
+    for h in range(1, heads):
+        own = jnp.where(mine == h, total[h], own)
+    own = after(own, m_ref[peers - 1, mine])
+    send_ref[...] = own.astype(BF16)
+    tot_ref[...] = own
     for h in range(heads):
-        send_ref[h] = total[h].astype(BF16)
-        tot_ref[h] = total[h]
         in_ref[h] = inside[h]
 
 
 def join_kernel(later_ref, earlier_ref, send_ref, out_ref):
+    later = later_ref[...]
     zero = jnp.zeros((HD, HD), F32)
-    for h in range(later_ref.shape[0]):
-        later = later_ref[h]
-        out = dot(wide(later[:, :HD]), square(earlier_ref[h])) + affine(zero, later[:, HD:])
-        send_ref[h] = out.astype(BF16)
-        out_ref[h] = out
+    out = dot(wide(later[:, :HD]), square(earlier_ref[...])) + affine(zero, later[:, HD:])
+    send_ref[...] = out.astype(BF16)
+    out_ref[...] = out
 
 
 def carry_kernel(later_ref, earlier_ref, send_ref):
-    for h in range(later_ref.shape[0]):
-        later = later_ref[h]
-        state = dot(wide(later[:, :HD]), square(earlier_ref[h][:, HD:])) + later[:, HD:]
-        send_ref[h] = state.astype(BF16)
-
-
-def entry_kernel(in_ref, near_ref, far_ref, out_ref):
+    later = later_ref[...]
+    earlier = earlier_ref[...]
+    state = dot(wide(later[:, :HD]), square(earlier[:, -HD:])) + later[:, HD:]
+    send_ref[...] = state.astype(BF16)
+
+
+def entry_kernel(near_ref, far_ref, out_ref):
+    near = near_ref[...]
     zero = jnp.zeros((HD, HD), F32)
-    for h in range(in_ref.shape[0]):
-        near = near_ref[h]
-        both = dot(near[:, :HD], far_ref[h]) + affine(zero, near[:, HD:].astype(F32))
+    out_ref[...] = dot(near[:, :HD], far_ref[...]) + affine(zero, near[:, HD:].astype(F32))
+
+
+def mix_kernel(x_ref, in_ref, own_ref, other_ref, l_ref, m_ref, s_ref, o_ref):
+    heads = in_ref.shape[0]
+    mine = x_ref[0] % heads
+    for h in range(heads):
+        state = jnp.where(mine == h, own_ref[...].astype(F32), other_ref[...].astype(F32))
         inner = in_ref[h]
-        bh, bl = split(both)
-        lhs = wide(inner[:, :HD])
-        out = dot(lhs, square(bh)) + dot(lhs[:, :HD], bl)
-        out_ref[h] = out + affine(zero, inner[:, HD:])
-
-
-def mix_kernel(entry_ref, state_ref, l_ref, m_ref, s_ref, o_ref):
-    for h in range(entry_ref.shape[0]):
-        entry = entry_ref[h]
-        start = dot(wide(entry[:, :HD]), square(state_ref[h])) + entry[:, HD:]
+        start = dot(wide(inner[:, :HD]), square(state.astype(BF16))) + inner[:, HD:]
         cols = slice(h * HD, (h + 1) * HD)
         att = l_ref[:, cols] + dot(m_ref[:, cols], start.astype(BF16))
         scale = lax.rsqrt(jnp.mean(att * att, axis=1, keepdims=True) + 1e-6)
@@ -267,38 +268,85 @@
         out_shape=outs,
         in_specs=specs or [VM] * len(args),
         out_specs=jax.tree.map(lambda _: VM, outs),
-        compiler_params=pltpu.CompilerParams(vmem_limit_bytes=32 * 1024 * 1024),
+        compiler_params=pltpu.CompilerParams(vmem_limit_bytes=16 * 1024 * 1024),
     )(*args)
 
 
-def term(at, a_ref, b_ref, w_ref, x_ref):
-    width = a_ref.shape[1]
-    cols = pl.ds(pl.multiple_of(at * width, width), width)
-    return dot(a_ref[...], w_ref[:, cols]) + dot(b_ref[...], x_ref[:, cols])
-
-
-def far_kernel(at_ref, a_ref, b_ref, w_ref, x_ref, up_ref, down_ref):
-    out = term(at_ref[0], a_ref, b_ref, w_ref, x_ref).astype(BF16)
-    up_ref[...] = out[: up_ref.shape[0]]
-    down_ref[...] = out[up_ref.shape[0] :]
-
-
-def terms_kernel(at_ref, a_ref, b_ref, w_ref, x_ref, o_ref):
+def pack_kernel(chips, me_ref, w_ref, x_ref, ring_ref, own_ref, sems):
+    rows, width = w_ref.shape[0], own_ref.shape[1]
+    count = ring_ref.shape[0]
+    chip, core = me_ref[0] // 2, me_ref[0] % 2
+    copies = []
+
+    def put(ref, at, cols):
+        block = pl.ds(pl.multiple_of(at * width, width), width)
+        for j, source in enumerate((w_ref, x_ref)):
+            target = ref.at[j * rows : (j + 1) * rows, cols]
+            copies.append(pltpu.make_async_copy(source.at[:, block], target, sems.at[len(copies)]))
+            copies[-1].start()
+
+    for i in range(count):
+        dest = (chip + chips + (1 - 2 * core) * (count - i)) % chips
+        put(ring_ref.at[i], 2 * dest + core, slice(0, width))
+        put(ring_ref.at[i], 2 * dest + 1 - core, slice(width, 2 * width))
+    put(own_ref, me_ref[0], slice(0, width))
+    for copy in copies:
+        copy.wait()
+
+
+def pack(chips, count, me, weight, mate_weight):
+    rows = weight.shape[0]
+    return pl.pallas_call(
+        functools.partial(pack_kernel, chips),
+        out_shape=(
+            jax.ShapeDtypeStruct((count, 2 * rows, 2 * rows), BF16),
+            jax.ShapeDtypeStruct((2 * rows, rows), BF16),
+        ),
+        in_specs=[SM] + [pl.BlockSpec(memory_space=pltpu.HBM)] * 2,
+        out_specs=(VM, VM),
+        scratch_shapes=[pltpu.SemaphoreType.DMA((4 * count + 2,))],
+        compiler_params=pltpu.CompilerParams(vmem_limit_bytes=16 * 1024 * 1024),
+    )(me, *(pltpu.with_memory_space_constraint(a, pltpu.HBM) for a in (weight, mate_weight)))
+
+
+def term(a, b, w):
+    rows = a.shape[1]
+    return dot(a, w[:rows]) + dot(b, w[rows:])
+
+
+def far_kernel(core_ref, a_ref, b_ref, w_ref, o_ref):
+    cut = o_ref.shape[0]
+    rows = pl.ds(pl.multiple_of(core_ref[0] * cut, cut), cut)
+    o_ref[...] = term(a_ref[rows, :], b_ref[rows, :], w_ref[0]).astype(BF16)
+
+
+def next_kernel(a_ref, b_ref, w_ref, o_ref):
+    o_ref[...] = term(a_ref[...], b_ref[...], w_ref[1])
+
+
+def rest_kernel(a_ref, b_ref, w_ref, own_w_ref, o_ref, own_ref):
     for i in range(o_ref.shape[0]):
-        o_ref[i] = term(at_ref[i], a_ref, b_ref, w_ref, x_ref)
-
-
-def first_add_kernel(at, rows, terms_ref, got_ref, o_ref):
-    o_ref[...] = terms_ref[at].astype(BF16)
-    o_ref[rows] = (terms_ref[at, rows] + got_ref[...].astype(F32)).astype(BF16)
-
-
-def add_kernel(at, terms_ref, got_ref, o_ref):
-    o_ref[...] = (terms_ref[at] + got_ref[...].astype(F32)).astype(o_ref.dtype)
-
-
-def last_add_kernel(a_ref, b_ref, o_ref):
-    o_ref[...] = (a_ref[...] + b_ref[...].astype(F32)).astype(BF16)
+        o_ref[i] = term(a_ref[...], b_ref[...], w_ref[2 + i])
+    own_ref[...] = term(a_ref[...], b_ref[...], own_w_ref[...])
+
+
+def first_add_kernel(core_ref, term_ref, got_ref, o_ref):
+    cut = got_ref.shape[0]
+    for i in range(2):
+        rows = slice(i * cut, (i + 1) * cut)
+        got = jnp.where(core_ref[0] == i, got_ref[...].astype(F32), 0.0)
+        o_ref[rows] = (term_ref[rows] + got).astype(BF16)
+
+
+def add_kernel(at, terms_ref, got_ref, *out_refs):
+    width = out_refs[0].shape[1]
+    for i, o_ref in enumerate(out_refs):
+        cols = slice(i * width, (i + 1) * width)
+        o_ref[...] = (terms_ref[at, :, cols] + got_ref[:, cols].astype(F32)).astype(BF16)
+
+
+def last_add_kernel(a_ref, b_ref, c_ref, o_ref):
+    o_ref[...] = (a_ref[...] + b_ref[...].astype(F32) + c_ref[...].astype(F32)).astype(BF16)
 
 
 def per_device(queries, keys, values, betas, gate, out_weight):
@@ -307,10 +355,13 @@
     devices = lax.axis_size("head")
     chips = devices // 2
     me = lax.axis_index("head")
-    chip, core = me // 2, me % 2
-
-    def shift(a, by):
-        return lax.ppermute(a, "head", [(i, (i + 2 * by) % devices) for i in range(devices)])
+    core = me % 2
+
+    def onward(a, cross):
+        hop = [
+            (2 * c + i, 2 * ((c + 1 - 2 * i) % chips) + (i ^ cross)) for c in range(chips) for i in (0, 1)
+        ]
+        return lax.ppermute(a, "head", hop)
 
     def mate(a):
         return lax.ppermute(a, "head", [(i, i ^ 1) for i in range(devices)])
@@ -320,23 +371,26 @@
         return lax.ppermute(a, "ctx_0", [(i, i + by) for i in range(groups - by)])
 
     mate_weight = mate(out_weight)
-    maps, inverse, scales, prefixes = local_maps(keys, values, beta_rows(betas), 8)
-
-    wide_map = jax.ShapeDtypeStruct((heads, HD, 2 * HD), F32)
-    wide_send = jax.ShapeDtypeStruct((heads, HD, 2 * HD), BF16)
-    state_send = jax.ShapeDtypeStruct((heads, HD, HD), BF16)
+    maps, inverse, scales, prefixes = local_maps(keys, values, betas, 8)
+
+    wide_map = jax.ShapeDtypeStruct((HD, 2 * HD), F32)
+    wide_send = jax.ShapeDtypeStruct((HD, 2 * HD), BF16)
+    state_send = jax.ShapeDtypeStruct((HD, HD), BF16)
+    inside_map = jax.ShapeDtypeStruct((heads, HD, 2 * HD), F32)
+    tokens = jax.ShapeDtypeStruct((tok, cols), F32)
+    sent = jax.ShapeDtypeStruct((tok, cols), BF16)
+
     gathered = lax.all_gather(maps, "ctx_1")
     x = lax.axis_index("ctx_1").astype(jnp.int32).reshape(1)
     send, total, inside = small(
-        fold_kernel, (wide_send, wide_map, wide_map), x, gathered, specs=[SM, VM]
+        fold_kernel, (wide_send, wide_map, inside_map), x, gathered, specs=[SM, VM]
     )
     near = later_z(send, 1)
     send, pair = small(join_kernel, (wide_send, wide_map), total, near)
     far = later_z(send, 2)
-    tokens = jax.ShapeDtypeStruct((tok, cols), F32)
     local, carry, silu = small(
         local_kernel,
-        (tokens, jax.ShapeDtypeStruct((tok, cols), BF16), tokens),
+        (tokens, sent, tokens),
         queries,
         keys,
         values,
@@ -345,51 +399,64 @@
         scales,
         lax.optimization_barrier((prefixes, near))[0],
     )
+    half = chips // 2
+    ring_w, own_w = pack(
+        chips,
+        half,
+        me.astype(jnp.int32).reshape(1),
+        out_weight,
+        lax.optimization_barrier((mate_weight, near))[0],
+    )
     send = small(carry_kernel, state_send, pair, far)
-    state = later_z(send, 4)
-    entry = small(entry_kernel, wide_map, inside, near, far)
+    last = later_z(send, 4)
+    entry = small(entry_kernel, wide_map, near, far)
+    entry = lax.optimization_barrier((entry, silu, own_w))[0]
+    own_state = small(carry_kernel, state_send, entry, last)
+    peers = lax.axis_size("ctx_1")
+    other_state = lax.ppermute(own_state, "ctx_1", [(i, i ^ 1) for i in range(peers)])
     mixed_in = small(
         mix_kernel,
-        jax.ShapeDtypeStruct((tok, cols), BF16),
-        entry,
-        state,
+        sent,
+        x,
+        inside,
+        own_state,
+        other_state,
         local,
         carry,
         silu,
+        specs=[SM] + [VM] * 6,
     )
     mate_in = mate(mixed_in)
 
-    half = chips // 2
-    sides = [s for k in range(half - 1, 0, -1) for s in (k, chips - k)] + [0]
-    at = [2 * ((chip + jnp.array(o, jnp.int32)) % chips) + core for o in ([half], sides)]
-
-    weights = (mixed_in, mate_in, out_weight, mate_weight)
-    specs = [SM] + [VM] * 4
-    cut = tok // 2
-    part = jax.ShapeDtypeStruct((cut, cols), BF16)
-    up, down = small(far_kernel, (part, part), at[0], *weights, specs=specs)
-    up, down = shift(up, 1), shift(down, -1)
-    several = jax.ShapeDtypeStruct((len(sides), tok, cols), F32)
-    terms = small(terms_kernel, several, at[1], *weights, specs=specs)
-    sent = jax.ShapeDtypeStruct((tok, cols), BF16)
-    down_sum = None
-    for k in range(half - 1):
-        adders = [functools.partial(add_kernel, 2 * k + i) for i in range(2)]
-        if k == 0:
-            adders = [
-                functools.partial(first_add_kernel, i, r)
-                for i, r in enumerate((slice(0, cut), slice(cut, tok)))
-            ]
-        else:
-            up = lax.optimization_barrier((up, down_sum))[0]
-        up_sum = small(adders[0], sent, terms, up)
-        down = lax.optimization_barrier((down, up_sum))[0]
-        down_sum = small(adders[1], sent, terms, down)
-        up, down = shift(up_sum, 1), shift(down_sum, -1)
-    last = functools.partial(add_kernel, 2 * half - 2)
-    up = lax.optimization_barrier((up, down_sum))[0]
-    total = small(last, tokens, terms, up)
-    return small(last_add_kernel, sent, total, down)
+    which = core.astype(jnp.int32).reshape(1)
+    got = small(
+        far_kernel,
+        jax.ShapeDtypeStruct((tok // 2, 2 * cols), BF16),
+        which,
+        mixed_in,
+        mate_in,
+        ring_w,
+        specs=[SM] + [VM] * 3,
+    )
+    got = onward(got, 0)
+    broad = jax.ShapeDtypeStruct((tok, 2 * cols), BF16)
+    third = small(
+        next_kernel, jax.ShapeDtypeStruct((tok, 2 * cols), F32), mixed_in, mate_in, ring_w
+    )
+    acc = small(first_add_kernel, broad, which, third, got, specs=[SM, VM, VM])
+    rest, own = small(
+        rest_kernel,
+        (jax.ShapeDtypeStruct((half - 2, tok, 2 * cols), F32), tokens),
+        lax.optimization_barrier((mixed_in, acc))[0],
+        mate_in,
+        ring_w,
+        own_w,
+    )
+    for k in range(half - 3):
+        acc = small(functools.partial(add_kernel, k), broad, rest, onward(acc, 0))
+    got = onward(acc, 0)
+    same, cross = small(functools.partial(add_kernel, half - 3), (sent, sent), rest, got)
+    return small(last_add_kernel, sent, own, onward(same, 0), onward(cross, 1))
 
 
 def solution(mesh):

time: 111 us -> 121 us (1.090)
  waiting for transfers between devices: 19.7 us -> 31.7 us
  starting transfers between devices: 55.7 us -> 53.1 us
    ppermute x8 -> x6, waiting for transfers between devices: 13.2 us -> 26.4 us  [the longest x5 22.9 us: onward(): return lax.ppermute(a, 'head', hop)]
    ppermute x8 -> x6, starting transfers between devices: 28.7 us -> 25.7 us  [the longest x5 23.4 us: onward(): return lax.ppermute(a, 'head', hop)]
    pallas_call x0 -> x1, Pallas kernels: none -> 1.92 us  [pack(): pl.pallas_call(functools.partial(pack_kernel, chips), out_shape=(jax.Shap...]
    pallas_call x16 -> x14, Pallas kernels: 9.04 us -> 7.16 us  [small(): pl.pallas_call(kernel, out_shape=outs, in_specs=specs or [VM] * len(args)...]
    ppermute x3, waiting for transfers between devices: 5.07 us -> 3.77 us  [later_z(): return lax.ppermute(a, 'ctx_0', [(i, i + by) for i in range(groups - by)])]
  transfers between devices with their start and end apart: 13 -> 11, of which waited for: 8 -> 9; matrix products, arithmetic and copies ran while one was open for 1% -> 0% of each run, Pallas kernels for 14% -> 14%
where the time goes in v3:
time: 121 us; the launch traced here: 120 us
  starting transfers between devices  53.1 us (44%)
  waiting for transfers between devices  31.7 us (26%)
  Pallas kernels  19.3 us (16%)
  blocking collectives  13.5 us (11%)
  local copies, waits for them, and re-layouts  2.35 us (2%)
    ppermute x5, starting transfers between devices, onward(): return lax.ppermute(a, 'head', hop)  23.4 us
    ppermute x3, starting transfers between devices, later_z(): return lax.ppermute(a, 'ctx_0', [(i, i + by) for i in range(groups - by)])  23.4 us
    ppermute x5, waiting for transfers between devices, onward(): return lax.ppermute(a, 'head', hop)  22.9 us
    all_gather x1, blocking collectives, per_device(): gathered = lax.all_gather(maps, 'ctx_1')  13.5 us
    pallas_call x1, Pallas kernels, local_maps(): pl.pallas_call(functools.partial(map_kernel, group), out_shape=(jax.Shape...  10.2 us
    pallas_call x14, Pallas kernels, small(): pl.pallas_call(kernel, out_shape=outs, in_specs=specs or [VM] * len(args)...  7.16 us
    ppermute x2, starting transfers between devices, mate(): return lax.ppermute(a, 'head', [(i, i ^ 1) for i in range(devices)])  3.98 us
    ppermute x3, waiting for transfers between devices, later_z(): return lax.ppermute(a, 'ctx_0', [(i, i + by) for i in range(groups - by)])  3.77 us
  transfers between devices with their start and end apart: 11, of which 9 were waited for; matrix products, arithmetic and copies ran while one was open for 0% of the time, Pallas kernels for 14%

profile of v3, /device:TPU:26, one launch (start us, length us, event | category | flops | bytes accessed | tf_op | source)
XLA Modules:
  0.0 120.1 jit_solution(5798065543652128669)
XLA Ops:
  0.0 0.0 copy-start.1
  0.0 0.0 copy-start
  0.0 0.0 copy-start.2
  0.0 2.1 %collective-permute-start.2 = (bf16[256,4096]{1,0:T(8,128)(2,1)}, bf16[256,4096]{1,0:T(8,128)(2,1)}, u32[]{:S(2)}, u32[]{:S(2)}) collective-permute-start(bf16[256,4096]{1,0:T(8,128)(2,1)} %w_ref.1), channel_id=1, source_target_pairs={{0,1},{1,0},{2,3},{3,2},{4,5},{5,4},{6,7},{7,6},{8,9},{9,8},{10,11... | collective-permute-start | bytes 6291464 | tf_op jit(solution)/shard_map/ppermute | solution.py:367
  2.1 0.0 copy-start.6
  2.1 0.7 copy-done.6
  2.8 10.2 %shard_map.64 = (bf16[2,128,256]{2,1,0:T(8,128)(2,1)S(1)}, bf16[16,128,256]{2,1,0:T(8,128)(2,1)S(1)}, f32[16,2,128]{2,1,0:T(2,128)S(1)}, bf16[16,128,256]{2,1,0:T(8,128)(2,1)S(1)}) custom-call(bf16[2,512,256]{2,1,0:T(8,128)(2,1)} %k_ref.1, bf16[2,512,256]{2,1,0:T(8,128)(2,1)} %v_ref.1, f32[2,2,512]{2,1,0:T(2,128)S(1)} %copy-done.6), custom_call_target="tpu_custom_call" | custom-call | tf_op jit(solution)/shard_map/pallas_call | solution.py:136
  13.0 13.5 %all-gather = bf16[8,128,256]{2,1,0:T(8,128)(2,1)S(1)} all-gather(bf16[2,128,256]{2,1,0:T(8,128)(2,1)S(1)} %get-tuple-element.27), channel_id=2, replica_groups=mesh['ctx_0'=8,'ctx_1'=4,'head'=16] {'ctx_1'}, dimensions={0}, use_global_device_ids=true | all-gather | bytes 655360 | tf_op jit(solution)/shard_map/all_gather | solution.py:383
  26.5 0.6 shard_map.65
  27.1 0.0 copy-start.4
  27.1 0.7 copy-done.4
  27.8 4.3 %collective-permute-start = (bf16[128,256]{1,0:T(8,128)(2,1)S(1)}, bf16[128,256]{1,0:T(8,128)(2,1)S(1)}, u32[]{:S(2)}, u32[]{:S(2)}) collective-permute-start(bf16[128,256]{1,0:T(8,128)(2,1)S(1)} %get-tuple-element.29), channel_id=1, source_target_pairs={{0,64},{64,128},{128,192},{192,256},{256,320},{320,384},{384,448},... | collective-permute-start | bytes 196616 | tf_op jit(solution)/shard_map/ppermute | solution.py:371
  32.1 1.9 %collective-permute-done.earlier_ref.near_ref = bf16[128,256]{1,0:T(8,128)(2,1)S(1)} collective-permute-done((bf16[128,256]{1,0:T(8,128)(2,1)S(1)}, bf16[128,256]{1,0:T(8,128)(2,1)S(1)}, u32[]{:S(2)}, u32[]{:S(2)}) %collective-permute-start) | collective-permute-done | bytes 65568 | tf_op jit(solution)/shard_map/ppermute | solution.py:371
  34.0 0.2 shard_map.66
  34.1 6.1 %collective-permute-start.1 = (bf16[128,256]{1,0:T(8,128)(2,1)S(1)}, bf16[128,256]{1,0:T(8,128)(2,1)S(1)}, u32[]{:S(2)}, u32[]{:S(2)}) collective-permute-start(bf16[128,256]{1,0:T(8,128)(2,1)S(1)} %get-tuple-element.31), channel_id=1, source_target_pairs={{0,128},{64,192},{128,256},{192,320},{256,384},{320,448},{1,129},{... | collective-permute-start | bytes 196616 | tf_op jit(solution)/shard_map/ppermute | solution.py:371
  40.2 1.9 %collective-permute-done.1.far_ref.earlier_ref = bf16[128,256]{1,0:T(8,128)(2,1)S(1)} collective-permute-done((bf16[128,256]{1,0:T(8,128)(2,1)S(1)}, bf16[128,256]{1,0:T(8,128)(2,1)S(1)}, u32[]{:S(2)}, u32[]{:S(2)}) %collective-permute-start.1) | collective-permute-done | bytes 65568 | tf_op jit(solution)/shard_map/ppermute | solution.py:371
  42.1 0.8 shard_map.70
  42.9 13.0 %collective-permute-start.3 = (bf16[128,128]{1,0:T(8,128)(2,1)}, bf16[128,128]{1,0:T(8,128)(2,1)}, u32[]{:S(2)}, u32[]{:S(2)}) collective-permute-start(bf16[128,128]{1,0:T(8,128)(2,1)} %shard_map.70), channel_id=1, source_target_pairs={{0,256},{64,320},{128,384},{192,448},{1,257},{65,321},{129,385},{1... | collective-permute-start | bytes 98312 | tf_op jit(solution)/shard_map/ppermute | solution.py:371
  55.9 0.0 copy-done.1
  55.9 0.0 copy-done
  55.9 0.0 copy-done.2
  55.9 0.0 copy-start.3
  55.9 0.9 copy-done.3
  56.8 1.4 %shard_map.68 = (f32[512,256]{1,0:T(8,128)S(1)}, bf16[512,256]{1,0:T(8,128)(2,1)S(1)}, f32[512,256]{1,0:T(8,128)S(1)}) custom-call(bf16[512,256]{1,0:T(8,128)(2,1)S(1)} %copy-done.2, bf16[2,512,256]{2,1,0:T(8,128)(2,1)S(1)} %copy-done, bf16[2,512,256]{2,1,0:T(8,128)(2,1)S(1)} %copy-done.1, bf16[512,256]{1,0:T(8,128)(2,1)S(1)} %copy-done.3, ...), custom_call_target="tpu_custom_call" | custom-call | tf_op jit(solution)/shard_map/pallas_call | solution.py:266
  58.2 0.1 shard_map.67.later_ref
  58.3 0.0 collective-permute-done.2.x_ref
  58.4 0.0 copy-start.5
  58.4 1.9 %shard_map.69 = (bf16[4,512,512]{2,1,0:T(8,128)(2,1)S(1)}, bf16[512,256]{1,0:T(8,128)(2,1)S(1)}) custom-call(s32[1]{0:T(128)} %bitcast.2.me_ref, bf16[256,4096]{1,0:T(8,128)(2,1)} %w_ref.1, bf16[256,4096]{1,0:T(8,128)(2,1)} %collective-permute-done.2.x_ref), custom_call_target="tpu_custom_call" | custom-call | tf_op jit(solution)/shard_map/pallas_call | solution.py:299
  60.3 0.0 collective-permute-done.3.earlier_ref
  60.3 0.9 shard_map.71.own_ref
  61.2 2.3 %collective-permute-start.4 = (bf16[128,128]{1,0:T(8,128)(2,1)S(1)}, bf16[128,128]{1,0:T(8,128)(2,1)S(1)}, u32[]{:S(2)}, u32[]{:S(2)}) collective-permute-start(bf16[128,128]{1,0:T(8,128)(2,1)S(1)} %shard_map.71.own_ref), channel_id=1, source_target_pairs={{0,16},{16,0},{32,48},{48,32},{1,17},{17,1},{33,49},{49,33},{2,18}... | collective-permute-start | bytes 98312 | tf_op jit(solution)/shard_map/ppermute | solution.py:416
  63.5 3.5 %collective-permute-done.4.other_ref = bf16[128,128]{1,0:T(8,128)(2,1)S(1)} collective-permute-done((bf16[128,128]{1,0:T(8,128)(2,1)S(1)}, bf16[128,128]{1,0:T(8,128)(2,1)S(1)}, u32[]{:S(2)}, u32[]{:S(2)}) %collective-permute-start.4) | collective-permute-done | bytes 32800 | tf_op jit(solution)/shard_map/ppermute | solution.py:416
  67.0 0.0 copy-done.5
  67.0 0.5 shard_map.72.a_ref
  67.6 1.9 %collective-permute-start.5 = (bf16[512,256]{1,0:T(8,128)(2,1)S(1)}, bf16[512,256]{1,0:T(8,128)(2,1)S(1)}, u32[]{:S(2)}, u32[]{:S(2)}) collective-permute-start(bf16[512,256]{1,0:T(8,128)(2,1)S(1)} %shard_map.72.a_ref), channel_id=1, source_target_pairs={{0,1},{1,0},{2,3},{3,2},{4,5},{5,4},{6,7},{7,6},{8,9},{9,8},{10,11... | collective-permute-start | bytes 786440 | tf_op jit(solution)/shard_map/ppermute | solution.py:367
  69.5 1.5 %collective-permute-done.5.b_ref = bf16[512,256]{1,0:T(8,128)(2,1)S(1)} collective-permute-done((bf16[512,256]{1,0:T(8,128)(2,1)S(1)}, bf16[512,256]{1,0:T(8,128)(2,1)S(1)}, u32[]{:S(2)}, u32[]{:S(2)}) %collective-permute-start.5) | collective-permute-done | bytes 262176 | tf_op jit(solution)/shard_map/ppermute | solution.py:367
  71.0 0.3 shard_map.74
  71.3 4.7 %collective-permute-start.6 = (bf16[256,512]{1,0:T(8,128)(2,1)S(1)}, bf16[256,512]{1,0:T(8,128)(2,1)S(1)}, u32[]{:S(2)}, u32[]{:S(2)}) collective-permute-start(bf16[256,512]{1,0:T(8,128)(2,1)S(1)} %shard_map.74), channel_id=1, source_target_pairs={{0,2},{1,15},{2,4},{3,1},{4,6},{5,3},{6,8},{7,5},{8,10},{9,7},{10,... | collective-permute-start | bytes 786440 | tf_op jit(solution)/shard_map/ppermute | solution.py:364
  76.0 0.4 shard_map.73.term_ref
  76.5 3.4 %collective-permute-done.6.got_ref = bf16[256,512]{1,0:T(8,128)(2,1)S(1)} collective-permute-done((bf16[256,512]{1,0:T(8,128)(2,1)S(1)}, bf16[256,512]{1,0:T(8,128)(2,1)S(1)}, u32[]{:S(2)}, u32[]{:S(2)}) %collective-permute-start.6) | collective-permute-done | bytes 262176 | tf_op jit(solution)/shard_map/ppermute | solution.py:364
  79.9 0.1 shard_map.75
  80.0 5.6 %collective-permute-start.7 = (bf16[512,512]{1,0:T(8,128)(2,1)S(1)}, bf16[512,512]{1,0:T(8,128)(2,1)S(1)}, u32[]{:S(2)}, u32[]{:S(2)}) collective-permute-start(bf16[512,512]{1,0:T(8,128)(2,1)S(1)} %shard_map.75), channel_id=1, source_target_pairs={{0,2},{1,15},{2,4},{3,1},{4,6},{5,3},{6,8},{7,5},{8,10},{9,7},{10,... | collective-permute-start | bytes 1572872 | tf_op jit(solution)/shard_map/ppermute | solution.py:364
  85.6 0.8 shard_map.76
  86.5 5.8 %collective-permute-done.7.got_ref = bf16[512,512]{1,0:T(8,128)(2,1)S(1)} collective-permute-done((bf16[512,512]{1,0:T(8,128)(2,1)S(1)}, bf16[512,512]{1,0:T(8,128)(2,1)S(1)}, u32[]{:S(2)}, u32[]{:S(2)}) %collective-permute-start.7) | collective-permute-done | bytes 524320 | tf_op jit(solution)/shard_map/ppermute | solution.py:364
  92.3 0.1 shard_map.77
  92.4 5.6 %collective-permute-start.8 = (bf16[512,512]{1,0:T(8,128)(2,1)S(1)}, bf16[512,512]{1,0:T(8,128)(2,1)S(1)}, u32[]{:S(2)}, u32[]{:S(2)}) collective-permute-start(bf16[512,512]{1,0:T(8,128)(2,1)S(1)} %shard_map.77), channel_id=1, source_target_pairs={{0,2},{1,15},{2,4},{3,1},{4,6},{5,3},{6,8},{7,5},{8,10},{9,7},{10,... | collective-permute-start | bytes 1572872 | tf_op jit(solution)/shard_map/ppermute | solution.py:364
  98.0 6.7 %collective-permute-done.8.got_ref = bf16[512,512]{1,0:T(8,128)(2,1)S(1)} collective-permute-done((bf16[512,512]{1,0:T(8,128)(2,1)S(1)}, bf16[512,512]{1,0:T(8,128)(2,1)S(1)}, u32[]{:S(2)}, u32[]{:S(2)}) %collective-permute-start.8) | collective-permute-done | bytes 524320 | tf_op jit(solution)/shard_map/ppermute | solution.py:364
  104.7 0.1 shard_map.78
  104.8 5.6 %collective-permute-start.9 = (bf16[512,256]{1,0:T(8,128)(2,1)S(1)}, bf16[512,256]{1,0:T(8,128)(2,1)S(1)}, u32[]{:S(2)}, u32[]{:S(2)}) collective-permute-start(bf16[512,256]{1,0:T(8,128)(2,1)S(1)} %get-tuple-element.47), channel_id=1, source_target_pairs={{0,2},{1,15},{2,4},{3,1},{4,6},{5,3},{6,8},{7,5},{8,10},{9,7},{10,... | collective-permute-start | bytes 786440 | tf_op jit(solution)/shard_map/ppermute | solution.py:364
  110.4 1.9 %collective-permute-start.10 = (bf16[512,256]{1,0:T(8,128)(2,1)S(1)}, bf16[512,256]{1,0:T(8,128)(2,1)S(1)}, u32[]{:S(2)}, u32[]{:S(2)}) collective-permute-start(bf16[512,256]{1,0:T(8,128)(2,1)S(1)} %get-tuple-element.48), channel_id=1, source_target_pairs={{0,3},{1,14},{2,5},{3,0},{4,7},{5,2},{6,9},{7,4},{8,11},{9,6},{10,... | collective-permute-start | bytes 786440 | tf_op jit(solution)/shard_map/ppermute | solution.py:364
  112.3 1.9 %collective-permute-done.9.b_ref = bf16[512,256]{1,0:T(8,128)(2,1)S(1)} collective-permute-done((bf16[512,256]{1,0:T(8,128)(2,1)S(1)}, bf16[512,256]{1,0:T(8,128)(2,1)S(1)}, u32[]{:S(2)}, u32[]{:S(2)}) %collective-permute-start.9) | collective-permute-done | bytes 262176 | tf_op jit(solution)/shard_map/ppermute | solution.py:364
  114.3 5.0 %collective-permute-done.10.c_ref = bf16[512,256]{1,0:T(8,128)(2,1)S(1)} collective-permute-done((bf16[512,256]{1,0:T(8,128)(2,1)S(1)}, bf16[512,256]{1,0:T(8,128)(2,1)S(1)}, u32[]{:S(2)}, u32[]{:S(2)}) %collective-permute-start.10) | collective-permute-done | bytes 262176 | tf_op jit(solution)/shard_map/ppermute | solution.py:364
  119.3 0.8 shard_map.79
Async XLA Ops:
  0.0 55.9 %copy-start.1 = (bf16[2,512,256]{2,1,0:T(8,128)(2,1)S(1)}, bf16[2,512,256]{2,1,0:T(8,128)(2,1)}, u32[]{:S(2)}) copy-start(bf16[2,512,256]{2,1,0:T(8,128)(2,1)} %v_ref.1) | copy-start | bytes 1572868
  0.0 55.9 %copy-start = (bf16[2,512,256]{2,1,0:T(8,128)(2,1)S(1)}, bf16[2,512,256]{2,1,0:T(8,128)(2,1)}, u32[]{:S(2)}) copy-start(bf16[2,512,256]{2,1,0:T(8,128)(2,1)} %k_ref.1) | copy-start | bytes 1572868
  0.0 55.9 %copy-start.2 = (bf16[512,256]{1,0:T(8,128)(2,1)S(1)}, bf16[512,256]{1,0:T(8,128)(2,1)}, u32[]{:S(2)}) copy-start(bf16[512,256]{1,0:T(8,128)(2,1)} %q_ref.1) | copy-start | bytes 786436
  0.0 58.3 %collective-permute-start.2 = (bf16[256,4096]{1,0:T(8,128)(2,1)}, bf16[256,4096]{1,0:T(8,128)(2,1)}, u32[]{:S(2)}, u32[]{:S(2)}) collective-permute-start(bf16[256,4096]{1,0:T(8,128)(2,1)} %w_ref.1), channel_id=1, source_target_pairs={{0,1},{1,0},{2,3},{3,2},{4,5},{5,4},{6,7},{7,6},{8,9},{9,8},{10,11... | collective-permute-start | bytes 6291464 | tf_op jit(solution)/shard_map/ppermute | solution.py:367
  2.1 0.7 copy-start.6
  27.1 0.7 copy-start.4
  27.8 6.2 %collective-permute-start = (bf16[128,256]{1,0:T(8,128)(2,1)S(1)}, bf16[128,256]{1,0:T(8,128)(2,1)S(1)}, u32[]{:S(2)}, u32[]{:S(2)}) collective-permute-start(bf16[128,256]{1,0:T(8,128)(2,1)S(1)} %get-tuple-element.29), channel_id=1, source_target_pairs={{0,64},{64,128},{128,192},{192,256},{256,320},{320,384},{384,448},... | collective-permute-start | bytes 196616 | tf_op jit(solution)/shard_map/ppermute | solution.py:371
  34.1 8.0 %collective-permute-start.1 = (bf16[128,256]{1,0:T(8,128)(2,1)S(1)}, bf16[128,256]{1,0:T(8,128)(2,1)S(1)}, u32[]{:S(2)}, u32[]{:S(2)}) collective-permute-start(bf16[128,256]{1,0:T(8,128)(2,1)S(1)} %get-tuple-element.31), channel_id=1, source_target_pairs={{0,128},{64,192},{128,256},{192,320},{256,384},{320,448},{1,129},{... | collective-permute-start | bytes 196616 | tf_op jit(solution)/shard_map/ppermute | solution.py:371
  42.9 17.4 %collective-permute-start.3 = (bf16[128,128]{1,0:T(8,128)(2,1)}, bf16[128,128]{1,0:T(8,128)(2,1)}, u32[]{:S(2)}, u32[]{:S(2)}) collective-permute-start(bf16[128,128]{1,0:T(8,128)(2,1)} %shard_map.70), channel_id=1, source_target_pairs={{0,256},{64,320},{128,384},{192,448},{1,257},{65,321},{129,385},{1... | collective-permute-start | bytes 98312 | tf_op jit(solution)/shard_map/ppermute | solution.py:371
  55.9 1.0 copy-start.3
  58.4 8.7 %copy-start.5 = (f32[2,128,256]{2,1,0:T(8,128)S(1)}, f32[2,128,256]{2,1,0:T(8,128)}, u32[]{:S(2)}) copy-start(f32[2,128,256]{2,1,0:T(8,128)} %copy-done.4) | copy-start | bytes 786436
  61.2 5.8 %collective-permute-start.4 = (bf16[128,128]{1,0:T(8,128)(2,1)S(1)}, bf16[128,128]{1,0:T(8,128)(2,1)S(1)}, u32[]{:S(2)}, u32[]{:S(2)}) collective-permute-start(bf16[128,128]{1,0:T(8,128)(2,1)S(1)} %shard_map.71.own_ref), channel_id=1, source_target_pairs={{0,16},{16,0},{32,48},{48,32},{1,17},{17,1},{33,49},{49,33},{2,18}... | collective-permute-start | bytes 98312 | tf_op jit(solution)/shard_map/ppermute | solution.py:416
  67.6 3.4 %collective-permute-start.5 = (bf16[512,256]{1,0:T(8,128)(2,1)S(1)}, bf16[512,256]{1,0:T(8,128)(2,1)S(1)}, u32[]{:S(2)}, u32[]{:S(2)}) collective-permute-start(bf16[512,256]{1,0:T(8,128)(2,1)S(1)} %shard_map.72.a_ref), channel_id=1, source_target_pairs={{0,1},{1,0},{2,3},{3,2},{4,5},{5,4},{6,7},{7,6},{8,9},{9,8},{10,11... | collective-permute-start | bytes 786440 | tf_op jit(solution)/shard_map/ppermute | solution.py:367
  71.3 8.6 %collective-permute-start.6 = (bf16[256,512]{1,0:T(8,128)(2,1)S(1)}, bf16[256,512]{1,0:T(8,128)(2,1)S(1)}, u32[]{:S(2)}, u32[]{:S(2)}) collective-permute-start(bf16[256,512]{1,0:T(8,128)(2,1)S(1)} %shard_map.74), channel_id=1, source_target_pairs={{0,2},{1,15},{2,4},{3,1},{4,6},{5,3},{6,8},{7,5},{8,10},{9,7},{10,... | collective-permute-start | bytes 786440 | tf_op jit(solution)/shard_map/ppermute | solution.py:364
  80.0 12.3 %collective-permute-start.7 = (bf16[512,512]{1,0:T(8,128)(2,1)S(1)}, bf16[512,512]{1,0:T(8,128)(2,1)S(1)}, u32[]{:S(2)}, u32[]{:S(2)}) collective-permute-start(bf16[512,512]{1,0:T(8,128)(2,1)S(1)} %shard_map.75), channel_id=1, source_target_pairs={{0,2},{1,15},{2,4},{3,1},{4,6},{5,3},{6,8},{7,5},{8,10},{9,7},{10,... | collective-permute-start | bytes 1572872 | tf_op jit(solution)/shard_map/ppermute | solution.py:364
  92.4 12.3 %collective-permute-start.8 = (bf16[512,512]{1,0:T(8,128)(2,1)S(1)}, bf16[512,512]{1,0:T(8,128)(2,1)S(1)}, u32[]{:S(2)}, u32[]{:S(2)}) collective-permute-start(bf16[512,512]{1,0:T(8,128)(2,1)S(1)} %shard_map.77), channel_id=1, source_target_pairs={{0,2},{1,15},{2,4},{3,1},{4,6},{5,3},{6,8},{7,5},{8,10},{9,7},{10,... | collective-permute-start | bytes 1572872 | tf_op jit(solution)/shard_map/ppermute | solution.py:364
  104.8 9.5 %collective-permute-start.9 = (bf16[512,256]{1,0:T(8,128)(2,1)S(1)}, bf16[512,256]{1,0:T(8,128)(2,1)S(1)}, u32[]{:S(2)}, u32[]{:S(2)}) collective-permute-start(bf16[512,256]{1,0:T(8,128)(2,1)S(1)} %get-tuple-element.47), channel_id=1, source_target_pairs={{0,2},{1,15},{2,4},{3,1},{4,6},{5,3},{6,8},{7,5},{8,10},{9,7},{10,... | collective-permute-start | bytes 786440 | tf_op jit(solution)/shard_map/ppermute | solution.py:364
  110.4 8.9 %collective-permute-start.10 = (bf16[512,256]{1,0:T(8,128)(2,1)S(1)}, bf16[512,256]{1,0:T(8,128)(2,1)S(1)}, u32[]{:S(2)}, u32[]{:S(2)}) collective-permute-start(bf16[512,256]{1,0:T(8,128)(2,1)S(1)} %get-tuple-element.48), channel_id=1, source_target_pairs={{0,3},{1,14},{2,5},{3,0},{4,7},{5,2},{6,9},{7,4},{8,11},{9,6},{10,... | collective-permute-start | bytes 786440 | tf_op jit(solution)/shard_map/ppermute | solution.py:364

commit v4 on v1

--- a/solution.py
+++ b/solution.py
@@ -55,11 +55,13 @@
 
 
 def map_kernel(
-    group, k_hbm, v_hbm, b_ref, ab_ref, x_ref, e_ref, pre_ref, k_ref, v_ref, lev_ref, p_ref, sems
+    group, k_hbm, v_hbm, b_hbm, ab_ref, x_ref, e_ref, pre_ref, k_ref, v_ref, b_ref, lev_ref, p_ref, sems
 ):
     get_k = pltpu.make_async_copy(k_hbm, k_ref, sems.at[0])
     get_v = pltpu.make_async_copy(v_hbm, v_ref, sems.at[1])
+    get_b = pltpu.make_async_copy(b_hbm, b_ref, sems.at[2])
     get_k.start()
+    get_b.start()
     get_v.start()
     heads = k_ref.shape[2] // HD
     blocks = k_ref.shape[1] // SPAN
@@ -75,10 +77,11 @@
     eye = (place_r == place_c).astype(F32)
     for h in range(heads):
         p_ref[h] = jnp.concatenate([eye, jnp.zeros((HD, HD), F32)], axis=1)
+    get_b.wait()
     get_k.wait()
     get_v.wait()
 
-    def body(step, carry):
+    for step in range(blocks // group):
         probs = [(step * group + i, h) for i in range(group) for h in range(heads)]
         kb = [read_block(k_ref, blk, h) for blk, h in probs]
         num = range(len(probs))
@@ -87,7 +90,16 @@
             blk, h = probs[i]
             gram = dot_nt(kb[i], kb[i])
             n2 = jnp.sum(gram * eye, axis=0, keepdims=True) + 1e-6
-            e.append(b_ref[pl.ds(h * blocks + blk, 1), :] / n2)
+            first = blk * SPAN
+            beta = jnp.concatenate(
+                [
+                    b_ref[h, j : j + 1, first + 16 * g : first + 16 * (g + 1)]
+                    for g in range(SPAN // 16)
+                    for j in range(2)
+                ],
+                axis=1,
+            )
+            e.append(beta / n2)
             n.append(jnp.sqrt(n2))
             e_ref[h * blocks + blk] = jnp.concatenate([e[i], n[i]], axis=0)
             N.append(jnp.where(lev_ref[...] >= 0, gram * e[i], 0.0))
@@ -116,14 +128,11 @@
             pre_ref[h * blocks + blk] = ph
             new = dot(A[i], square(ph)) + dot(A[i][:, :HD], plo)
             p_ref[h] = new + jnp.concatenate([jnp.zeros((HD, HD), F32), B[i]], axis=1)
-        return carry
-
-    lax.fori_loop(0, blocks // group, body, 0)
     for h in range(heads):
         ab_ref[h] = p_ref[h].astype(BF16)
 
 
-def local_maps(k, v, b_rows, group):
+def local_maps(k, v, betas, group):
     _, tok, cols = k.shape
     heads = cols // HD
     count = heads * tok // SPAN
@@ -135,17 +144,18 @@
             jax.ShapeDtypeStruct((count, 2, 2 * SPAN), F32),
             jax.ShapeDtypeStruct((count, HD, 2 * HD), BF16),
         ),
-        in_specs=[pl.BlockSpec(memory_space=pltpu.HBM)] * 2 + [pl.BlockSpec(memory_space=pltpu.VMEM)],
+        in_specs=[pl.BlockSpec(memory_space=pltpu.HBM)] * 3,
         out_specs=[pl.BlockSpec(memory_space=pltpu.VMEM)] * 4,
         scratch_shapes=[
             pltpu.VMEM(k.shape, k.dtype),
             pltpu.VMEM(v.shape, v.dtype),
+            pltpu.VMEM(betas.shape, betas.dtype),
             pltpu.VMEM((2 * SPAN, 2 * SPAN), jnp.int32),
             pltpu.VMEM((heads, HD, 2 * HD), F32),
-            pltpu.SemaphoreType.DMA((2,)),
+            pltpu.SemaphoreType.DMA((3,)),
         ],
-        compiler_params=pltpu.CompilerParams(vmem_limit_bytes=32 * 1024 * 1024),
-    )(k, v, b_rows)
+        compiler_params=pltpu.CompilerParams(vmem_limit_bytes=16 * 1024 * 1024),
+    )(*(pltpu.with_memory_space_constraint(a, pltpu.HBM) for a in (k, v, betas)))
 
 
 def local_kernel(q_ref, k_ref, v_ref, g_ref, x_ref, e_ref, pre_ref, l_ref, m_ref, s_ref):
@@ -185,16 +195,6 @@
         s_ref[rows, cols] = gate / (1.0 + jnp.exp(-gate))
 
 
-def beta_rows(betas):
-    heads, _, tok = betas.shape
-    blocks = tok // SPAN
-    return (
-        betas.reshape(heads, 2, blocks, SPAN // 16, 16)
-        .transpose(0, 2, 3, 1, 4)
-        .reshape(heads * blocks, 2 * SPAN)
-    )
-
-
 def affine(a, b):
     return jnp.concatenate([a, b], axis=1)
 
@@ -267,38 +267,74 @@
         out_shape=outs,
         in_specs=specs or [VM] * len(args),
         out_specs=jax.tree.map(lambda _: VM, outs),
-        compiler_params=pltpu.CompilerParams(vmem_limit_bytes=32 * 1024 * 1024),
+        compiler_params=pltpu.CompilerParams(vmem_limit_bytes=16 * 1024 * 1024),
     )(*args)
 
 
-def term(at, a_ref, b_ref, w_ref, x_ref):
-    width = a_ref.shape[1]
-    cols = pl.ds(pl.multiple_of(at * width, width), width)
-    return dot(a_ref[...], w_ref[:, cols]) + dot(b_ref[...], x_ref[:, cols])
-
-
-def far_kernel(at_ref, a_ref, b_ref, w_ref, x_ref, up_ref, down_ref):
-    out = term(at_ref[0], a_ref, b_ref, w_ref, x_ref).astype(BF16)
-    up_ref[...] = out[: up_ref.shape[0]]
-    down_ref[...] = out[up_ref.shape[0] :]
-
-
-def terms_kernel(at_ref, a_ref, b_ref, w_ref, x_ref, o_ref):
-    for i in range(o_ref.shape[0]):
-        o_ref[i] = term(at_ref[i], a_ref, b_ref, w_ref, x_ref)
-
-
-def first_add_kernel(at, rows, terms_ref, got_ref, o_ref):
-    o_ref[...] = terms_ref[at].astype(BF16)
-    o_ref[rows] = (terms_ref[at, rows] + got_ref[...].astype(F32)).astype(BF16)
-
-
-def add_kernel(at, terms_ref, got_ref, o_ref):
-    o_ref[...] = (terms_ref[at] + got_ref[...].astype(F32)).astype(o_ref.dtype)
-
-
-def last_add_kernel(a_ref, b_ref, o_ref):
-    o_ref[...] = (a_ref[...] + b_ref[...].astype(F32)).astype(BF16)
+def pack_kernel(chips, me_ref, w_ref, x_ref, ring_ref, sems):
+    rows, width = w_ref.shape[0], ring_ref.shape[2]
+    chip, core = me_ref[0] // 2, me_ref[0] % 2
+    sign = 1 - 2 * (chip % 2)
+    half = chips // 2
+    hops = [half] + list(range(half - 1, 0, -1)) + list(range(1 - half, 0)) + [0]
+    copies = []
+    for i, hop in enumerate(hops):
+        dest = (chip + chips + sign * hop) % chips
+        block = pl.ds(pl.multiple_of((2 * dest + core) * width, width), width)
+        for j, source in enumerate((w_ref, x_ref)):
+            target = ring_ref.at[i, j * rows : (j + 1) * rows]
+            copies.append(pltpu.make_async_copy(source.at[:, block], target, sems.at[2 * i + j]))
+            copies[-1].start()
+    for copy in copies:
+        copy.wait()
+
+
+def pack(chips, me, weight, mate_weight):
+    rows = weight.shape[0]
+    return pl.pallas_call(
+        functools.partial(pack_kernel, chips),
+        out_shape=jax.ShapeDtypeStruct((chips, 2 * rows, rows), BF16),
+        in_specs=[SM] + [pl.BlockSpec(memory_space=pltpu.HBM)] * 2,
+        out_specs=VM,
+        scratch_shapes=[pltpu.SemaphoreType.DMA((2 * chips,))],
+        compiler_params=pltpu.CompilerParams(vmem_limit_bytes=16 * 1024 * 1024),
+    )(me, *(pltpu.with_memory_space_constraint(a, pltpu.HBM) for a in (weight, mate_weight)))
+
+
+def term(a, b, w):
+    rows = a.shape[1]
+    return dot(a, w[:rows]) + dot(b, w[rows:])
+
+
+def hop_kernel(jobs, got_count, me_ref, a_ref, b_ref, w_ref, *refs):
+    odd = (me_ref[0] // 2) % 2
+    got_refs, out_refs = refs[:got_count], refs[got_count:]
+    cut = out_refs[0].shape[0]
+    for i, (at, side) in enumerate(jobs):
+        rows = pl.ds(pl.multiple_of(((odd + side) % 2) * cut, cut), cut)
+        out = term(a_ref[rows, :], b_ref[rows, :], w_ref[at])
+        if got_refs:
+            out = out + got_refs[i][...].astype(F32)
+        out_refs[i][...] = out.astype(BF16)
+
+
+def own_kernel(me_ref, a_ref, b_ref, w_ref, even_ref, odd_ref, o_ref):
+    odd = (me_ref[0] // 2) % 2
+    cut = even_ref.shape[0]
+    out = term(a_ref[...], b_ref[...], w_ref[w_ref.shape[0] - 1])
+    for i in range(2):
+        rows = slice(i * cut, (i + 1) * cut)
+        got = jnp.where(odd == i, even_ref[...].astype(F32), odd_ref[...].astype(F32))
+        o_ref[rows] = out[rows] + got
+
+
+def last_kernel(me_ref, sum_ref, even_ref, odd_ref, o_ref):
+    odd = (me_ref[0] // 2) % 2
+    cut = even_ref.shape[0]
+    for i in range(2):
+        rows = slice(i * cut, (i + 1) * cut)
+        got = jnp.where(odd == i, even_ref[...].astype(F32), odd_ref[...].astype(F32))
+        o_ref[rows] = (sum_ref[rows] + got).astype(BF16)
 
 
 def per_device(queries, keys, values, betas, gate, out_weight):
@@ -307,10 +343,12 @@
     devices = lax.axis_size("head")
     chips = devices // 2
     me = lax.axis_index("head")
-    chip, core = me // 2, me % 2
-
-    def shift(a, by):
-        return lax.ppermute(a, "head", [(i, (i + 2 * by) % devices) for i in range(devices)])
+    core = me % 2
+
+    def across(a, odd):
+        pairs = [(c, (c + 1) % chips) for c in range(odd, chips, 2)]
+        both = pairs + [(d, c) for c, d in pairs]
+        return lax.ppermute(a, "head", [(2 * c + i, 2 * d + i) for c, d in both for i in range(2)])
 
     def mate(a):
         return lax.ppermute(a, "head", [(i, i ^ 1) for i in range(devices)])
@@ -320,7 +358,7 @@
         return lax.ppermute(a, "ctx_0", [(i, i + by) for i in range(groups - by)])
 
     mate_weight = mate(out_weight)
-    maps, inverse, scales, prefixes = local_maps(keys, values, beta_rows(betas), 8)
+    maps, inverse, scales, prefixes = local_maps(keys, values, betas, 8)
 
     wide_map = jax.ShapeDtypeStruct((heads, HD, 2 * HD), F32)
     wide_send = jax.ShapeDtypeStruct((heads, HD, 2 * HD), BF16)
@@ -348,6 +386,9 @@
     send = small(carry_kernel, state_send, pair, far)
     state = later_z(send, 4)
     entry = small(entry_kernel, wide_map, inside, near, far)
+    place = me.astype(jnp.int32).reshape(1)
+    ring_w = pack(chips, place, out_weight, lax.optimization_barrier((mate_weight, near))[0])
+    entry = lax.optimization_barrier((entry, ring_w, silu))[0]
     mixed_in = small(
         mix_kernel,
         jax.ShapeDtypeStruct((tok, cols), BF16),
@@ -360,36 +401,44 @@
     mate_in = mate(mixed_in)
 
     half = chips // 2
-    sides = [s for k in range(half - 1, 0, -1) for s in (k, chips - k)] + [0]
-    at = [2 * ((chip + jnp.array(o, jnp.int32)) % chips) + core for o in ([half], sides)]
-
-    weights = (mixed_in, mate_in, out_weight, mate_weight)
-    specs = [SM] + [VM] * 4
-    cut = tok // 2
-    part = jax.ShapeDtypeStruct((cut, cols), BF16)
-    up, down = small(far_kernel, (part, part), at[0], *weights, specs=specs)
-    up, down = shift(up, 1), shift(down, -1)
-    several = jax.ShapeDtypeStruct((len(sides), tok, cols), F32)
-    terms = small(terms_kernel, several, at[1], *weights, specs=specs)
+    chunk = jax.ShapeDtypeStruct((tok // 2, cols), BF16)
+    both = (mixed_in, mate_in, ring_w)
+
+    def hop(jobs, prior, *got):
+        got = [lax.optimization_barrier((g, prior))[0] for g in got]
+        ins = both if prior is None or got else (lax.optimization_barrier((mixed_in, prior))[0], *both[1:])
+        body = functools.partial(hop_kernel, jobs, len(got))
+        return small(body, (chunk,) * len(jobs), place, *ins, *got, specs=[SM] + [VM] * (3 + len(got)))
+
+    slots = [(half, 0)] + [s for k in range(half - 1, 0, -1) for s in ((k, 1), (k, 0))]
+    prior, moved = None, []
+    for n, (k, late) in enumerate(slots):
+        at = [half - k, 0 if k == half else 2 * half - 1 - k]
+        side = [late, 1 - late]
+        if n < 2:
+            ahead, back = hop([(at[0], side[0]), (at[1], side[1])], prior)
+            prior = back
+        else:
+            from_even, from_odd = moved[n - 2]
+            order = (1, 0) if n % 4 in (2, 3) else (0, 1)
+            sums = {}
+            for i in order:
+                (sums[i],) = hop([(at[i], side[i])], prior, from_odd if i == 0 else from_even)
+                prior = sums[i]
+            ahead, back = sums[0], sums[1]
+        moved.append((across(ahead, 0), across(back, 1)))
+    (even_t, odd_t), (even_f, odd_f) = moved[-2:]
+    total = small(
+        own_kernel,
+        jax.ShapeDtypeStruct((tok, cols), F32),
+        place,
+        *both,
+        even_t,
+        odd_t,
+        specs=[SM] + [VM] * 5,
+    )
     sent = jax.ShapeDtypeStruct((tok, cols), BF16)
-    down_sum = None
-    for k in range(half - 1):
-        adders = [functools.partial(add_kernel, 2 * k + i) for i in range(2)]
-        if k == 0:
-            adders = [
-                functools.partial(first_add_kernel, i, r)
-                for i, r in enumerate((slice(0, cut), slice(cut, tok)))
-            ]
-        else:
-            up = lax.optimization_barrier((up, down_sum))[0]
-        up_sum = small(adders[0], sent, terms, up)
-        down = lax.optimization_barrier((down, up_sum))[0]
-        down_sum = small(adders[1], sent, terms, down)
-        up, down = shift(up_sum, 1), shift(down_sum, -1)
-    last = functools.partial(add_kernel, 2 * half - 2)
-    up = lax.optimization_barrier((up, down_sum))[0]
-    total = small(last, tokens, terms, up)
-    return small(last_add_kernel, sent, total, down)
+    return small(last_kernel, sent, place, total, odd_f, even_f, specs=[SM] + [VM] * 3)
 
 
 def solution(mesh):

time: 111 us -> 119 us (1.072)
  the two profiles are of different devices: /device:TPU:26 before, /device:TPU:6 now
where the time goes in v4:
time: 119 us
  starting transfers between devices  69.3 us (58%)
  Pallas kernels  19.3 us (16%)
  blocking collectives  15.9 us (13%)
  waiting for transfers between devices  11.8 us (10%)
  local copies, waits for them, and re-layouts  1.91 us (2%)
    ppermute x14, starting transfers between devices, across(): lax.ppermute(a, 'head', [(2 * c + i, 2 * d + i) for c, d in both for i in...  44.8 us
    ppermute x3, starting transfers between devices, later_z(): return lax.ppermute(a, 'ctx_0', [(i, i + by) for i in range(groups - by)])  20.6 us
    all_gather x1, blocking collectives, per_device(): gathered = lax.all_gather(maps, 'ctx_1')  15.9 us
    pallas_call x1, Pallas kernels, local_maps(): pl.pallas_call(functools.partial(map_kernel, group), out_shape=(jax.Shape...  10.2 us
    pallas_call x20, Pallas kernels, small(): pl.pallas_call(kernel, out_shape=outs, in_specs=specs or [VM] * len(args)...  7.28 us
    ppermute x14, waiting for transfers between devices, across(): lax.ppermute(a, 'head', [(2 * c + i, 2 * d + i) for c, d in both for i in...  5.31 us
    ppermute x3, waiting for transfers between devices, later_z(): return lax.ppermute(a, 'ctx_0', [(i, i + by) for i in range(groups - by)])  5 us
    ppermute x2, starting transfers between devices, mate(): return lax.ppermute(a, 'head', [(i, i ^ 1) for i in range(devices)])  3.96 us
  transfers between devices with their start and end apart: 19, of which 5 were waited for; matrix products, arithmetic and copies ran while one was open for 0% of the time, Pallas kernels for 15%

profile of v4, /device:TPU:6, one launch (start us, length us, event | category | flops | bytes accessed | tf_op | source)
XLA Modules:
  0.0 118.7 jit_solution(14305564941180728332)
XLA Ops:
  0.0 2.0 %collective-permute-start.2 = (bf16[256,4096]{1,0:T(8,128)(2,1)}, bf16[256,4096]{1,0:T(8,128)(2,1)}, u32[]{:S(2)}, u32[]{:S(2)}) collective-permute-start(bf16[256,4096]{1,0:T(8,128)(2,1)} %w_ref.1), channel_id=1, source_target_pairs={{0,1},{1,0},{2,3},{3,2},{4,5},{5,4},{6,7},{7,6},{8,9},{9,8},{10,11... | collective-permute-start | bytes 6291464 | tf_op jit(solution)/shard_map/ppermute | solution.py:354
  2.1 10.2 %shard_map.64 = (bf16[2,128,256]{2,1,0:T(8,128)(2,1)S(1)}, bf16[16,128,256]{2,1,0:T(8,128)(2,1)S(1)}, f32[16,2,128]{2,1,0:T(2,128)S(1)}, bf16[16,128,256]{2,1,0:T(8,128)(2,1)S(1)}) custom-call(bf16[2,512,256]{2,1,0:T(8,128)(2,1)} %k_ref.1, bf16[2,512,256]{2,1,0:T(8,128)(2,1)} %v_ref.1, f32[2,2,512]{2,1,0:T(2,128)} %b_hbm.1), custom_call_target="tpu_custom_call" | custom-call | tf_op jit(solution)/shard_map/pallas_call | solution.py:139
  12.3 15.9 %all-gather = bf16[8,128,256]{2,1,0:T(8,128)(2,1)S(1)} all-gather(bf16[2,128,256]{2,1,0:T(8,128)(2,1)S(1)} %get-tuple-element.35), channel_id=2, replica_groups=mesh['ctx_0'=8,'ctx_1'=4,'head'=16] {'ctx_1'}, dimensions={0}, use_global_device_ids=true | all-gather | bytes 655360 | tf_op jit(solution)/shard_map/all_gather | solution.py:366
  28.2 0.6 shard_map.65
  28.9 0.0 copy-start.4
  28.9 1.8 %collective-permute-start = (bf16[2,128,256]{2,1,0:T(8,128)(2,1)S(1)}, bf16[2,128,256]{2,1,0:T(8,128)(2,1)S(1)}, u32[]{:S(2)}, u32[]{:S(2)}) collective-permute-start(bf16[2,128,256]{2,1,0:T(8,128)(2,1)S(1)} %get-tuple-element.37), channel_id=1, source_target_pairs={{0,64},{64,128},{128,192},{192,256},{256,320},{320,384},{384,448},... | collective-permute-start | bytes 393224 | tf_op jit(solution)/shard_map/ppermute | solution.py:358
  30.7 2.5 %collective-permute-done.earlier_ref.near_ref = bf16[2,128,256]{2,1,0:T(8,128)(2,1)S(1)} collective-permute-done((bf16[2,128,256]{2,1,0:T(8,128)(2,1)S(1)}, bf16[2,128,256]{2,1,0:T(8,128)(2,1)S(1)}, u32[]{:S(2)}, u32[]{:S(2)}) %collective-permute-start) | collective-permute-done | bytes 131104 | tf_op jit(solution)/shard_map/ppermute | solution.py:358
  33.2 0.2 shard_map.66
  33.4 6.2 %collective-permute-start.1 = (bf16[2,128,256]{2,1,0:T(8,128)(2,1)S(1)}, bf16[2,128,256]{2,1,0:T(8,128)(2,1)S(1)}, u32[]{:S(2)}, u32[]{:S(2)}) collective-permute-start(bf16[2,128,256]{2,1,0:T(8,128)(2,1)S(1)} %get-tuple-element.39), channel_id=1, source_target_pairs={{0,128},{64,192},{128,256},{192,320},{256,384},{320,448},{1,129},{... | collective-permute-start | bytes 393224 | tf_op jit(solution)/shard_map/ppermute | solution.py:358
  39.5 2.5 %collective-permute-done.1.far_ref.earlier_ref = bf16[2,128,256]{2,1,0:T(8,128)(2,1)S(1)} collective-permute-done((bf16[2,128,256]{2,1,0:T(8,128)(2,1)S(1)}, bf16[2,128,256]{2,1,0:T(8,128)(2,1)S(1)}, u32[]{:S(2)}, u32[]{:S(2)}) %collective-permute-start.1) | collective-permute-done | bytes 131104 | tf_op jit(solution)/shard_map/ppermute | solution.py:358
  42.0 0.2 shard_map.70
  42.2 12.6 %collective-permute-start.3 = (bf16[2,128,128]{2,1,0:T(8,128)(2,1)S(1)}, bf16[2,128,128]{2,1,0:T(8,128)(2,1)S(1)}, u32[]{:S(2)}, u32[]{:S(2)}) collective-permute-start(bf16[2,128,128]{2,1,0:T(8,128)(2,1)S(1)} %shard_map.70), channel_id=1, source_target_pairs={{0,256},{64,320},{128,384},{192,448},{1,257},{65,321},{129,385},{1... | collective-permute-start | bytes 196616 | tf_op jit(solution)/shard_map/ppermute | solution.py:358
  54.9 0.0 copy-start.2
  54.9 0.9 copy-done.2
  55.8 0.9 copy-done.3
  56.8 1.4 %shard_map.69 = (f32[512,256]{1,0:T(8,128)S(1)}, bf16[512,256]{1,0:T(8,128)(2,1)S(1)}, f32[512,256]{1,0:T(8,128)S(1)}) custom-call(bf16[512,256]{1,0:T(8,128)(2,1)S(1)} %copy-done.2, bf16[2,512,256]{2,1,0:T(8,128)(2,1)S(1)} %copy-done, bf16[2,512,256]{2,1,0:T(8,128)(2,1)S(1)} %copy-done.1, bf16[512,256]{1,0:T(8,128)(2,1)S(1)} %copy-done.3, ...), custom_call_target="tpu_custom_call" | custom-call | tf_op jit(solution)/shard_map/pallas_call | solution.py:265
  58.1 0.4 shard_map.67.entry_ref
  58.5 0.0 collective-permute-done.2.x_ref
  58.5 1.8 %shard_map.68.w_ref = bf16[8,512,256]{2,1,0:T(8,128)(2,1)S(1)} custom-call(s32[1]{0:T(128)} %bitcast.me_ref, bf16[256,4096]{1,0:T(8,128)(2,1)} %w_ref.1, bf16[256,4096]{1,0:T(8,128)(2,1)} %collective-permute-done.2.x_ref), custom_call_target="tpu_custom_call" | custom-call | tf_op jit(solution)/shard_map/pallas_call | solution.py:294
  60.4 0.0 collective-permute-done.3.state_ref
  60.4 0.5 shard_map.71.a_ref
  60.9 1.9 %collective-permute-start.4 = (bf16[512,256]{1,0:T(8,128)(2,1)S(1)}, bf16[512,256]{1,0:T(8,128)(2,1)S(1)}, u32[]{:S(2)}, u32[]{:S(2)}) collective-permute-start(bf16[512,256]{1,0:T(8,128)(2,1)S(1)} %shard_map.71.a_ref), channel_id=1, source_target_pairs={{0,1},{1,0},{2,3},{3,2},{4,5},{5,4},{6,7},{7,6},{8,9},{9,8},{10,11... | collective-permute-start | bytes 786440 | tf_op jit(solution)/shard_map/ppermute | solution.py:354
  62.8 1.5 %collective-permute-done.4.b_ref = bf16[512,256]{1,0:T(8,128)(2,1)S(1)} collective-permute-done((bf16[512,256]{1,0:T(8,128)(2,1)S(1)}, bf16[512,256]{1,0:T(8,128)(2,1)S(1)}, u32[]{:S(2)}, u32[]{:S(2)}) %collective-permute-start.4) | collective-permute-done | bytes 262176 | tf_op jit(solution)/shard_map/ppermute | solution.py:354
  64.3 0.3 shard_map.72
  64.6 3.5 %collective-permute-start.7 = (bf16[256,256]{1,0:T(8,128)(2,1)S(1)}, bf16[256,256]{1,0:T(8,128)(2,1)S(1)}, u32[]{:S(2)}, u32[]{:S(2)}) collective-permute-start(bf16[256,256]{1,0:T(8,128)(2,1)S(1)} %get-tuple-element.53), channel_id=1, source_target_pairs={{0,2},{1,3},{4,6},{5,7},{8,10},{9,11},{12,14},{13,15},{2,0},{3,1},... | collective-permute-start | bytes 393224 | tf_op jit(solution)/shard_map/ppermute | solution.py:351
  68.1 5.2 %collective-permute-start.6 = (bf16[256,256]{1,0:T(8,128)(2,1)S(1)}, bf16[256,256]{1,0:T(8,128)(2,1)S(1)}, u32[]{:S(2)}, u32[]{:S(2)}) collective-permute-start(bf16[256,256]{1,0:T(8,128)(2,1)S(1)} %get-tuple-element.50), channel_id=1, source_target_pairs={{2,4},{3,5},{6,8},{7,9},{10,12},{11,13},{14,0},{15,1},{4,2},{5,3},... | collective-permute-start | bytes 393224 | tf_op jit(solution)/shard_map/ppermute | solution.py:351
  73.3 0.3 shard_map.73
  73.6 1.9 %collective-permute-start.5 = (bf16[256,256]{1,0:T(8,128)(2,1)S(1)}, bf16[256,256]{1,0:T(8,128)(2,1)S(1)}, u32[]{:S(2)}, u32[]{:S(2)}) collective-permute-start(bf16[256,256]{1,0:T(8,128)(2,1)S(1)} %get-tuple-element.52), channel_id=1, source_target_pairs={{0,2},{1,3},{4,6},{5,7},{8,10},{9,11},{12,14},{13,15},{2,0},{3,1},... | collective-permute-start | bytes 393224 | tf_op jit(solution)/shard_map/ppermute | solution.py:351
  75.5 4.6 %collective-permute-start.11 = (bf16[256,256]{1,0:T(8,128)(2,1)S(1)}, bf16[256,256]{1,0:T(8,128)(2,1)S(1)}, u32[]{:S(2)}, u32[]{:S(2)}) collective-permute-start(bf16[256,256]{1,0:T(8,128)(2,1)S(1)} %get-tuple-element.54), channel_id=1, source_target_pairs={{2,4},{3,5},{6,8},{7,9},{10,12},{11,13},{14,0},{15,1},{4,2},{5,3},... | collective-permute-start | bytes 393224 | tf_op jit(solution)/shard_map/ppermute | solution.py:351
  80.1 0.0 collective-permute-done.7.refs_0_
  80.1 0.2 shard_map.74
  80.4 2.5 %collective-permute-start.10 = (bf16[256,256]{1,0:T(8,128)(2,1)S(1)}, bf16[256,256]{1,0:T(8,128)(2,1)S(1)}, u32[]{:S(2)}, u32[]{:S(2)}) collective-permute-start(bf16[256,256]{1,0:T(8,128)(2,1)S(1)} %shard_map.74), channel_id=1, source_target_pairs={{2,4},{3,5},{6,8},{7,9},{10,12},{11,13},{14,0},{15,1},{4,2},{5,3},... | collective-permute-start | bytes 393224 | tf_op jit(solution)/shard_map/ppermute | solution.py:351
  82.8 0.0 collective-permute-done.6.refs_0_
  82.9 0.2 shard_map.75
  83.1 2.7 %collective-permute-start.9 = (bf16[256,256]{1,0:T(8,128)(2,1)S(1)}, bf16[256,256]{1,0:T(8,128)(2,1)S(1)}, u32[]{:S(2)}, u32[]{:S(2)}) collective-permute-start(bf16[256,256]{1,0:T(8,128)(2,1)S(1)} %shard_map.75), channel_id=1, source_target_pairs={{0,2},{1,3},{4,6},{5,7},{8,10},{9,11},{12,14},{13,15},{2,0},{3,1},... | collective-permute-start | bytes 393224 | tf_op jit(solution)/shard_map/ppermute | solution.py:351
  85.8 0.0 collective-permute-done.5.refs_0_
  85.8 0.2 shard_map.76
  86.1 3.8 %collective-permute-start.8 = (bf16[256,256]{1,0:T(8,128)(2,1)S(1)}, bf16[256,256]{1,0:T(8,128)(2,1)S(1)}, u32[]{:S(2)}, u32[]{:S(2)}) collective-permute-start(bf16[256,256]{1,0:T(8,128)(2,1)S(1)} %shard_map.76), channel_id=1, source_target_pairs={{2,4},{3,5},{6,8},{7,9},{10,12},{11,13},{14,0},{15,1},{4,2},{5,3},... | collective-permute-start | bytes 393224 | tf_op jit(solution)/shard_map/ppermute | solution.py:351
  89.9 0.0 collective-permute-done.11.refs_0_
  89.9 0.2 shard_map.77
  90.1 2.6 %collective-permute-start.13 = (bf16[256,256]{1,0:T(8,128)(2,1)S(1)}, bf16[256,256]{1,0:T(8,128)(2,1)S(1)}, u32[]{:S(2)}, u32[]{:S(2)}) collective-permute-start(bf16[256,256]{1,0:T(8,128)(2,1)S(1)} %shard_map.77), channel_id=1, source_target_pairs={{0,2},{1,3},{4,6},{5,7},{8,10},{9,11},{12,14},{13,15},{2,0},{3,1},... | collective-permute-start | bytes 393224 | tf_op jit(solution)/shard_map/ppermute | solution.py:351
  92.7 0.0 collective-permute-done.10.refs_0_
  92.7 0.2 shard_map.78
  92.9 3.3 %collective-permute-start.15 = (bf16[256,256]{1,0:T(8,128)(2,1)S(1)}, bf16[256,256]{1,0:T(8,128)(2,1)S(1)}, u32[]{:S(2)}, u32[]{:S(2)}) collective-permute-start(bf16[256,256]{1,0:T(8,128)(2,1)S(1)} %shard_map.78), channel_id=1, source_target_pairs={{0,2},{1,3},{4,6},{5,7},{8,10},{9,11},{12,14},{13,15},{2,0},{3,1},... | collective-permute-start | bytes 393224 | tf_op jit(solution)/shard_map/ppermute | solution.py:351
  96.2 0.0 collective-permute-done.9.refs_0_
  96.2 0.2 shard_map.79
  96.5 3.3 %collective-permute-start.17 = (bf16[256,256]{1,0:T(8,128)(2,1)S(1)}, bf16[256,256]{1,0:T(8,128)(2,1)S(1)}, u32[]{:S(2)}, u32[]{:S(2)}) collective-permute-start(bf16[256,256]{1,0:T(8,128)(2,1)S(1)} %shard_map.79), channel_id=1, source_target_pairs={{2,4},{3,5},{6,8},{7,9},{10,12},{11,13},{14,0},{15,1},{4,2},{5,3},... | collective-permute-start | bytes 393224 | tf_op jit(solution)/shard_map/ppermute | solution.py:351
  99.7 0.0 collective-permute-done.8.refs_0_
  99.7 0.2 shard_map.80
  100.0 1.9 %collective-permute-start.12 = (bf16[256,256]{1,0:T(8,128)(2,1)S(1)}, bf16[256,256]{1,0:T(8,128)(2,1)S(1)}, u32[]{:S(2)}, u32[]{:S(2)}) collective-permute-start(bf16[256,256]{1,0:T(8,128)(2,1)S(1)} %shard_map.80), channel_id=1, source_target_pairs={{0,2},{1,3},{4,6},{5,7},{8,10},{9,11},{12,14},{13,15},{2,0},{3,1},... | collective-permute-start | bytes 393224 | tf_op jit(solution)/shard_map/ppermute | solution.py:351
  101.9 0.0 collective-permute-done.13.refs_0_
  101.9 0.2 shard_map.81
  102.2 4.6 %collective-permute-start.14 = (bf16[256,256]{1,0:T(8,128)(2,1)S(1)}, bf16[256,256]{1,0:T(8,128)(2,1)S(1)}, u32[]{:S(2)}, u32[]{:S(2)}) collective-permute-start(bf16[256,256]{1,0:T(8,128)(2,1)S(1)} %shard_map.81), channel_id=1, source_target_pairs={{2,4},{3,5},{6,8},{7,9},{10,12},{11,13},{14,0},{15,1},{4,2},{5,3},... | collective-permute-start | bytes 393224 | tf_op jit(solution)/shard_map/ppermute | solution.py:351
  106.7 0.0 collective-permute-done.15.refs_0_
  106.8 0.2 shard_map.83
  107.0 0.2 shard_map.84
  107.2 2.6 %collective-permute-start.18 = (bf16[256,256]{1,0:T(8,128)(2,1)S(1)}, bf16[256,256]{1,0:T(8,128)(2,1)S(1)}, u32[]{:S(2)}, u32[]{:S(2)}) collective-permute-start(bf16[256,256]{1,0:T(8,128)(2,1)S(1)} %shard_map.84), channel_id=1, source_target_pairs={{0,2},{1,3},{4,6},{5,7},{8,10},{9,11},{12,14},{13,15},{2,0},{3,1},... | collective-permute-start | bytes 393224 | tf_op jit(solution)/shard_map/ppermute | solution.py:351
  109.8 2.5 %collective-permute-start.16 = (bf16[256,256]{1,0:T(8,128)(2,1)S(1)}, bf16[256,256]{1,0:T(8,128)(2,1)S(1)}, u32[]{:S(2)}, u32[]{:S(2)}) collective-permute-start(bf16[256,256]{1,0:T(8,128)(2,1)S(1)} %shard_map.83), channel_id=1, source_target_pairs={{2,4},{3,5},{6,8},{7,9},{10,12},{11,13},{14,0},{15,1},{4,2},{5,3},... | collective-permute-start | bytes 393224 | tf_op jit(solution)/shard_map/ppermute | solution.py:351
  112.3 0.0 collective-permute-done.12.even_ref
  112.3 0.0 collective-permute-done.14.odd_ref
  112.3 0.3 shard_map.82.sum_ref
  112.6 1.5 %collective-permute-done.18.odd_ref = bf16[256,256]{1,0:T(8,128)(2,1)S(1)} collective-permute-done((bf16[256,256]{1,0:T(8,128)(2,1)S(1)}, bf16[256,256]{1,0:T(8,128)(2,1)S(1)}, u32[]{:S(2)}, u32[]{:S(2)}) %collective-permute-start.18) | collective-permute-done | bytes 131104 | tf_op jit(solution)/shard_map/ppermute | solution.py:351
  114.1 3.8 %collective-permute-done.16.even_ref = bf16[256,256]{1,0:T(8,128)(2,1)S(1)} collective-permute-done((bf16[256,256]{1,0:T(8,128)(2,1)S(1)}, bf16[256,256]{1,0:T(8,128)(2,1)S(1)}, u32[]{:S(2)}, u32[]{:S(2)}) %collective-permute-start.16) | collective-permute-done | bytes 131104 | tf_op jit(solution)/shard_map/ppermute | solution.py:351
  117.9 0.8 shard_map.85
  (9 shorter events, 0.0 us)
Async XLA Ops:
  0.0 54.8 %copy-start.1 = (bf16[2,512,256]{2,1,0:T(8,128)(2,1)S(1)}, bf16[2,512,256]{2,1,0:T(8,128)(2,1)}, u32[]{:S(2)}) copy-start(bf16[2,512,256]{2,1,0:T(8,128)(2,1)} %v_ref.1) | copy-start | bytes 1572868
  0.0 54.9 %copy-start = (bf16[2,512,256]{2,1,0:T(8,128)(2,1)S(1)}, bf16[2,512,256]{2,1,0:T(8,128)(2,1)}, u32[]{:S(2)}) copy-start(bf16[2,512,256]{2,1,0:T(8,128)(2,1)} %k_ref.1) | copy-start | bytes 1572868
  0.0 58.5 %collective-permute-start.2 = (bf16[256,4096]{1,0:T(8,128)(2,1)}, bf16[256,4096]{1,0:T(8,128)(2,1)}, u32[]{:S(2)}, u32[]{:S(2)}) collective-permute-start(bf16[256,4096]{1,0:T(8,128)(2,1)} %w_ref.1), channel_id=1, source_target_pairs={{0,1},{1,0},{2,3},{3,2},{4,5},{5,4},{6,7},{7,6},{8,9},{9,8},{10,11... | collective-permute-start | bytes 6291464 | tf_op jit(solution)/shard_map/ppermute | solution.py:354
  28.9 13.2 %copy-start.4 = (f32[2,128,256]{2,1,0:T(8,128)}, f32[2,128,256]{2,1,0:T(8,128)S(1)}, u32[]{:S(2)}) copy-start(f32[2,128,256]{2,1,0:T(8,128)S(1)} %get-tuple-element.36.in_ref) | copy-start | bytes 786436
  28.9 4.3 %collective-permute-start = (bf16[2,128,256]{2,1,0:T(8,128)(2,1)S(1)}, bf16[2,128,256]{2,1,0:T(8,128)(2,1)S(1)}, u32[]{:S(2)}, u32[]{:S(2)}) collective-permute-start(bf16[2,128,256]{2,1,0:T(8,128)(2,1)S(1)} %get-tuple-element.37), channel_id=1, source_target_pairs={{0,64},{64,128},{128,192},{192,256},{256,320},{320,384},{384,448},... | collective-permute-start | bytes 393224 | tf_op jit(solution)/shard_map/ppermute | solution.py:358
  33.4 8.7 %collective-permute-start.1 = (bf16[2,128,256]{2,1,0:T(8,128)(2,1)S(1)}, bf16[2,128,256]{2,1,0:T(8,128)(2,1)S(1)}, u32[]{:S(2)}, u32[]{:S(2)}) collective-permute-start(bf16[2,128,256]{2,1,0:T(8,128)(2,1)S(1)} %get-tuple-element.39), channel_id=1, source_target_pairs={{0,128},{64,192},{128,256},{192,320},{256,384},{320,448},{1,129},{... | collective-permute-start | bytes 393224 | tf_op jit(solution)/shard_map/ppermute | solution.py:358
  42.2 18.1 %collective-permute-start.3 = (bf16[2,128,128]{2,1,0:T(8,128)(2,1)S(1)}, bf16[2,128,128]{2,1,0:T(8,128)(2,1)S(1)}, u32[]{:S(2)}, u32[]{:S(2)}) collective-permute-start(bf16[2,128,128]{2,1,0:T(8,128)(2,1)S(1)} %shard_map.70), channel_id=1, source_target_pairs={{0,256},{64,320},{128,384},{192,448},{1,257},{65,321},{129,385},{1... | collective-permute-start | bytes 196616 | tf_op jit(solution)/shard_map/ppermute | solution.py:358
  54.9 1.0 copy-start.2
  55.8 0.9 copy-start.3
  56.8 1.4 %copy-start.5 = (f32[2,128,256]{2,1,0:T(8,128)S(1)}, f32[2,128,256]{2,1,0:T(8,128)}, u32[]{:S(2)}) copy-start(f32[2,128,256]{2,1,0:T(8,128)} %copy-done.4) | copy-start | bytes 786436
  60.9 3.4 %collective-permute-start.4 = (bf16[512,256]{1,0:T(8,128)(2,1)S(1)}, bf16[512,256]{1,0:T(8,128)(2,1)S(1)}, u32[]{:S(2)}, u32[]{:S(2)}) collective-permute-start(bf16[512,256]{1,0:T(8,128)(2,1)S(1)} %shard_map.71.a_ref), channel_id=1, source_target_pairs={{0,1},{1,0},{2,3},{3,2},{4,5},{5,4},{6,7},{7,6},{8,9},{9,8},{10,11... | collective-permute-start | bytes 786440 | tf_op jit(solution)/shard_map/ppermute | solution.py:354
  64.6 15.5 %collective-permute-start.7 = (bf16[256,256]{1,0:T(8,128)(2,1)S(1)}, bf16[256,256]{1,0:T(8,128)(2,1)S(1)}, u32[]{:S(2)}, u32[]{:S(2)}) collective-permute-start(bf16[256,256]{1,0:T(8,128)(2,1)S(1)} %get-tuple-element.53), channel_id=1, source_target_pairs={{0,2},{1,3},{4,6},{5,7},{8,10},{9,11},{12,14},{13,15},{2,0},{3,1},... | collective-permute-start | bytes 393224 | tf_op jit(solution)/shard_map/ppermute | solution.py:351
  68.1 14.7 %collective-permute-start.6 = (bf16[256,256]{1,0:T(8,128)(2,1)S(1)}, bf16[256,256]{1,0:T(8,128)(2,1)S(1)}, u32[]{:S(2)}, u32[]{:S(2)}) collective-permute-start(bf16[256,256]{1,0:T(8,128)(2,1)S(1)} %get-tuple-element.50), channel_id=1, source_target_pairs={{2,4},{3,5},{6,8},{7,9},{10,12},{11,13},{14,0},{15,1},{4,2},{5,3},... | collective-permute-start | bytes 393224 | tf_op jit(solution)/shard_map/ppermute | solution.py:351
  73.6 12.2 %collective-permute-start.5 = (bf16[256,256]{1,0:T(8,128)(2,1)S(1)}, bf16[256,256]{1,0:T(8,128)(2,1)S(1)}, u32[]{:S(2)}, u32[]{:S(2)}) collective-permute-start(bf16[256,256]{1,0:T(8,128)(2,1)S(1)} %get-tuple-element.52), channel_id=1, source_target_pairs={{0,2},{1,3},{4,6},{5,7},{8,10},{9,11},{12,14},{13,15},{2,0},{3,1},... | collective-permute-start | bytes 393224 | tf_op jit(solution)/shard_map/ppermute | solution.py:351
  75.5 14.3 %collective-permute-start.11 = (bf16[256,256]{1,0:T(8,128)(2,1)S(1)}, bf16[256,256]{1,0:T(8,128)(2,1)S(1)}, u32[]{:S(2)}, u32[]{:S(2)}) collective-permute-start(bf16[256,256]{1,0:T(8,128)(2,1)S(1)} %get-tuple-element.54), channel_id=1, source_target_pairs={{2,4},{3,5},{6,8},{7,9},{10,12},{11,13},{14,0},{15,1},{4,2},{5,3},... | collective-permute-start | bytes 393224 | tf_op jit(solution)/shard_map/ppermute | solution.py:351
  80.4 12.3 %collective-permute-start.10 = (bf16[256,256]{1,0:T(8,128)(2,1)S(1)}, bf16[256,256]{1,0:T(8,128)(2,1)S(1)}, u32[]{:S(2)}, u32[]{:S(2)}) collective-permute-start(bf16[256,256]{1,0:T(8,128)(2,1)S(1)} %shard_map.74), channel_id=1, source_target_pairs={{2,4},{3,5},{6,8},{7,9},{10,12},{11,13},{14,0},{15,1},{4,2},{5,3},... | collective-permute-start | bytes 393224 | tf_op jit(solution)/shard_map/ppermute | solution.py:351
  83.1 13.1 %collective-permute-start.9 = (bf16[256,256]{1,0:T(8,128)(2,1)S(1)}, bf16[256,256]{1,0:T(8,128)(2,1)S(1)}, u32[]{:S(2)}, u32[]{:S(2)}) collective-permute-start(bf16[256,256]{1,0:T(8,128)(2,1)S(1)} %shard_map.75), channel_id=1, source_target_pairs={{0,2},{1,3},{4,6},{5,7},{8,10},{9,11},{12,14},{13,15},{2,0},{3,1},... | collective-permute-start | bytes 393224 | tf_op jit(solution)/shard_map/ppermute | solution.py:351
  86.1 13.7 %collective-permute-start.8 = (bf16[256,256]{1,0:T(8,128)(2,1)S(1)}, bf16[256,256]{1,0:T(8,128)(2,1)S(1)}, u32[]{:S(2)}, u32[]{:S(2)}) collective-permute-start(bf16[256,256]{1,0:T(8,128)(2,1)S(1)} %shard_map.76), channel_id=1, source_target_pairs={{2,4},{3,5},{6,8},{7,9},{10,12},{11,13},{14,0},{15,1},{4,2},{5,3},... | collective-permute-start | bytes 393224 | tf_op jit(solution)/shard_map/ppermute | solution.py:351
  90.1 11.8 %collective-permute-start.13 = (bf16[256,256]{1,0:T(8,128)(2,1)S(1)}, bf16[256,256]{1,0:T(8,128)(2,1)S(1)}, u32[]{:S(2)}, u32[]{:S(2)}) collective-permute-start(bf16[256,256]{1,0:T(8,128)(2,1)S(1)} %shard_map.77), channel_id=1, source_target_pairs={{0,2},{1,3},{4,6},{5,7},{8,10},{9,11},{12,14},{13,15},{2,0},{3,1},... | collective-permute-start | bytes 393224 | tf_op jit(solution)/shard_map/ppermute | solution.py:351
  92.9 13.8 %collective-permute-start.15 = (bf16[256,256]{1,0:T(8,128)(2,1)S(1)}, bf16[256,256]{1,0:T(8,128)(2,1)S(1)}, u32[]{:S(2)}, u32[]{:S(2)}) collective-permute-start(bf16[256,256]{1,0:T(8,128)(2,1)S(1)} %shard_map.78), channel_id=1, source_target_pairs={{0,2},{1,3},{4,6},{5,7},{8,10},{9,11},{12,14},{13,15},{2,0},{3,1},... | collective-permute-start | bytes 393224 | tf_op jit(solution)/shard_map/ppermute | solution.py:351
  96.5 10.5 %collective-permute-start.17 = (bf16[256,256]{1,0:T(8,128)(2,1)S(1)}, bf16[256,256]{1,0:T(8,128)(2,1)S(1)}, u32[]{:S(2)}, u32[]{:S(2)}) collective-permute-start(bf16[256,256]{1,0:T(8,128)(2,1)S(1)} %shard_map.79), channel_id=1, source_target_pairs={{2,4},{3,5},{6,8},{7,9},{10,12},{11,13},{14,0},{15,1},{4,2},{5,3},... | collective-permute-start | bytes 393224 | tf_op jit(solution)/shard_map/ppermute | solution.py:351
  100.0 12.3 %collective-permute-start.12 = (bf16[256,256]{1,0:T(8,128)(2,1)S(1)}, bf16[256,256]{1,0:T(8,128)(2,1)S(1)}, u32[]{:S(2)}, u32[]{:S(2)}) collective-permute-start(bf16[256,256]{1,0:T(8,128)(2,1)S(1)} %shard_map.80), channel_id=1, source_target_pairs={{0,2},{1,3},{4,6},{5,7},{8,10},{9,11},{12,14},{13,15},{2,0},{3,1},... | collective-permute-start | bytes 393224 | tf_op jit(solution)/shard_map/ppermute | solution.py:351
  102.2 10.2 %collective-permute-start.14 = (bf16[256,256]{1,0:T(8,128)(2,1)S(1)}, bf16[256,256]{1,0:T(8,128)(2,1)S(1)}, u32[]{:S(2)}, u32[]{:S(2)}) collective-permute-start(bf16[256,256]{1,0:T(8,128)(2,1)S(1)} %shard_map.81), channel_id=1, source_target_pairs={{2,4},{3,5},{6,8},{7,9},{10,12},{11,13},{14,0},{15,1},{4,2},{5,3},... | collective-permute-start | bytes 393224 | tf_op jit(solution)/shard_map/ppermute | solution.py:351
  107.2 6.9 %collective-permute-start.18 = (bf16[256,256]{1,0:T(8,128)(2,1)S(1)}, bf16[256,256]{1,0:T(8,128)(2,1)S(1)}, u32[]{:S(2)}, u32[]{:S(2)}) collective-permute-start(bf16[256,256]{1,0:T(8,128)(2,1)S(1)} %shard_map.84), channel_id=1, source_target_pairs={{0,2},{1,3},{4,6},{5,7},{8,10},{9,11},{12,14},{13,15},{2,0},{3,1},... | collective-permute-start | bytes 393224 | tf_op jit(solution)/shard_map/ppermute | solution.py:351
  109.8 8.1 %collective-permute-start.16 = (bf16[256,256]{1,0:T(8,128)(2,1)S(1)}, bf16[256,256]{1,0:T(8,128)(2,1)S(1)}, u32[]{:S(2)}, u32[]{:S(2)}) collective-permute-start(bf16[256,256]{1,0:T(8,128)(2,1)S(1)} %shard_map.83), channel_id=1, source_target_pairs={{2,4},{3,5},{6,8},{7,9},{10,12},{11,13},{14,0},{15,1},{4,2},{5,3},... | collective-permute-start | bytes 393224 | tf_op jit(solution)/shard_map/ppermute | solution.py:351

commit v5 on v4

--- a/solution.py
+++ b/solution.py
@@ -306,35 +306,35 @@
     return dot(a, w[:rows]) + dot(b, w[rows:])
 
 
-def hop_kernel(jobs, got_count, me_ref, a_ref, b_ref, w_ref, *refs):
+def far_kernel(me_ref, a_ref, b_ref, w_ref, ahead_ref, back_ref):
+    odd = (me_ref[0] // 2) % 2 != 0
+    out = term(a_ref[...], b_ref[...], w_ref[0]).astype(BF16)
+    cut = ahead_ref.shape[0]
+    ahead_ref[...] = jnp.where(odd, out[cut:], out[:cut])
+    back_ref[...] = jnp.where(odd, out[:cut], out[cut:])
+
+
+def hop_kernel(at, side, me_ref, a_ref, b_ref, w_ref, got_ref, o_ref):
     odd = (me_ref[0] // 2) % 2
-    got_refs, out_refs = refs[:got_count], refs[got_count:]
-    cut = out_refs[0].shape[0]
-    for i, (at, side) in enumerate(jobs):
-        rows = pl.ds(pl.multiple_of(((odd + side) % 2) * cut, cut), cut)
-        out = term(a_ref[rows, :], b_ref[rows, :], w_ref[at])
-        if got_refs:
-            out = out + got_refs[i][...].astype(F32)
-        out_refs[i][...] = out.astype(BF16)
-
-
-def own_kernel(me_ref, a_ref, b_ref, w_ref, even_ref, odd_ref, o_ref):
-    odd = (me_ref[0] // 2) % 2
-    cut = even_ref.shape[0]
-    out = term(a_ref[...], b_ref[...], w_ref[w_ref.shape[0] - 1])
+    out = term(a_ref[...], b_ref[...], w_ref[at])
+    cut = got_ref.shape[0]
     for i in range(2):
         rows = slice(i * cut, (i + 1) * cut)
-        got = jnp.where(odd == i, even_ref[...].astype(F32), odd_ref[...].astype(F32))
-        o_ref[rows] = out[rows] + got
-
-
-def last_kernel(me_ref, sum_ref, even_ref, odd_ref, o_ref):
-    odd = (me_ref[0] // 2) % 2
-    cut = even_ref.shape[0]
-    for i in range(2):
-        rows = slice(i * cut, (i + 1) * cut)
-        got = jnp.where(odd == i, even_ref[...].astype(F32), odd_ref[...].astype(F32))
-        o_ref[rows] = (sum_ref[rows] + got).astype(BF16)
+        got = jnp.where((odd + side) % 2 == i, got_ref[...].astype(F32), 0.0)
+        o_ref[rows] = (out[rows] + got).astype(BF16)
+
+
+def rest_kernel(picks, a_ref, b_ref, w_ref, o_ref):
+    for i, at in enumerate(picks):
+        o_ref[i] = term(a_ref[...], b_ref[...], w_ref[at])
+
+
+def add_kernel(at, terms_ref, got_ref, o_ref):
+    o_ref[...] = (terms_ref[at] + got_ref[...].astype(F32)).astype(o_ref.dtype)
+
+
+def last_kernel(sum_ref, got_ref, o_ref):
+    o_ref[...] = (sum_ref[...] + got_ref[...].astype(F32)).astype(BF16)
 
 
 def per_device(queries, keys, values, betas, gate, out_weight):
@@ -363,15 +363,13 @@
     wide_map = jax.ShapeDtypeStruct((heads, HD, 2 * HD), F32)
     wide_send = jax.ShapeDtypeStruct((heads, HD, 2 * HD), BF16)
     state_send = jax.ShapeDtypeStruct((heads, HD, HD), BF16)
+    tokens = jax.ShapeDtypeStruct((tok, cols), F32)
     gathered = lax.all_gather(maps, "ctx_1")
     x = lax.axis_index("ctx_1").astype(jnp.int32).reshape(1)
     send, total, inside = small(
         fold_kernel, (wide_send, wide_map, wide_map), x, gathered, specs=[SM, VM]
     )
     near = later_z(send, 1)
-    send, pair = small(join_kernel, (wide_send, wide_map), total, near)
-    far = later_z(send, 2)
-    tokens = jax.ShapeDtypeStruct((tok, cols), F32)
     local, carry, silu = small(
         local_kernel,
         (tokens, jax.ShapeDtypeStruct((tok, cols), BF16), tokens),
@@ -381,14 +379,17 @@
         gate,
         inverse,
         scales,
-        lax.optimization_barrier((prefixes, near))[0],
-    )
+        lax.optimization_barrier((prefixes, total))[0],
+    )
+    near = lax.optimization_barrier((near, silu))[0]
+    send, pair = small(join_kernel, (wide_send, wide_map), total, near)
+    far = later_z(send, 2)
+    place = me.astype(jnp.int32).reshape(1)
+    ring_w = pack(chips, place, out_weight, lax.optimization_barrier((mate_weight, pair))[0])
+    far = lax.optimization_barrier((far, ring_w))[0]
     send = small(carry_kernel, state_send, pair, far)
     state = later_z(send, 4)
     entry = small(entry_kernel, wide_map, inside, near, far)
-    place = me.astype(jnp.int32).reshape(1)
-    ring_w = pack(chips, place, out_weight, lax.optimization_barrier((mate_weight, near))[0])
-    entry = lax.optimization_barrier((entry, ring_w, silu))[0]
     mixed_in = small(
         mix_kernel,
         jax.ShapeDtypeStruct((tok, cols), BF16),
@@ -401,44 +402,37 @@
     mate_in = mate(mixed_in)
 
     half = chips // 2
-    chunk = jax.ShapeDtypeStruct((tok // 2, cols), BF16)
+    sent = jax.ShapeDtypeStruct((tok, cols), BF16)
+    part = jax.ShapeDtypeStruct((tok // 2, cols), BF16)
     both = (mixed_in, mate_in, ring_w)
-
-    def hop(jobs, prior, *got):
-        got = [lax.optimization_barrier((g, prior))[0] for g in got]
-        ins = both if prior is None or got else (lax.optimization_barrier((mixed_in, prior))[0], *both[1:])
-        body = functools.partial(hop_kernel, jobs, len(got))
-        return small(body, (chunk,) * len(jobs), place, *ins, *got, specs=[SM] + [VM] * (3 + len(got)))
-
-    slots = [(half, 0)] + [s for k in range(half - 1, 0, -1) for s in ((k, 1), (k, 0))]
-    prior, moved = None, []
-    for n, (k, late) in enumerate(slots):
-        at = [half - k, 0 if k == half else 2 * half - 1 - k]
-        side = [late, 1 - late]
-        if n < 2:
-            ahead, back = hop([(at[0], side[0]), (at[1], side[1])], prior)
-            prior = back
-        else:
-            from_even, from_odd = moved[n - 2]
-            order = (1, 0) if n % 4 in (2, 3) else (0, 1)
-            sums = {}
-            for i in order:
-                (sums[i],) = hop([(at[i], side[i])], prior, from_odd if i == 0 else from_even)
-                prior = sums[i]
-            ahead, back = sums[0], sums[1]
-        moved.append((across(ahead, 0), across(back, 1)))
-    (even_t, odd_t), (even_f, odd_f) = moved[-2:]
-    total = small(
-        own_kernel,
-        jax.ShapeDtypeStruct((tok, cols), F32),
-        place,
-        *both,
-        even_t,
-        odd_t,
-        specs=[SM] + [VM] * 5,
-    )
-    sent = jax.ShapeDtypeStruct((tok, cols), BF16)
-    return small(last_kernel, sent, place, total, odd_f, even_f, specs=[SM] + [VM] * 3)
+    ahead, back = small(far_kernel, (part, part), place, *both, specs=[SM] + [VM] * 3)
+    got, prior, terms = (across(back, 1), across(ahead, 0)), None, None
+    for k in range(half - 1, 0, -1):
+        sums = [None, None]
+        for i in (1, 0) if k % 2 else (0, 1):
+            came = got[i]
+            if prior is not None:
+                came = lax.optimization_barrier((came, prior))[0]
+            if k == half - 1:
+                body = functools.partial(hop_kernel, 1 + i * (half - 1), i)
+                sums[i] = small(body, sent, place, *both, came, specs=[SM] + [VM] * 4)
+            else:
+                body = functools.partial(add_kernel, 2 * (half - 2 - k) + i)
+                sums[i] = small(body, sent, terms, came)
+            prior = sums[i]
+        if k == half - 1:
+            picks = [j + i * (half - 1) for j in range(2, half) for i in range(2)] + [chips - 1]
+            terms = small(
+                functools.partial(rest_kernel, picks),
+                jax.ShapeDtypeStruct((len(picks), tok, cols), F32),
+                lax.optimization_barrier((mixed_in, prior))[0],
+                mate_in,
+                ring_w,
+            )
+        got = (across(sums[1], 1), across(sums[0], 0))
+    came = lax.optimization_barrier((got[0], prior))[0]
+    total = small(functools.partial(add_kernel, 2 * half - 4), tokens, terms, came)
+    return small(last_kernel, sent, total, got[1])
 
 
 def solution(mesh):

time: 119 us -> 103 us (0.87)
  starting transfers between devices: 69.3 us -> 51.4 us
  waiting for transfers between devices: 11.8 us -> 16.8 us
  local copies, waits for them, and re-layouts: 1.91 us -> 0.02 us
  Pallas kernels: 19.3 us -> 18 us
    ppermute x14 -> x8, starting transfers between devices: 44.8 us -> 26.9 us  [across(): lax.ppermute(a, 'head', [(2 * c + i, 2 * d + i) for c, d in both for i in...]
    ppermute x14 -> x8, waiting for transfers between devices: 5.31 us -> 12 us  [across(): lax.ppermute(a, 'head', [(2 * c + i, 2 * d + i) for c, d in both for i in...]
    unnamed x12 -> x8, local copies, waits for them, and re-layouts: 1.91 us -> 0.02 us
    ppermute x3, waiting for transfers between devices: 5 us -> 3.27 us  [later_z(): return lax.ppermute(a, 'ctx_0', [(i, i + by) for i in range(groups - by)])]
    pallas_call x20 -> x16, Pallas kernels: 7.28 us -> 6.03 us  [small(): pl.pallas_call(kernel, out_shape=outs, in_specs=specs or [VM] * len(args)...]
  transfers between devices with their start and end apart: 19 -> 13, of which waited for: 5 -> 9; matrix products, arithmetic and copies ran while one was open for 0% -> 0% of each run, Pallas kernels for 15% -> 16%
where the time goes in v5:
time: 103 us; the launch traced here: 102 us
  starting transfers between devices  51.4 us (50%)
  Pallas kernels  18 us (17%)
  waiting for transfers between devices  16.8 us (16%)
  blocking collectives  15.9 us (15%)
    ppermute x8, starting transfers between devices, across(): lax.ppermute(a, 'head', [(2 * c + i, 2 * d + i) for c, d in both for i in...  26.9 us
    ppermute x3, starting transfers between devices, later_z(): return lax.ppermute(a, 'ctx_0', [(i, i + by) for i in range(groups - by)])  20.6 us
    all_gather x1, blocking collectives, per_device(): gathered = lax.all_gather(maps, 'ctx_1')  15.9 us
    ppermute x8, waiting for transfers between devices, across(): lax.ppermute(a, 'head', [(2 * c + i, 2 * d + i) for c, d in both for i in...  12 us
    pallas_call x1, Pallas kernels, local_maps(): pl.pallas_call(functools.partial(map_kernel, group), out_shape=(jax.Shape...  10.2 us
    pallas_call x16, Pallas kernels, small(): pl.pallas_call(kernel, out_shape=outs, in_specs=specs or [VM] * len(args)...  6.03 us
    ppermute x2, starting transfers between devices, mate(): return lax.ppermute(a, 'head', [(i, i ^ 1) for i in range(devices)])  3.98 us
    ppermute x3, waiting for transfers between devices, later_z(): return lax.ppermute(a, 'ctx_0', [(i, i + by) for i in range(groups - by)])  3.27 us
  transfers between devices with their start and end apart: 13, of which 9 were waited for; matrix products, arithmetic and copies ran while one was open for 0% of the time, Pallas kernels for 16%

profile of v5, /device:TPU:6, one launch (start us, length us, event | category | flops | bytes accessed | tf_op | source)
XLA Modules:
  0.0 102.4 jit_solution(13284033836460406703)
XLA Ops:
  0.0 0.0 copy-start.1
  0.0 0.0 copy-start
  0.0 0.0 copy-start.3
  0.0 0.0 copy-start.2
  0.0 2.1 %collective-permute-start.2 = (bf16[256,4096]{1,0:T(8,128)(2,1)}, bf16[256,4096]{1,0:T(8,128)(2,1)}, u32[]{:S(2)}, u32[]{:S(2)}) collective-permute-start(bf16[256,4096]{1,0:T(8,128)(2,1)} %w_ref.1), channel_id=1, source_target_pairs={{0,1},{1,0},{2,3},{3,2},{4,5},{5,4},{6,7},{7,6},{8,9},{9,8},{10,11... | collective-permute-start | bytes 6291464 | tf_op jit(solution)/shard_map/ppermute | solution.py:354
  2.1 10.2 %shard_map.64 = (bf16[2,128,256]{2,1,0:T(8,128)(2,1)S(1)}, bf16[16,128,256]{2,1,0:T(8,128)(2,1)S(1)}, f32[16,2,128]{2,1,0:T(2,128)S(1)}, bf16[16,128,256]{2,1,0:T(8,128)(2,1)S(1)}) custom-call(bf16[2,512,256]{2,1,0:T(8,128)(2,1)} %k_ref.1, bf16[2,512,256]{2,1,0:T(8,128)(2,1)} %v_ref.1, f32[2,2,512]{2,1,0:T(2,128)} %b_hbm.1), custom_call_target="tpu_custom_call" | custom-call | tf_op jit(solution)/shard_map/pallas_call | solution.py:139
  12.3 15.9 %all-gather = bf16[8,128,256]{2,1,0:T(8,128)(2,1)S(1)} all-gather(bf16[2,128,256]{2,1,0:T(8,128)(2,1)S(1)} %get-tuple-element.30), channel_id=2, replica_groups=mesh['ctx_0'=8,'ctx_1'=4,'head'=16] {'ctx_1'}, dimensions={0}, use_global_device_ids=true | all-gather | bytes 655360 | tf_op jit(solution)/shard_map/all_gather | solution.py:367
  28.2 0.6 shard_map.65
  28.9 1.8 %collective-permute-start = (bf16[2,128,256]{2,1,0:T(8,128)(2,1)S(1)}, bf16[2,128,256]{2,1,0:T(8,128)(2,1)S(1)}, u32[]{:S(2)}, u32[]{:S(2)}) collective-permute-start(bf16[2,128,256]{2,1,0:T(8,128)(2,1)S(1)} %get-tuple-element.32), channel_id=1, source_target_pairs={{0,64},{64,128},{128,192},{192,256},{256,320},{320,384},{384,448},... | collective-permute-start | bytes 393224 | tf_op jit(solution)/shard_map/ppermute | solution.py:358
  30.7 0.0 copy-done.1
  30.7 0.0 copy-done
  30.7 0.0 copy-done.3
  30.7 0.0 copy-done.2
  30.7 1.4 %shard_map.66 = (f32[512,256]{1,0:T(8,128)S(1)}, bf16[512,256]{1,0:T(8,128)(2,1)S(1)}, f32[512,256]{1,0:T(8,128)S(1)}) custom-call(bf16[512,256]{1,0:T(8,128)(2,1)S(1)} %copy-done.2, bf16[2,512,256]{2,1,0:T(8,128)(2,1)S(1)} %copy-done, bf16[2,512,256]{2,1,0:T(8,128)(2,1)S(1)} %copy-done.1, bf16[512,256]{1,0:T(8,128)(2,1)S(1)} %copy-done.3, ...), custom_call_target="tpu_custom_call" | custom-call | tf_op jit(solution)/shard_map/pallas_call | solution.py:265
  32.1 1.1 %collective-permute-done.earlier_ref.near_ref = bf16[2,128,256]{2,1,0:T(8,128)(2,1)S(1)} collective-permute-done((bf16[2,128,256]{2,1,0:T(8,128)(2,1)S(1)}, bf16[2,128,256]{2,1,0:T(8,128)(2,1)S(1)}, u32[]{:S(2)}, u32[]{:S(2)}) %collective-permute-start) | collective-permute-done | bytes 131104 | tf_op jit(solution)/shard_map/ppermute | solution.py:358
  33.2 0.2 shard_map.67
  33.4 6.2 %collective-permute-start.1 = (bf16[2,128,256]{2,1,0:T(8,128)(2,1)S(1)}, bf16[2,128,256]{2,1,0:T(8,128)(2,1)S(1)}, u32[]{:S(2)}, u32[]{:S(2)}) collective-permute-start(bf16[2,128,256]{2,1,0:T(8,128)(2,1)S(1)} %get-tuple-element.40), channel_id=1, source_target_pairs={{0,128},{64,192},{128,256},{192,320},{256,384},{320,448},{1,129},{... | collective-permute-start | bytes 393224 | tf_op jit(solution)/shard_map/ppermute | solution.py:358
  39.6 0.0 collective-permute-done.2.x_ref
  39.6 1.8 %shard_map.68.w_ref = bf16[8,512,256]{2,1,0:T(8,128)(2,1)S(1)} custom-call(s32[1]{0:T(128)} %bitcast.2.me_ref, bf16[256,4096]{1,0:T(8,128)(2,1)} %w_ref.1, bf16[256,4096]{1,0:T(8,128)(2,1)} %collective-permute-done.2.x_ref), custom_call_target="tpu_custom_call" | custom-call | tf_op jit(solution)/shard_map/pallas_call | solution.py:294
  41.4 0.7 collective-permute-done.1.far_ref.earlier_ref
  42.1 0.2 shard_map.70
  42.2 12.6 %collective-permute-start.3 = (bf16[2,128,128]{2,1,0:T(8,128)(2,1)S(1)}, bf16[2,128,128]{2,1,0:T(8,128)(2,1)S(1)}, u32[]{:S(2)}, u32[]{:S(2)}) collective-permute-start(bf16[2,128,128]{2,1,0:T(8,128)(2,1)S(1)} %shard_map.70), channel_id=1, source_target_pairs={{0,256},{64,320},{128,384},{192,448},{1,257},{65,321},{129,385},{1... | collective-permute-start | bytes 196616 | tf_op jit(solution)/shard_map/ppermute | solution.py:358
  54.8 0.4 shard_map.69.entry_ref
  55.2 1.5 %collective-permute-done.3.state_ref = bf16[2,128,128]{2,1,0:T(8,128)(2,1)S(1)} collective-permute-done((bf16[2,128,128]{2,1,0:T(8,128)(2,1)S(1)}, bf16[2,128,128]{2,1,0:T(8,128)(2,1)S(1)}, u32[]{:S(2)}, u32[]{:S(2)}) %collective-permute-start.3) | collective-permute-done | bytes 65568 | tf_op jit(solution)/shard_map/ppermute | solution.py:358
  56.7 0.5 shard_map.71.a_ref
  57.3 1.9 %collective-permute-start.4 = (bf16[512,256]{1,0:T(8,128)(2,1)S(1)}, bf16[512,256]{1,0:T(8,128)(2,1)S(1)}, u32[]{:S(2)}, u32[]{:S(2)}) collective-permute-start(bf16[512,256]{1,0:T(8,128)(2,1)S(1)} %shard_map.71.a_ref), channel_id=1, source_target_pairs={{0,1},{1,0},{2,3},{3,2},{4,5},{5,4},{6,7},{7,6},{8,9},{9,8},{10,11... | collective-permute-start | bytes 786440 | tf_op jit(solution)/shard_map/ppermute | solution.py:354
  59.2 1.5 %collective-permute-done.4.b_ref = bf16[512,256]{1,0:T(8,128)(2,1)S(1)} collective-permute-done((bf16[512,256]{1,0:T(8,128)(2,1)S(1)}, bf16[512,256]{1,0:T(8,128)(2,1)S(1)}, u32[]{:S(2)}, u32[]{:S(2)}) %collective-permute-start.4) | collective-permute-done | bytes 262176 | tf_op jit(solution)/shard_map/ppermute | solution.py:354
  60.7 0.3 shard_map.72
  61.0 3.5 %collective-permute-start.6 = (bf16[256,256]{1,0:T(8,128)(2,1)S(1)}, bf16[256,256]{1,0:T(8,128)(2,1)S(1)}, u32[]{:S(2)}, u32[]{:S(2)}) collective-permute-start(bf16[256,256]{1,0:T(8,128)(2,1)S(1)} %get-tuple-element.47), channel_id=1, source_target_pairs={{0,2},{1,3},{4,6},{5,7},{8,10},{9,11},{12,14},{13,15},{2,0},{3,1},... | collective-permute-start | bytes 393224 | tf_op jit(solution)/shard_map/ppermute | solution.py:351
  64.5 5.2 %collective-permute-start.5 = (bf16[256,256]{1,0:T(8,128)(2,1)S(1)}, bf16[256,256]{1,0:T(8,128)(2,1)S(1)}, u32[]{:S(2)}, u32[]{:S(2)}) collective-permute-start(bf16[256,256]{1,0:T(8,128)(2,1)S(1)} %get-tuple-element.46), channel_id=1, source_target_pairs={{2,4},{3,5},{6,8},{7,9},{10,12},{11,13},{14,0},{15,1},{4,2},{5,3},... | collective-permute-start | bytes 393224 | tf_op jit(solution)/shard_map/ppermute | solution.py:351
  69.6 0.0 collective-permute-done.6.got_ref
  69.7 0.3 shard_map.73
  70.0 4.2 %collective-permute-start.7 = (bf16[512,256]{1,0:T(8,128)(2,1)S(1)}, bf16[512,256]{1,0:T(8,128)(2,1)S(1)}, u32[]{:S(2)}, u32[]{:S(2)}) collective-permute-start(bf16[512,256]{1,0:T(8,128)(2,1)S(1)} %shard_map.73), channel_id=1, source_target_pairs={{2,4},{3,5},{6,8},{7,9},{10,12},{11,13},{14,0},{15,1},{4,2},{5,3},... | collective-permute-start | bytes 786440 | tf_op jit(solution)/shard_map/ppermute | solution.py:351
  74.1 0.0 collective-permute-done.5.got_ref
  74.1 0.3 shard_map.74
  74.4 1.9 %collective-permute-start.9 = (bf16[512,256]{1,0:T(8,128)(2,1)S(1)}, bf16[512,256]{1,0:T(8,128)(2,1)S(1)}, u32[]{:S(2)}, u32[]{:S(2)}) collective-permute-start(bf16[512,256]{1,0:T(8,128)(2,1)S(1)} %shard_map.74), channel_id=1, source_target_pairs={{0,2},{1,3},{4,6},{5,7},{8,10},{9,11},{12,14},{13,15},{2,0},{3,1},... | collective-permute-start | bytes 786440 | tf_op jit(solution)/shard_map/ppermute | solution.py:351
  76.4 0.9 shard_map.75.terms_ref
  77.2 3.6 %collective-permute-done.7.got_ref = bf16[512,256]{1,0:T(8,128)(2,1)S(1)} collective-permute-done((bf16[512,256]{1,0:T(8,128)(2,1)S(1)}, bf16[512,256]{1,0:T(8,128)(2,1)S(1)}, u32[]{:S(2)}, u32[]{:S(2)}) %collective-permute-start.7) | collective-permute-done | bytes 262176 | tf_op jit(solution)/shard_map/ppermute | solution.py:351
  80.9 0.1 shard_map.76
  80.9 1.9 %collective-permute-start.8 = (bf16[512,256]{1,0:T(8,128)(2,1)S(1)}, bf16[512,256]{1,0:T(8,128)(2,1)S(1)}, u32[]{:S(2)}, u32[]{:S(2)}) collective-permute-start(bf16[512,256]{1,0:T(8,128)(2,1)S(1)} %shard_map.76), channel_id=1, source_target_pairs={{0,2},{1,3},{4,6},{5,7},{8,10},{9,11},{12,14},{13,15},{2,0},{3,1},... | collective-permute-start | bytes 786440 | tf_op jit(solution)/shard_map/ppermute | solution.py:351
  82.9 0.7 collective-permute-done.9.got_ref
  83.6 0.1 shard_map.77
  83.6 3.8 %collective-permute-start.11 = (bf16[512,256]{1,0:T(8,128)(2,1)S(1)}, bf16[512,256]{1,0:T(8,128)(2,1)S(1)}, u32[]{:S(2)}, u32[]{:S(2)}) collective-permute-start(bf16[512,256]{1,0:T(8,128)(2,1)S(1)} %shard_map.77), channel_id=1, source_target_pairs={{2,4},{3,5},{6,8},{7,9},{10,12},{11,13},{14,0},{15,1},{4,2},{5,3},... | collective-permute-start | bytes 786440 | tf_op jit(solution)/shard_map/ppermute | solution.py:351
  87.5 2.2 %collective-permute-done.8.got_ref = bf16[512,256]{1,0:T(8,128)(2,1)S(1)} collective-permute-done((bf16[512,256]{1,0:T(8,128)(2,1)S(1)}, bf16[512,256]{1,0:T(8,128)(2,1)S(1)}, u32[]{:S(2)}, u32[]{:S(2)}) %collective-permute-start.8) | collective-permute-done | bytes 262176 | tf_op jit(solution)/shard_map/ppermute | solution.py:351
  89.8 3.6 %collective-permute-start.10 = (bf16[512,256]{1,0:T(8,128)(2,1)S(1)}, bf16[512,256]{1,0:T(8,128)(2,1)S(1)}, u32[]{:S(2)}, u32[]{:S(2)}) collective-permute-start(bf16[512,256]{1,0:T(8,128)(2,1)S(1)} %shard_map.78), channel_id=1, source_target_pairs={{2,4},{3,5},{6,8},{7,9},{10,12},{11,13},{14,0},{15,1},{4,2},{5,3},... | collective-permute-start | bytes 786440 | tf_op jit(solution)/shard_map/ppermute | solution.py:351
  93.4 0.0 collective-permute-done.11.got_ref
  93.4 2.8 %collective-permute-start.12 = (bf16[512,256]{1,0:T(8,128)(2,1)S(1)}, bf16[512,256]{1,0:T(8,128)(2,1)S(1)}, u32[]{:S(2)}, u32[]{:S(2)}) collective-permute-start(bf16[512,256]{1,0:T(8,128)(2,1)S(1)} %shard_map.79), channel_id=1, source_target_pairs={{0,2},{1,3},{4,6},{5,7},{8,10},{9,11},{12,14},{13,15},{2,0},{3,1},... | collective-permute-start | bytes 786440 | tf_op jit(solution)/shard_map/ppermute | solution.py:351
  96.2 3.0 %collective-permute-done.10.got_ref = bf16[512,256]{1,0:T(8,128)(2,1)S(1)} collective-permute-done((bf16[512,256]{1,0:T(8,128)(2,1)S(1)}, bf16[512,256]{1,0:T(8,128)(2,1)S(1)}, u32[]{:S(2)}, u32[]{:S(2)}) %collective-permute-start.10) | collective-permute-done | bytes 262176 | tf_op jit(solution)/shard_map/ppermute | solution.py:351
  99.3 2.4 %collective-permute-done.12.got_ref = bf16[512,256]{1,0:T(8,128)(2,1)S(1)} collective-permute-done((bf16[512,256]{1,0:T(8,128)(2,1)S(1)}, bf16[512,256]{1,0:T(8,128)(2,1)S(1)}, u32[]{:S(2)}, u32[]{:S(2)}) %collective-permute-start.12) | collective-permute-done | bytes 262176 | tf_op jit(solution)/shard_map/ppermute | solution.py:351
  101.7 0.7 shard_map.81
  (3 shorter events, 0.1 us)
Async XLA Ops:
  0.0 30.7 %copy-start.1 = (bf16[2,512,256]{2,1,0:T(8,128)(2,1)S(1)}, bf16[2,512,256]{2,1,0:T(8,128)(2,1)}, u32[]{:S(2)}) copy-start(bf16[2,512,256]{2,1,0:T(8,128)(2,1)} %v_ref.1) | copy-start | bytes 1572868
  0.0 30.7 %copy-start = (bf16[2,512,256]{2,1,0:T(8,128)(2,1)S(1)}, bf16[2,512,256]{2,1,0:T(8,128)(2,1)}, u32[]{:S(2)}) copy-start(bf16[2,512,256]{2,1,0:T(8,128)(2,1)} %k_ref.1) | copy-start | bytes 1572868
  0.0 30.7 %copy-start.3 = (bf16[512,256]{1,0:T(8,128)(2,1)S(1)}, bf16[512,256]{1,0:T(8,128)(2,1)}, u32[]{:S(2)}) copy-start(bf16[512,256]{1,0:T(8,128)(2,1)} %g_ref.1) | copy-start | bytes 786436
  0.0 30.7 %copy-start.2 = (bf16[512,256]{1,0:T(8,128)(2,1)S(1)}, bf16[512,256]{1,0:T(8,128)(2,1)}, u32[]{:S(2)}) copy-start(bf16[512,256]{1,0:T(8,128)(2,1)} %q_ref.1) | copy-start | bytes 786436
  0.0 39.5 %collective-permute-start.2 = (bf16[256,4096]{1,0:T(8,128)(2,1)}, bf16[256,4096]{1,0:T(8,128)(2,1)}, u32[]{:S(2)}, u32[]{:S(2)}) collective-permute-start(bf16[256,4096]{1,0:T(8,128)(2,1)} %w_ref.1), channel_id=1, source_target_pairs={{0,1},{1,0},{2,3},{3,2},{4,5},{5,4},{6,7},{7,6},{8,9},{9,8},{10,11... | collective-permute-start | bytes 6291464 | tf_op jit(solution)/shard_map/ppermute | solution.py:354
  28.9 4.3 %collective-permute-start = (bf16[2,128,256]{2,1,0:T(8,128)(2,1)S(1)}, bf16[2,128,256]{2,1,0:T(8,128)(2,1)S(1)}, u32[]{:S(2)}, u32[]{:S(2)}) collective-permute-start(bf16[2,128,256]{2,1,0:T(8,128)(2,1)S(1)} %get-tuple-element.32), channel_id=1, source_target_pairs={{0,64},{64,128},{128,192},{192,256},{256,320},{320,384},{384,448},... | collective-permute-start | bytes 393224 | tf_op jit(solution)/shard_map/ppermute | solution.py:358
  33.4 8.7 %collective-permute-start.1 = (bf16[2,128,256]{2,1,0:T(8,128)(2,1)S(1)}, bf16[2,128,256]{2,1,0:T(8,128)(2,1)S(1)}, u32[]{:S(2)}, u32[]{:S(2)}) collective-permute-start(bf16[2,128,256]{2,1,0:T(8,128)(2,1)S(1)} %get-tuple-element.40), channel_id=1, source_target_pairs={{0,128},{64,192},{128,256},{192,320},{256,384},{320,448},{1,129},{... | collective-permute-start | bytes 393224 | tf_op jit(solution)/shard_map/ppermute | solution.py:358
  42.2 14.5 %collective-permute-start.3 = (bf16[2,128,128]{2,1,0:T(8,128)(2,1)S(1)}, bf16[2,128,128]{2,1,0:T(8,128)(2,1)S(1)}, u32[]{:S(2)}, u32[]{:S(2)}) collective-permute-start(bf16[2,128,128]{2,1,0:T(8,128)(2,1)S(1)} %shard_map.70), channel_id=1, source_target_pairs={{0,256},{64,320},{128,384},{192,448},{1,257},{65,321},{129,385},{1... | collective-permute-start | bytes 196616 | tf_op jit(solution)/shard_map/ppermute | solution.py:358
  57.3 3.4 %collective-permute-start.4 = (bf16[512,256]{1,0:T(8,128)(2,1)S(1)}, bf16[512,256]{1,0:T(8,128)(2,1)S(1)}, u32[]{:S(2)}, u32[]{:S(2)}) collective-permute-start(bf16[512,256]{1,0:T(8,128)(2,1)S(1)} %shard_map.71.a_ref), channel_id=1, source_target_pairs={{0,1},{1,0},{2,3},{3,2},{4,5},{5,4},{6,7},{7,6},{8,9},{9,8},{10,11... | collective-permute-start | bytes 786440 | tf_op jit(solution)/shard_map/ppermute | solution.py:354
  61.0 8.7 %collective-permute-start.6 = (bf16[256,256]{1,0:T(8,128)(2,1)S(1)}, bf16[256,256]{1,0:T(8,128)(2,1)S(1)}, u32[]{:S(2)}, u32[]{:S(2)}) collective-permute-start(bf16[256,256]{1,0:T(8,128)(2,1)S(1)} %get-tuple-element.47), channel_id=1, source_target_pairs={{0,2},{1,3},{4,6},{5,7},{8,10},{9,11},{12,14},{13,15},{2,0},{3,1},... | collective-permute-start | bytes 393224 | tf_op jit(solution)/shard_map/ppermute | solution.py:351
  64.5 9.6 %collective-permute-start.5 = (bf16[256,256]{1,0:T(8,128)(2,1)S(1)}, bf16[256,256]{1,0:T(8,128)(2,1)S(1)}, u32[]{:S(2)}, u32[]{:S(2)}) collective-permute-start(bf16[256,256]{1,0:T(8,128)(2,1)S(1)} %get-tuple-element.46), channel_id=1, source_target_pairs={{2,4},{3,5},{6,8},{7,9},{10,12},{11,13},{14,0},{15,1},{4,2},{5,3},... | collective-permute-start | bytes 393224 | tf_op jit(solution)/shard_map/ppermute | solution.py:351
  70.0 10.9 %collective-permute-start.7 = (bf16[512,256]{1,0:T(8,128)(2,1)S(1)}, bf16[512,256]{1,0:T(8,128)(2,1)S(1)}, u32[]{:S(2)}, u32[]{:S(2)}) collective-permute-start(bf16[512,256]{1,0:T(8,128)(2,1)S(1)} %shard_map.73), channel_id=1, source_target_pairs={{2,4},{3,5},{6,8},{7,9},{10,12},{11,13},{14,0},{15,1},{4,2},{5,3},... | collective-permute-start | bytes 786440 | tf_op jit(solution)/shard_map/ppermute | solution.py:351
  74.4 9.1 %collective-permute-start.9 = (bf16[512,256]{1,0:T(8,128)(2,1)S(1)}, bf16[512,256]{1,0:T(8,128)(2,1)S(1)}, u32[]{:S(2)}, u32[]{:S(2)}) collective-permute-start(bf16[512,256]{1,0:T(8,128)(2,1)S(1)} %shard_map.74), channel_id=1, source_target_pairs={{0,2},{1,3},{4,6},{5,7},{8,10},{9,11},{12,14},{13,15},{2,0},{3,1},... | collective-permute-start | bytes 786440 | tf_op jit(solution)/shard_map/ppermute | solution.py:351
  80.9 8.8 %collective-permute-start.8 = (bf16[512,256]{1,0:T(8,128)(2,1)S(1)}, bf16[512,256]{1,0:T(8,128)(2,1)S(1)}, u32[]{:S(2)}, u32[]{:S(2)}) collective-permute-start(bf16[512,256]{1,0:T(8,128)(2,1)S(1)} %shard_map.76), channel_id=1, source_target_pairs={{0,2},{1,3},{4,6},{5,7},{8,10},{9,11},{12,14},{13,15},{2,0},{3,1},... | collective-permute-start | bytes 786440 | tf_op jit(solution)/shard_map/ppermute | solution.py:351
  83.6 9.7 %collective-permute-start.11 = (bf16[512,256]{1,0:T(8,128)(2,1)S(1)}, bf16[512,256]{1,0:T(8,128)(2,1)S(1)}, u32[]{:S(2)}, u32[]{:S(2)}) collective-permute-start(bf16[512,256]{1,0:T(8,128)(2,1)S(1)} %shard_map.77), channel_id=1, source_target_pairs={{2,4},{3,5},{6,8},{7,9},{10,12},{11,13},{14,0},{15,1},{4,2},{5,3},... | collective-permute-start | bytes 786440 | tf_op jit(solution)/shard_map/ppermute | solution.py:351
  89.8 9.5 %collective-permute-start.10 = (bf16[512,256]{1,0:T(8,128)(2,1)S(1)}, bf16[512,256]{1,0:T(8,128)(2,1)S(1)}, u32[]{:S(2)}, u32[]{:S(2)}) collective-permute-start(bf16[512,256]{1,0:T(8,128)(2,1)S(1)} %shard_map.78), channel_id=1, source_target_pairs={{2,4},{3,5},{6,8},{7,9},{10,12},{11,13},{14,0},{15,1},{4,2},{5,3},... | collective-permute-start | bytes 786440 | tf_op jit(solution)/shard_map/ppermute | solution.py:351
  93.4 8.3 %collective-permute-start.12 = (bf16[512,256]{1,0:T(8,128)(2,1)S(1)}, bf16[512,256]{1,0:T(8,128)(2,1)S(1)}, u32[]{:S(2)}, u32[]{:S(2)}) collective-permute-start(bf16[512,256]{1,0:T(8,128)(2,1)S(1)} %shard_map.79), channel_id=1, source_target_pairs={{0,2},{1,3},{4,6},{5,7},{8,10},{9,11},{12,14},{13,15},{2,0},{3,1},... | collective-permute-start | bytes 786440 | tf_op jit(solution)/shard_map/ppermute | solution.py:351

commit v6 on v5

--- a/solution.py
+++ b/solution.py
@@ -55,14 +55,18 @@
 
 
 def map_kernel(
-    group, k_hbm, v_hbm, b_hbm, ab_ref, x_ref, e_ref, pre_ref, k_ref, v_ref, b_ref, lev_ref, p_ref, sems
+    group, k_hbm, v_hbm, b_hbm, ab_ref, x_ref, e_ref, a_ref, c_ref, k_ref, v_ref, b_ref, lev_ref, sems
 ):
-    get_k = pltpu.make_async_copy(k_hbm, k_ref, sems.at[0])
-    get_v = pltpu.make_async_copy(v_hbm, v_ref, sems.at[1])
-    get_b = pltpu.make_async_copy(b_hbm, b_ref, sems.at[2])
-    get_k.start()
-    get_b.start()
-    get_v.start()
+    copies = [pltpu.make_async_copy(b_hbm, b_ref, sems.at[0])]
+    piece = k_ref.shape[1] // 4
+    for source, target in ((k_hbm, k_ref), (v_hbm, v_ref)):
+        for j in range(2):
+            for i in range(4):
+                part = (j, slice(i * piece, (i + 1) * piece))
+                at = sems.at[len(copies)]
+                copies.append(pltpu.make_async_copy(source.at[part], target.at[part], at))
+    for copy in copies:
+        copy.start()
     heads = k_ref.shape[2] // HD
     blocks = k_ref.shape[1] // SPAN
     sub = 2 * SPAN
@@ -75,12 +79,10 @@
         level = level + (apart >= 2**bit).astype(jnp.int32)
     lev_ref[...] = jnp.where(s_r > s_c, level, -1)
     eye = (place_r == place_c).astype(F32)
-    for h in range(heads):
-        p_ref[h] = jnp.concatenate([eye, jnp.zeros((HD, HD), F32)], axis=1)
-    get_b.wait()
-    get_k.wait()
-    get_v.wait()
-
+    for copy in copies:
+        copy.wait()
+
+    blocks_of = [[] for _ in range(heads)]
     for step in range(blocks // group):
         probs = [(step * group + i, h) for i in range(group) for h in range(heads)]
         kb = [read_block(k_ref, blk, h) for blk, h in probs]
@@ -123,13 +125,26 @@
             B.append(dot(wide(y * n[i]), square(read_block(v_ref, blk, h))))
         for i in num:
             blk, h = probs[i]
-            p = p_ref[h]
-            ph, plo = split(p)
-            pre_ref[h * blocks + blk] = ph
-            new = dot(A[i], square(ph)) + dot(A[i][:, :HD], plo)
-            p_ref[h] = new + jnp.concatenate([jnp.zeros((HD, HD), F32), B[i]], axis=1)
+            a_ref[h * blocks + blk] = A[i]
+            c_ref[h * blocks + blk] = B[i]
+            blocks_of[h].append((A[i], B[i]))
+
+    while len(blocks_of[0]) > 1:
+        blocks_of = [
+            [joined(maps[i + 1], maps[i]) for i in range(0, len(maps), 2)] for maps in blocks_of
+        ]
     for h in range(heads):
-        ab_ref[h] = p_ref[h].astype(BF16)
+        a, c = blocks_of[h][0]
+        ab_ref[h] = jnp.concatenate([a[:, :HD], c.astype(BF16)], axis=1)
+
+
+def joined(later, earlier):
+    left, source = later
+    b_hi, b_lo = split(earlier[1])
+    hi = jnp.concatenate([earlier[0][:, :HD], b_hi], axis=1)
+    lo = jnp.concatenate([earlier[0][:, HD:], b_lo], axis=1)
+    new = dot(left, square(hi)) + dot(left[:, :HD], lo)
+    return wide(new[:, :HD]), new[:, HD:] + source
 
 
 def local_maps(k, v, betas, group):
@@ -143,22 +158,22 @@
             jax.ShapeDtypeStruct((count, 2 * SPAN, 4 * SPAN), BF16),
             jax.ShapeDtypeStruct((count, 2, 2 * SPAN), F32),
             jax.ShapeDtypeStruct((count, HD, 2 * HD), BF16),
+            jax.ShapeDtypeStruct((count, HD, HD), F32),
         ),
         in_specs=[pl.BlockSpec(memory_space=pltpu.HBM)] * 3,
-        out_specs=[pl.BlockSpec(memory_space=pltpu.VMEM)] * 4,
+        out_specs=[pl.BlockSpec(memory_space=pltpu.VMEM)] * 5,
         scratch_shapes=[
             pltpu.VMEM(k.shape, k.dtype),
             pltpu.VMEM(v.shape, v.dtype),
             pltpu.VMEM(betas.shape, betas.dtype),
             pltpu.VMEM((2 * SPAN, 2 * SPAN), jnp.int32),
-            pltpu.VMEM((heads, HD, 2 * HD), F32),
-            pltpu.SemaphoreType.DMA((3,)),
+            pltpu.SemaphoreType.DMA((17,)),
         ],
         compiler_params=pltpu.CompilerParams(vmem_limit_bytes=16 * 1024 * 1024),
     )(*(pltpu.with_memory_space_constraint(a, pltpu.HBM) for a in (k, v, betas)))
 
 
-def local_kernel(q_ref, k_ref, v_ref, g_ref, x_ref, e_ref, pre_ref, l_ref, m_ref, s_ref):
+def local_kernel(q_ref, k_ref, v_ref, g_ref, x_ref, e_ref, a_ref, c_ref, l_ref, m_ref, s_ref):
     heads = q_ref.shape[1] // HD
     blocks = q_ref.shape[0] // SPAN
     sub = 2 * SPAN
@@ -185,7 +200,19 @@
         dot(wide(zq[i] * e_ref[spots[i][0], 1:]), square(read_block(v_ref, i // heads, i % heads)))
         for i in num
     ]
-    prod = [dot(carry[i], pre_ref[spots[i][0]]) for i in num]
+    prefix = {}
+    r = lax.broadcasted_iota(jnp.int32, (HD, 2 * HD), 0)
+    c = lax.broadcasted_iota(jnp.int32, (HD, 2 * HD), 1)
+    state = [(r == c).astype(F32)] * heads
+    for i in num:
+        at, h = spots[i][0], i % heads
+        hi, lo = split(state[h])
+        prefix[i] = hi
+        if i < len(spots) - heads:
+            left = a_ref[at]
+            new = dot(left, square(hi)) + dot(left[:, :HD], lo)
+            state[h] = jnp.concatenate([new[:, :HD], new[:, HD:] + c_ref[at]], axis=1)
+    prod = [dot(carry[i], prefix[i]) for i in num]
     for i, (_, rows, cols) in enumerate(spots):
         qf = q_ref[rows, cols].astype(F32)
         unit = lax.rsqrt(jnp.sum(qf * qf, axis=1, keepdims=True) + 1e-6)
@@ -306,22 +333,13 @@
     return dot(a, w[:rows]) + dot(b, w[rows:])
 
 
-def far_kernel(me_ref, a_ref, b_ref, w_ref, ahead_ref, back_ref):
-    odd = (me_ref[0] // 2) % 2 != 0
-    out = term(a_ref[...], b_ref[...], w_ref[0]).astype(BF16)
-    cut = ahead_ref.shape[0]
-    ahead_ref[...] = jnp.where(odd, out[cut:], out[:cut])
-    back_ref[...] = jnp.where(odd, out[:cut], out[cut:])
-
-
-def hop_kernel(at, side, me_ref, a_ref, b_ref, w_ref, got_ref, o_ref):
-    odd = (me_ref[0] // 2) % 2
+def term_kernel(at, a_ref, b_ref, w_ref, o_ref):
+    o_ref[...] = term(a_ref[...], b_ref[...], w_ref[at]).astype(BF16)
+
+
+def hop_kernel(at, a_ref, b_ref, w_ref, got_ref, o_ref):
     out = term(a_ref[...], b_ref[...], w_ref[at])
-    cut = got_ref.shape[0]
-    for i in range(2):
-        rows = slice(i * cut, (i + 1) * cut)
-        got = jnp.where((odd + side) % 2 == i, got_ref[...].astype(F32), 0.0)
-        o_ref[rows] = (out[rows] + got).astype(BF16)
+    o_ref[...] = (out + got_ref[...].astype(F32)).astype(BF16)
 
 
 def rest_kernel(picks, a_ref, b_ref, w_ref, o_ref):
@@ -358,7 +376,7 @@
         return lax.ppermute(a, "ctx_0", [(i, i + by) for i in range(groups - by)])
 
     mate_weight = mate(out_weight)
-    maps, inverse, scales, prefixes = local_maps(keys, values, betas, 8)
+    maps, inverse, scales, lefts, sources = local_maps(keys, values, betas, 8)
 
     wide_map = jax.ShapeDtypeStruct((heads, HD, 2 * HD), F32)
     wide_send = jax.ShapeDtypeStruct((heads, HD, 2 * HD), BF16)
@@ -379,7 +397,8 @@
         gate,
         inverse,
         scales,
-        lax.optimization_barrier((prefixes, total))[0],
+        lax.optimization_barrier((lefts, total))[0],
+        sources,
     )
     near = lax.optimization_barrier((near, silu))[0]
     send, pair = small(join_kernel, (wide_send, wide_map), total, near)
@@ -403,36 +422,32 @@
 
     half = chips // 2
     sent = jax.ShapeDtypeStruct((tok, cols), BF16)
-    part = jax.ShapeDtypeStruct((tok // 2, cols), BF16)
     both = (mixed_in, mate_in, ring_w)
-    ahead, back = small(far_kernel, (part, part), place, *both, specs=[SM] + [VM] * 3)
-    got, prior, terms = (across(back, 1), across(ahead, 0)), None, None
-    for k in range(half - 1, 0, -1):
+    far = small(functools.partial(term_kernel, 0), sent, *both)
+    came = across(far, 0)
+    late_in = lax.optimization_barrier((mixed_in, far))[0]
+    third = small(functools.partial(term_kernel, 1), sent, late_in, mate_in, ring_w)
+    came = lax.optimization_barrier((came, third))[0]
+    prior = small(functools.partial(hop_kernel, half), sent, *both, came)
+    got = (across(prior, 1), across(third, 0))
+    picks = [j + i * (half - 1) for j in range(2, half) for i in range(2)] + [chips - 1]
+    terms = small(
+        functools.partial(rest_kernel, picks),
+        jax.ShapeDtypeStruct((len(picks), tok, cols), F32),
+        lax.optimization_barrier((mixed_in, prior))[0],
+        mate_in,
+        ring_w,
+    )
+    for k in range(half - 2, 0, -1):
         sums = [None, None]
-        for i in (1, 0) if k % 2 else (0, 1):
-            came = got[i]
-            if prior is not None:
-                came = lax.optimization_barrier((came, prior))[0]
-            if k == half - 1:
-                body = functools.partial(hop_kernel, 1 + i * (half - 1), i)
-                sums[i] = small(body, sent, place, *both, came, specs=[SM] + [VM] * 4)
-            else:
-                body = functools.partial(add_kernel, 2 * (half - 2 - k) + i)
-                sums[i] = small(body, sent, terms, came)
-            prior = sums[i]
-        if k == half - 1:
-            picks = [j + i * (half - 1) for j in range(2, half) for i in range(2)] + [chips - 1]
-            terms = small(
-                functools.partial(rest_kernel, picks),
-                jax.ShapeDtypeStruct((len(picks), tok, cols), F32),
-                lax.optimization_barrier((mixed_in, prior))[0],
-                mate_in,
-                ring_w,
-            )
+        for i in (0, 1) if k % 2 else (1, 0):
+            came = lax.optimization_barrier((got[i], prior))[0]
+            body = functools.partial(add_kernel, 2 * (half - 2 - k) + i)
+            sums[i] = prior = small(body, sent, terms, came)
         got = (across(sums[1], 1), across(sums[0], 0))
-    came = lax.optimization_barrier((got[0], prior))[0]
+    came = lax.optimization_barrier((got[1], prior))[0]
     total = small(functools.partial(add_kernel, 2 * half - 4), tokens, terms, came)
-    return small(last_kernel, sent, total, got[1])
+    return small(last_kernel, sent, total, got[0])
 
 
 def solution(mesh):

time: 103 us -> 103 us (level)
  starting transfers between devices: 51.4 us -> 46.7 us
  waiting for transfers between devices: 16.8 us -> 21.3 us
    ppermute x8 -> x7, waiting for transfers between devices: 12 us -> 17.6 us  [across(): lax.ppermute(a, 'head', [(2 * c + i, 2 * d + i) for c, d in both for i in...]
    ppermute x8 -> x7, starting transfers between devices: 26.9 us -> 22.3 us  [across(): lax.ppermute(a, 'head', [(2 * c + i, 2 * d + i) for c, d in both for i in...]
    pallas_call x16, Pallas kernels: 6.03 us -> 7.21 us  [small(): pl.pallas_call(kernel, out_shape=outs, in_specs=specs or [VM] * len(args)...]
    ppermute x3, waiting for transfers between devices: 3.27 us -> 2.18 us  [later_z(): return lax.ppermute(a, 'ctx_0', [(i, i + by) for i in range(groups - by)])]
  transfers between devices with their start and end apart: 13 -> 12, of which waited for: 9 -> 8; matrix products, arithmetic and copies ran while one was open for 0% -> 0% of each run, Pallas kernels for 16% -> 16%
where the time goes in v6:
time: 103 us
  starting transfers between devices  46.7 us (45%)
  waiting for transfers between devices  21.3 us (21%)
  Pallas kernels  18.6 us (18%)
  blocking collectives  15.9 us (15%)
    ppermute x7, starting transfers between devices, across(): lax.ppermute(a, 'head', [(2 * c + i, 2 * d + i) for c, d in both for i in...  22.3 us
    ppermute x3, starting transfers between devices, later_z(): return lax.ppermute(a, 'ctx_0', [(i, i + by) for i in range(groups - by)])  20.4 us
    ppermute x7, waiting for transfers between devices, across(): lax.ppermute(a, 'head', [(2 * c + i, 2 * d + i) for c, d in both for i in...  17.6 us
    all_gather x1, blocking collectives, per_device(): gathered = lax.all_gather(maps, 'ctx_1')  15.9 us
    pallas_call x1, Pallas kernels, local_maps(): pl.pallas_call(functools.partial(map_kernel, group), out_shape=(jax.Shape...  9.55 us
    pallas_call x16, Pallas kernels, small(): pl.pallas_call(kernel, out_shape=outs, in_specs=specs or [VM] * len(args)...  7.21 us
    ppermute x2, starting transfers between devices, mate(): return lax.ppermute(a, 'head', [(i, i ^ 1) for i in range(devices)])  3.98 us
    ppermute x3, waiting for transfers between devices, later_z(): return lax.ppermute(a, 'ctx_0', [(i, i + by) for i in range(groups - by)])  2.18 us
  transfers between devices with their start and end apart: 12, of which 8 were waited for; matrix products, arithmetic and copies ran while one was open for 0% of the time, Pallas kernels for 16%

profile of v6, /device:TPU:6, one launch (start us, length us, event | category | flops | bytes accessed | tf_op | source)
XLA Modules:
  0.0 102.8 jit_solution(4819366564880183117)
XLA Ops:
  0.0 0.0 copy-start
  0.0 0.0 copy-start.1
  0.0 0.0 copy-start.2
  0.0 0.0 copy-start.3
  0.0 2.1 %collective-permute-start.2 = (bf16[256,4096]{1,0:T(8,128)(2,1)}, bf16[256,4096]{1,0:T(8,128)(2,1)}, u32[]{:S(2)}, u32[]{:S(2)}) collective-permute-start(bf16[256,4096]{1,0:T(8,128)(2,1)} %w_ref.1), channel_id=1, source_target_pairs={{0,1},{1,0},{2,3},{3,2},{4,5},{5,4},{6,7},{7,6},{8,9},{9,8},{10,11... | collective-permute-start | bytes 6291464 | tf_op jit(solution)/shard_map/ppermute | solution.py:372
  2.1 9.5 %shard_map.64 = (bf16[2,128,256]{2,1,0:T(8,128)(2,1)S(1)}, bf16[16,128,256]{2,1,0:T(8,128)(2,1)S(1)}, f32[16,2,128]{2,1,0:T(2,128)S(1)}, bf16[16,128,256]{2,1,0:T(8,128)(2,1)S(1)}, f32[16,128,128]{2,1,0:T(8,128)S(1)}) custom-call(bf16[2,512,256]{2,1,0:T(8,128)(2,1)} %k_ref.1, bf16[2,512,256]{2,1,0:T(8,128)(2,1)} %v_ref.1, f32[2,2,512]{2,1,0:T(2,128)} %b_hbm.1), custom_call_target="tpu_custom_call" | custom-call | tf_op jit(solution)/shard_map/pallas_call | solution.py:154
  11.6 15.9 %all-gather = bf16[8,128,256]{2,1,0:T(8,128)(2,1)S(1)} all-gather(bf16[2,128,256]{2,1,0:T(8,128)(2,1)S(1)} %get-tuple-element.30), channel_id=2, replica_groups=mesh['ctx_0'=8,'ctx_1'=4,'head'=16] {'ctx_1'}, dimensions={0}, use_global_device_ids=true | all-gather | bytes 655360 | tf_op jit(solution)/shard_map/all_gather | solution.py:385
  27.6 0.6 shard_map.65
  28.2 1.8 %collective-permute-start = (bf16[2,128,256]{2,1,0:T(8,128)(2,1)S(1)}, bf16[2,128,256]{2,1,0:T(8,128)(2,1)S(1)}, u32[]{:S(2)}, u32[]{:S(2)}) collective-permute-start(bf16[2,128,256]{2,1,0:T(8,128)(2,1)S(1)} %get-tuple-element.32), channel_id=1, source_target_pairs={{0,64},{64,128},{128,192},{192,256},{256,320},{320,384},{384,448},... | collective-permute-start | bytes 393224 | tf_op jit(solution)/shard_map/ppermute | solution.py:376
  30.0 0.0 copy-done
  30.0 0.0 copy-done.1
  30.0 0.0 copy-done.2
  30.0 0.0 copy-done.3
  30.1 2.6 %shard_map.66 = (f32[512,256]{1,0:T(8,128)S(1)}, bf16[512,256]{1,0:T(8,128)(2,1)S(1)}, f32[512,256]{1,0:T(8,128)S(1)}) custom-call(bf16[512,256]{1,0:T(8,128)(2,1)S(1)} %copy-done.2, bf16[2,512,256]{2,1,0:T(8,128)(2,1)S(1)} %copy-done, bf16[2,512,256]{2,1,0:T(8,128)(2,1)S(1)} %copy-done.1, bf16[512,256]{1,0:T(8,128)(2,1)S(1)} %copy-done.3, ...), custom_call_target="tpu_custom_call" | custom-call | tf_op jit(solution)/shard_map/pallas_call | solution.py:292
  32.7 0.0 collective-permute-done.earlier_ref.near_ref
  32.7 0.2 shard_map.67
  32.9 6.1 %collective-permute-start.1 = (bf16[2,128,256]{2,1,0:T(8,128)(2,1)S(1)}, bf16[2,128,256]{2,1,0:T(8,128)(2,1)S(1)}, u32[]{:S(2)}, u32[]{:S(2)}) collective-permute-start(bf16[2,128,256]{2,1,0:T(8,128)(2,1)S(1)} %get-tuple-element.41), channel_id=1, source_target_pairs={{0,128},{64,192},{128,256},{192,320},{256,384},{320,448},{1,129},{... | collective-permute-start | bytes 393224 | tf_op jit(solution)/shard_map/ppermute | solution.py:376
  39.0 0.0 collective-permute-done.2.x_ref
  39.0 1.8 %shard_map.68.w_ref = bf16[8,512,256]{2,1,0:T(8,128)(2,1)S(1)} custom-call(s32[1]{0:T(128)} %bitcast.2.me_ref, bf16[256,4096]{1,0:T(8,128)(2,1)} %w_ref.1, bf16[256,4096]{1,0:T(8,128)(2,1)} %collective-permute-done.2.x_ref), custom_call_target="tpu_custom_call" | custom-call | tf_op jit(solution)/shard_map/pallas_call | solution.py:321
  40.8 0.7 collective-permute-done.1.far_ref.earlier_ref
  41.5 0.2 shard_map.70
  41.7 12.5 %collective-permute-start.3 = (bf16[2,128,128]{2,1,0:T(8,128)(2,1)S(1)}, bf16[2,128,128]{2,1,0:T(8,128)(2,1)S(1)}, u32[]{:S(2)}, u32[]{:S(2)}) collective-permute-start(bf16[2,128,128]{2,1,0:T(8,128)(2,1)S(1)} %shard_map.70), channel_id=1, source_target_pairs={{0,256},{64,320},{128,384},{192,448},{1,257},{65,321},{129,385},{1... | collective-permute-start | bytes 196616 | tf_op jit(solution)/shard_map/ppermute | solution.py:376
  54.2 0.4 shard_map.69.entry_ref
  54.6 1.5 %collective-permute-done.3.state_ref = bf16[2,128,128]{2,1,0:T(8,128)(2,1)S(1)} collective-permute-done((bf16[2,128,128]{2,1,0:T(8,128)(2,1)S(1)}, bf16[2,128,128]{2,1,0:T(8,128)(2,1)S(1)}, u32[]{:S(2)}, u32[]{:S(2)}) %collective-permute-start.3) | collective-permute-done | bytes 65568 | tf_op jit(solution)/shard_map/ppermute | solution.py:376
  56.1 0.5 shard_map.71.a_ref
  56.6 1.9 %collective-permute-start.4 = (bf16[512,256]{1,0:T(8,128)(2,1)S(1)}, bf16[512,256]{1,0:T(8,128)(2,1)S(1)}, u32[]{:S(2)}, u32[]{:S(2)}) collective-permute-start(bf16[512,256]{1,0:T(8,128)(2,1)S(1)} %shard_map.71.a_ref), channel_id=1, source_target_pairs={{0,1},{1,0},{2,3},{3,2},{4,5},{5,4},{6,7},{7,6},{8,9},{9,8},{10,11... | collective-permute-start | bytes 786440 | tf_op jit(solution)/shard_map/ppermute | solution.py:372
  58.5 1.5 %collective-permute-done.4.b_ref = bf16[512,256]{1,0:T(8,128)(2,1)S(1)} collective-permute-done((bf16[512,256]{1,0:T(8,128)(2,1)S(1)}, bf16[512,256]{1,0:T(8,128)(2,1)S(1)}, u32[]{:S(2)}, u32[]{:S(2)}) %collective-permute-start.4) | collective-permute-done | bytes 262176 | tf_op jit(solution)/shard_map/ppermute | solution.py:372
  60.0 0.3 shard_map.72
  60.3 3.5 %collective-permute-start.5 = (bf16[512,256]{1,0:T(8,128)(2,1)S(1)}, bf16[512,256]{1,0:T(8,128)(2,1)S(1)}, u32[]{:S(2)}, u32[]{:S(2)}) collective-permute-start(bf16[512,256]{1,0:T(8,128)(2,1)S(1)} %shard_map.72), channel_id=1, source_target_pairs={{0,2},{1,3},{4,6},{5,7},{8,10},{9,11},{12,14},{13,15},{2,0},{3,1},... | collective-permute-start | bytes 786440 | tf_op jit(solution)/shard_map/ppermute | solution.py:369
  63.8 0.3 shard_map.73
  64.1 2.4 %collective-permute-start.6 = (bf16[512,256]{1,0:T(8,128)(2,1)S(1)}, bf16[512,256]{1,0:T(8,128)(2,1)S(1)}, u32[]{:S(2)}, u32[]{:S(2)}) collective-permute-start(bf16[512,256]{1,0:T(8,128)(2,1)S(1)} %shard_map.73), channel_id=1, source_target_pairs={{0,2},{1,3},{4,6},{5,7},{8,10},{9,11},{12,14},{13,15},{2,0},{3,1},... | collective-permute-start | bytes 786440 | tf_op jit(solution)/shard_map/ppermute | solution.py:369
  66.5 4.9 %collective-permute-done.5.got_ref = bf16[512,256]{1,0:T(8,128)(2,1)S(1)} collective-permute-done((bf16[512,256]{1,0:T(8,128)(2,1)S(1)}, bf16[512,256]{1,0:T(8,128)(2,1)S(1)}, u32[]{:S(2)}, u32[]{:S(2)}) %collective-permute-start.5) | collective-permute-done | bytes 262176 | tf_op jit(solution)/shard_map/ppermute | solution.py:369
  71.4 0.3 shard_map.74
  71.7 5.4 %collective-permute-start.8 = (bf16[512,256]{1,0:T(8,128)(2,1)S(1)}, bf16[512,256]{1,0:T(8,128)(2,1)S(1)}, u32[]{:S(2)}, u32[]{:S(2)}) collective-permute-start(bf16[512,256]{1,0:T(8,128)(2,1)S(1)} %shard_map.74), channel_id=1, source_target_pairs={{2,4},{3,5},{6,8},{7,9},{10,12},{11,13},{14,0},{15,1},{4,2},{5,3},... | collective-permute-start | bytes 786440 | tf_op jit(solution)/shard_map/ppermute | solution.py:369
  77.0 0.0 collective-permute-done.6.got_ref
  77.1 0.8 shard_map.75.terms_ref
  78.0 4.5 %collective-permute-start.7 = (bf16[512,256]{1,0:T(8,128)(2,1)S(1)}, bf16[512,256]{1,0:T(8,128)(2,1)S(1)}, u32[]{:S(2)}, u32[]{:S(2)}) collective-permute-start(bf16[512,256]{1,0:T(8,128)(2,1)S(1)} %shard_map.76), channel_id=1, source_target_pairs={{2,4},{3,5},{6,8},{7,9},{10,12},{11,13},{14,0},{15,1},{4,2},{5,3},... | collective-permute-start | bytes 786440 | tf_op jit(solution)/shard_map/ppermute | solution.py:369
  82.5 0.0 collective-permute-done.8.got_ref
  82.5 1.9 %collective-permute-start.10 = (bf16[512,256]{1,0:T(8,128)(2,1)S(1)}, bf16[512,256]{1,0:T(8,128)(2,1)S(1)}, u32[]{:S(2)}, u32[]{:S(2)}) collective-permute-start(bf16[512,256]{1,0:T(8,128)(2,1)S(1)} %shard_map.77), channel_id=1, source_target_pairs={{0,2},{1,3},{4,6},{5,7},{8,10},{9,11},{12,14},{13,15},{2,0},{3,1},... | collective-permute-start | bytes 786440 | tf_op jit(solution)/shard_map/ppermute | solution.py:369
  84.5 3.8 %collective-permute-done.7.got_ref = bf16[512,256]{1,0:T(8,128)(2,1)S(1)} collective-permute-done((bf16[512,256]{1,0:T(8,128)(2,1)S(1)}, bf16[512,256]{1,0:T(8,128)(2,1)S(1)}, u32[]{:S(2)}, u32[]{:S(2)}) %collective-permute-start.7) | collective-permute-done | bytes 262176 | tf_op jit(solution)/shard_map/ppermute | solution.py:369
  88.3 1.9 %collective-permute-start.9 = (bf16[512,256]{1,0:T(8,128)(2,1)S(1)}, bf16[512,256]{1,0:T(8,128)(2,1)S(1)}, u32[]{:S(2)}, u32[]{:S(2)}) collective-permute-start(bf16[512,256]{1,0:T(8,128)(2,1)S(1)} %shard_map.78), channel_id=1, source_target_pairs={{0,2},{1,3},{4,6},{5,7},{8,10},{9,11},{12,14},{13,15},{2,0},{3,1},... | collective-permute-start | bytes 786440 | tf_op jit(solution)/shard_map/ppermute | solution.py:369
  90.2 2.3 %collective-permute-done.10.got_ref = bf16[512,256]{1,0:T(8,128)(2,1)S(1)} collective-permute-done((bf16[512,256]{1,0:T(8,128)(2,1)S(1)}, bf16[512,256]{1,0:T(8,128)(2,1)S(1)}, u32[]{:S(2)}, u32[]{:S(2)}) %collective-permute-start.10) | collective-permute-done | bytes 262176 | tf_op jit(solution)/shard_map/ppermute | solution.py:369
  92.5 2.7 %collective-permute-start.11 = (bf16[512,256]{1,0:T(8,128)(2,1)S(1)}, bf16[512,256]{1,0:T(8,128)(2,1)S(1)}, u32[]{:S(2)}, u32[]{:S(2)}) collective-permute-start(bf16[512,256]{1,0:T(8,128)(2,1)S(1)} %shard_map.79), channel_id=1, source_target_pairs={{2,4},{3,5},{6,8},{7,9},{10,12},{11,13},{14,0},{15,1},{4,2},{5,3},... | collective-permute-start | bytes 786440 | tf_op jit(solution)/shard_map/ppermute | solution.py:369
  95.3 2.0 %collective-permute-done.9.got_ref = bf16[512,256]{1,0:T(8,128)(2,1)S(1)} collective-permute-done((bf16[512,256]{1,0:T(8,128)(2,1)S(1)}, bf16[512,256]{1,0:T(8,128)(2,1)S(1)}, u32[]{:S(2)}, u32[]{:S(2)}) %collective-permute-start.9) | collective-permute-done | bytes 262176 | tf_op jit(solution)/shard_map/ppermute | solution.py:369
  97.3 4.7 %collective-permute-done.11.got_ref = bf16[512,256]{1,0:T(8,128)(2,1)S(1)} collective-permute-done((bf16[512,256]{1,0:T(8,128)(2,1)S(1)}, bf16[512,256]{1,0:T(8,128)(2,1)S(1)}, u32[]{:S(2)}, u32[]{:S(2)}) %collective-permute-start.11) | collective-permute-done | bytes 262176 | tf_op jit(solution)/shard_map/ppermute | solution.py:369
  102.0 0.7 shard_map.81
  (5 shorter events, 0.2 us)
Async XLA Ops:
  0.0 30.0 %copy-start = (bf16[2,512,256]{2,1,0:T(8,128)(2,1)S(1)}, bf16[2,512,256]{2,1,0:T(8,128)(2,1)}, u32[]{:S(2)}) copy-start(bf16[2,512,256]{2,1,0:T(8,128)(2,1)} %k_ref.1) | copy-start | bytes 1572868
  0.0 30.0 %copy-start.1 = (bf16[2,512,256]{2,1,0:T(8,128)(2,1)S(1)}, bf16[2,512,256]{2,1,0:T(8,128)(2,1)}, u32[]{:S(2)}) copy-start(bf16[2,512,256]{2,1,0:T(8,128)(2,1)} %v_ref.1) | copy-start | bytes 1572868
  0.0 30.0 %copy-start.2 = (bf16[512,256]{1,0:T(8,128)(2,1)S(1)}, bf16[512,256]{1,0:T(8,128)(2,1)}, u32[]{:S(2)}) copy-start(bf16[512,256]{1,0:T(8,128)(2,1)} %q_ref.1) | copy-start | bytes 786436
  0.0 30.0 %copy-start.3 = (bf16[512,256]{1,0:T(8,128)(2,1)S(1)}, bf16[512,256]{1,0:T(8,128)(2,1)}, u32[]{:S(2)}) copy-start(bf16[512,256]{1,0:T(8,128)(2,1)} %g_ref.1) | copy-start | bytes 786436
  0.0 39.0 %collective-permute-start.2 = (bf16[256,4096]{1,0:T(8,128)(2,1)}, bf16[256,4096]{1,0:T(8,128)(2,1)}, u32[]{:S(2)}, u32[]{:S(2)}) collective-permute-start(bf16[256,4096]{1,0:T(8,128)(2,1)} %w_ref.1), channel_id=1, source_target_pairs={{0,1},{1,0},{2,3},{3,2},{4,5},{5,4},{6,7},{7,6},{8,9},{9,8},{10,11... | collective-permute-start | bytes 6291464 | tf_op jit(solution)/shard_map/ppermute | solution.py:372
  28.2 4.5 %collective-permute-start = (bf16[2,128,256]{2,1,0:T(8,128)(2,1)S(1)}, bf16[2,128,256]{2,1,0:T(8,128)(2,1)S(1)}, u32[]{:S(2)}, u32[]{:S(2)}) collective-permute-start(bf16[2,128,256]{2,1,0:T(8,128)(2,1)S(1)} %get-tuple-element.32), channel_id=1, source_target_pairs={{0,64},{64,128},{128,192},{192,256},{256,320},{320,384},{384,448},... | collective-permute-start | bytes 393224 | tf_op jit(solution)/shard_map/ppermute | solution.py:376
  32.9 8.6 %collective-permute-start.1 = (bf16[2,128,256]{2,1,0:T(8,128)(2,1)S(1)}, bf16[2,128,256]{2,1,0:T(8,128)(2,1)S(1)}, u32[]{:S(2)}, u32[]{:S(2)}) collective-permute-start(bf16[2,128,256]{2,1,0:T(8,128)(2,1)S(1)} %get-tuple-element.41), channel_id=1, source_target_pairs={{0,128},{64,192},{128,256},{192,320},{256,384},{320,448},{1,129},{... | collective-permute-start | bytes 393224 | tf_op jit(solution)/shard_map/ppermute | solution.py:376
  41.7 14.4 %collective-permute-start.3 = (bf16[2,128,128]{2,1,0:T(8,128)(2,1)S(1)}, bf16[2,128,128]{2,1,0:T(8,128)(2,1)S(1)}, u32[]{:S(2)}, u32[]{:S(2)}) collective-permute-start(bf16[2,128,128]{2,1,0:T(8,128)(2,1)S(1)} %shard_map.70), channel_id=1, source_target_pairs={{0,256},{64,320},{128,384},{192,448},{1,257},{65,321},{129,385},{1... | collective-permute-start | bytes 196616 | tf_op jit(solution)/shard_map/ppermute | solution.py:376
  56.6 3.4 %collective-permute-start.4 = (bf16[512,256]{1,0:T(8,128)(2,1)S(1)}, bf16[512,256]{1,0:T(8,128)(2,1)S(1)}, u32[]{:S(2)}, u32[]{:S(2)}) collective-permute-start(bf16[512,256]{1,0:T(8,128)(2,1)S(1)} %shard_map.71.a_ref), channel_id=1, source_target_pairs={{0,1},{1,0},{2,3},{3,2},{4,5},{5,4},{6,7},{7,6},{8,9},{9,8},{10,11... | collective-permute-start | bytes 786440 | tf_op jit(solution)/shard_map/ppermute | solution.py:372
  60.3 11.0 %collective-permute-start.5 = (bf16[512,256]{1,0:T(8,128)(2,1)S(1)}, bf16[512,256]{1,0:T(8,128)(2,1)S(1)}, u32[]{:S(2)}, u32[]{:S(2)}) collective-permute-start(bf16[512,256]{1,0:T(8,128)(2,1)S(1)} %shard_map.72), channel_id=1, source_target_pairs={{0,2},{1,3},{4,6},{5,7},{8,10},{9,11},{12,14},{13,15},{2,0},{3,1},... | collective-permute-start | bytes 786440 | tf_op jit(solution)/shard_map/ppermute | solution.py:369
  64.1 12.9 %collective-permute-start.6 = (bf16[512,256]{1,0:T(8,128)(2,1)S(1)}, bf16[512,256]{1,0:T(8,128)(2,1)S(1)}, u32[]{:S(2)}, u32[]{:S(2)}) collective-permute-start(bf16[512,256]{1,0:T(8,128)(2,1)S(1)} %shard_map.73), channel_id=1, source_target_pairs={{0,2},{1,3},{4,6},{5,7},{8,10},{9,11},{12,14},{13,15},{2,0},{3,1},... | collective-permute-start | bytes 786440 | tf_op jit(solution)/shard_map/ppermute | solution.py:369
  71.7 10.8 %collective-permute-start.8 = (bf16[512,256]{1,0:T(8,128)(2,1)S(1)}, bf16[512,256]{1,0:T(8,128)(2,1)S(1)}, u32[]{:S(2)}, u32[]{:S(2)}) collective-permute-start(bf16[512,256]{1,0:T(8,128)(2,1)S(1)} %shard_map.74), channel_id=1, source_target_pairs={{2,4},{3,5},{6,8},{7,9},{10,12},{11,13},{14,0},{15,1},{4,2},{5,3},... | collective-permute-start | bytes 786440 | tf_op jit(solution)/shard_map/ppermute | solution.py:369
  78.0 10.3 %collective-permute-start.7 = (bf16[512,256]{1,0:T(8,128)(2,1)S(1)}, bf16[512,256]{1,0:T(8,128)(2,1)S(1)}, u32[]{:S(2)}, u32[]{:S(2)}) collective-permute-start(bf16[512,256]{1,0:T(8,128)(2,1)S(1)} %shard_map.76), channel_id=1, source_target_pairs={{2,4},{3,5},{6,8},{7,9},{10,12},{11,13},{14,0},{15,1},{4,2},{5,3},... | collective-permute-start | bytes 786440 | tf_op jit(solution)/shard_map/ppermute | solution.py:369
  82.5 9.9 %collective-permute-start.10 = (bf16[512,256]{1,0:T(8,128)(2,1)S(1)}, bf16[512,256]{1,0:T(8,128)(2,1)S(1)}, u32[]{:S(2)}, u32[]{:S(2)}) collective-permute-start(bf16[512,256]{1,0:T(8,128)(2,1)S(1)} %shard_map.77), channel_id=1, source_target_pairs={{0,2},{1,3},{4,6},{5,7},{8,10},{9,11},{12,14},{13,15},{2,0},{3,1},... | collective-permute-start | bytes 786440 | tf_op jit(solution)/shard_map/ppermute | solution.py:369
  88.3 9.0 %collective-permute-start.9 = (bf16[512,256]{1,0:T(8,128)(2,1)S(1)}, bf16[512,256]{1,0:T(8,128)(2,1)S(1)}, u32[]{:S(2)}, u32[]{:S(2)}) collective-permute-start(bf16[512,256]{1,0:T(8,128)(2,1)S(1)} %shard_map.78), channel_id=1, source_target_pairs={{0,2},{1,3},{4,6},{5,7},{8,10},{9,11},{12,14},{13,15},{2,0},{3,1},... | collective-permute-start | bytes 786440 | tf_op jit(solution)/shard_map/ppermute | solution.py:369
  92.5 9.5 %collective-permute-start.11 = (bf16[512,256]{1,0:T(8,128)(2,1)S(1)}, bf16[512,256]{1,0:T(8,128)(2,1)S(1)}, u32[]{:S(2)}, u32[]{:S(2)}) collective-permute-start(bf16[512,256]{1,0:T(8,128)(2,1)S(1)} %shard_map.79), channel_id=1, source_target_pairs={{2,4},{3,5},{6,8},{7,9},{10,12},{11,13},{14,0},{15,1},{4,2},{5,3},... | collective-permute-start | bytes 786440 | tf_op jit(solution)/shard_map/ppermute | solution.py:369

commit v7 on v6

--- a/solution.py
+++ b/solution.py
@@ -79,7 +79,7 @@
         level = level + (apart >= 2**bit).astype(jnp.int32)
     lev_ref[...] = jnp.where(s_r > s_c, level, -1)
     eye = (place_r == place_c).astype(F32)
-    for copy in copies:
+    for copy in copies[: len(copies) // 2 + 1]:
         copy.wait()
 
     blocks_of = [[] for _ in range(heads)]
@@ -114,6 +114,9 @@
                 Z.append(halves(dot(wide(C), square(xw[i]))))
             for i in num:
                 X[i] = X[i] - halves(dot(xw[i], square(wide(Z[i]))))
+        if step == 0:
+            for copy in copies[len(copies) // 2 + 1 :]:
+                copy.wait()
         A, B = [], []
         for i in num:
             blk, h = probs[i]
@@ -173,7 +176,35 @@
     )(*(pltpu.with_memory_space_constraint(a, pltpu.HBM) for a in (k, v, betas)))
 
 
-def local_kernel(q_ref, k_ref, v_ref, g_ref, x_ref, e_ref, a_ref, c_ref, l_ref, m_ref, s_ref):
+def local_kernel(
+    q_hbm,
+    k_hbm,
+    v_hbm,
+    g_hbm,
+    x_ref,
+    e_ref,
+    a_ref,
+    c_ref,
+    l_ref,
+    m_ref,
+    s_ref,
+    q_ref,
+    k_ref,
+    v_ref,
+    g_ref,
+    sems,
+):
+    copies = []
+    cut = q_ref.shape[0] // 2
+    for source, target in ((k_hbm, k_ref), (q_hbm, q_ref), (v_hbm, v_ref), (g_hbm, g_ref)):
+        for i in range(2):
+            rows = slice(i * cut, (i + 1) * cut)
+            for part in ((rows,),) if len(source.shape) == 2 else ((0, rows), (1, rows)):
+                at = sems.at[len(copies)]
+                copies.append(pltpu.make_async_copy(source.at[part], target.at[part], at))
+                copies[-1].start()
+    for copy in copies:
+        copy.wait()
     heads = q_ref.shape[1] // HD
     blocks = q_ref.shape[0] // SPAN
     sub = 2 * SPAN
@@ -226,24 +257,37 @@
     return jnp.concatenate([a, b], axis=1)
 
 
-def fold_kernel(x_ref, m_ref, send_ref, tot_ref, in_ref):
-    peers, heads = m_ref.shape[:2]
-    x = x_ref[0]
+def pair_kernel(x_ref, own_ref, got_ref, send_ref):
+    odd = x_ref[0] % 2 == 1
+    zero = jnp.zeros((HD, HD), F32)
+    for h in range(own_ref.shape[0]):
+        own, got = own_ref[h], got_ref[h]
+        low, high = jnp.where(odd, got, own), jnp.where(odd, own, got)
+        out = dot(high[:, :HD], low) + affine(zero, high[:, HD:].astype(F32))
+        send_ref[h] = out.astype(BF16)
+
+
+def group_kernel(x_ref, own_ref, got_ref, send_ref, tot_ref):
+    late = x_ref[0] >= 2
+    zero = jnp.zeros((HD, HD), F32)
+    for h in range(own_ref.shape[0]):
+        own, got = own_ref[h], got_ref[h]
+        low, high = jnp.where(late, got, own), jnp.where(late, own, got)
+        out = dot(high[:, :HD], low) + affine(zero, high[:, HD:].astype(F32))
+        send_ref[h] = out.astype(BF16)
+        tot_ref[h] = out
+
+
+def inside_kernel(x_ref, pair_ref, mate_ref, in_ref):
+    late, odd = x_ref[0] >= 2, x_ref[0] % 2 == 1
     r = lax.broadcasted_iota(jnp.int32, (HD, 2 * HD), 0)
     c = lax.broadcasted_iota(jnp.int32, (HD, 2 * HD), 1)
     zero = jnp.zeros((HD, HD), F32)
-    total = [m_ref[0, h].astype(F32) for h in range(heads)]
-    inside = [(r == c).astype(F32)] * heads
-    for k in range(1, peers):
-        for h in range(heads):
-            inside[h] = jnp.where(x == k, total[h], inside[h])
-            later = m_ref[k, h]
-            prod = halves(dot(later[:, :HD], jnp.concatenate(split(total[h]), axis=1)))
-            total[h] = prod + affine(zero, later[:, HD:].astype(F32))
-    for h in range(heads):
-        send_ref[h] = total[h].astype(BF16)
-        tot_ref[h] = total[h]
-        in_ref[h] = inside[h]
+    for h in range(pair_ref.shape[0]):
+        base = jnp.where(late, pair_ref[h], (r == c).astype(BF16))
+        map_ = mate_ref[h]
+        out = dot(map_[:, :HD], base) + affine(zero, map_[:, HD:].astype(F32))
+        in_ref[h] = jnp.where(odd, out, base.astype(F32))
 
 
 def join_kernel(later_ref, earlier_ref, send_ref, out_ref):
@@ -316,6 +360,18 @@
         copy.wait()
 
 
+def token_parts(big, made):
+    tokens = jax.ShapeDtypeStruct(big[0].shape, F32)
+    return pl.pallas_call(
+        local_kernel,
+        out_shape=(tokens, jax.ShapeDtypeStruct(big[0].shape, BF16), tokens),
+        in_specs=[pl.BlockSpec(memory_space=pltpu.HBM)] * 4 + [VM] * 4,
+        out_specs=(VM, VM, VM),
+        scratch_shapes=[pltpu.VMEM(a.shape, a.dtype) for a in big] + [pltpu.SemaphoreType.DMA((12,))],
+        compiler_params=pltpu.CompilerParams(vmem_limit_bytes=16 * 1024 * 1024),
+    )(*(pltpu.with_memory_space_constraint(a, pltpu.HBM) for a in big), *made)
+
+
 def pack(chips, me, weight, mate_weight):
     rows = weight.shape[0]
     return pl.pallas_call(
@@ -333,13 +389,22 @@
     return dot(a, w[:rows]) + dot(b, w[rows:])
 
 
-def term_kernel(at, a_ref, b_ref, w_ref, o_ref):
-    o_ref[...] = term(a_ref[...], b_ref[...], w_ref[at]).astype(BF16)
-
-
-def hop_kernel(at, a_ref, b_ref, w_ref, got_ref, o_ref):
+def far_kernel(me_ref, a_ref, b_ref, w_ref, ahead_ref, back_ref):
+    odd = (me_ref[0] // 2) % 2 != 0
+    out = term(a_ref[...], b_ref[...], w_ref[0]).astype(BF16)
+    cut = ahead_ref.shape[0]
+    ahead_ref[...] = jnp.where(odd, out[cut:], out[:cut])
+    back_ref[...] = jnp.where(odd, out[:cut], out[cut:])
+
+
+def hop_kernel(at, side, me_ref, a_ref, b_ref, w_ref, got_ref, o_ref):
+    odd = (me_ref[0] // 2) % 2
     out = term(a_ref[...], b_ref[...], w_ref[at])
-    o_ref[...] = (out + got_ref[...].astype(F32)).astype(BF16)
+    cut = got_ref.shape[0]
+    for i in range(2):
+        rows = slice(i * cut, (i + 1) * cut)
+        got = jnp.where((odd + side) % 2 == i, got_ref[...].astype(F32), 0.0)
+        o_ref[rows] = (out[rows] + got).astype(BF16)
 
 
 def rest_kernel(picks, a_ref, b_ref, w_ref, o_ref):
@@ -371,6 +436,11 @@
     def mate(a):
         return lax.ppermute(a, "head", [(i, i ^ 1) for i in range(devices)])
 
+    def swap_x(a, odd):
+        peers = lax.axis_size("ctx_1")
+        pairs = [(i, (i + 1) % peers) for i in range(odd, peers, 2)]
+        return lax.ppermute(a, "ctx_1", pairs + [(j, i) for i, j in pairs])
+
     def later_z(a, by):
         groups = lax.axis_size("ctx_0")
         return lax.ppermute(a, "ctx_0", [(i, i + by) for i in range(groups - by)])
@@ -382,23 +452,17 @@
     wide_send = jax.ShapeDtypeStruct((heads, HD, 2 * HD), BF16)
     state_send = jax.ShapeDtypeStruct((heads, HD, HD), BF16)
     tokens = jax.ShapeDtypeStruct((tok, cols), F32)
-    gathered = lax.all_gather(maps, "ctx_1")
     x = lax.axis_index("ctx_1").astype(jnp.int32).reshape(1)
-    send, total, inside = small(
-        fold_kernel, (wide_send, wide_map, wide_map), x, gathered, specs=[SM, VM]
+    beside = swap_x(maps, 0)
+    pair = small(pair_kernel, wide_send, x, maps, beside, specs=[SM, VM, VM])
+    other = swap_x(pair, 1)
+    send, total = small(
+        group_kernel, (wide_send, wide_map), x, pair, other, specs=[SM, VM, VM]
     )
+    inside = small(inside_kernel, wide_map, x, other, beside, specs=[SM, VM, VM])
     near = later_z(send, 1)
-    local, carry, silu = small(
-        local_kernel,
-        (tokens, jax.ShapeDtypeStruct((tok, cols), BF16), tokens),
-        queries,
-        keys,
-        values,
-        gate,
-        inverse,
-        scales,
-        lax.optimization_barrier((lefts, total))[0],
-        sources,
+    local, carry, silu = token_parts(
+        (queries, keys, values, gate), (inverse, scales, lax.optimization_barrier((lefts, total))[0], sources)
     )
     near = lax.optimization_barrier((near, silu))[0]
     send, pair = small(join_kernel, (wide_send, wide_map), total, near)
@@ -422,32 +486,36 @@
 
     half = chips // 2
     sent = jax.ShapeDtypeStruct((tok, cols), BF16)
+    part = jax.ShapeDtypeStruct((tok // 2, cols), BF16)
     both = (mixed_in, mate_in, ring_w)
-    far = small(functools.partial(term_kernel, 0), sent, *both)
-    came = across(far, 0)
-    late_in = lax.optimization_barrier((mixed_in, far))[0]
-    third = small(functools.partial(term_kernel, 1), sent, late_in, mate_in, ring_w)
-    came = lax.optimization_barrier((came, third))[0]
-    prior = small(functools.partial(hop_kernel, half), sent, *both, came)
-    got = (across(prior, 1), across(third, 0))
-    picks = [j + i * (half - 1) for j in range(2, half) for i in range(2)] + [chips - 1]
-    terms = small(
-        functools.partial(rest_kernel, picks),
-        jax.ShapeDtypeStruct((len(picks), tok, cols), F32),
-        lax.optimization_barrier((mixed_in, prior))[0],
-        mate_in,
-        ring_w,
-    )
-    for k in range(half - 2, 0, -1):
+    ahead, back = small(far_kernel, (part, part), place, *both, specs=[SM] + [VM] * 3)
+    got, prior, terms = (across(back, 1), across(ahead, 0)), None, None
+    for k in range(half - 1, 0, -1):
         sums = [None, None]
-        for i in (0, 1) if k % 2 else (1, 0):
-            came = lax.optimization_barrier((got[i], prior))[0]
-            body = functools.partial(add_kernel, 2 * (half - 2 - k) + i)
-            sums[i] = prior = small(body, sent, terms, came)
+        for i in (1, 0) if k % 2 else (0, 1):
+            came = got[i]
+            if prior is not None:
+                came = lax.optimization_barrier((came, prior))[0]
+            if k == half - 1:
+                body = functools.partial(hop_kernel, 1 + i * (half - 1), i)
+                sums[i] = small(body, sent, place, *both, came, specs=[SM] + [VM] * 4)
+            else:
+                body = functools.partial(add_kernel, 2 * (half - 2 - k) + i)
+                sums[i] = small(body, sent, terms, came)
+            prior = sums[i]
+        if k == half - 1:
+            picks = [j + i * (half - 1) for j in range(2, half) for i in range(2)] + [chips - 1]
+            terms = small(
+                functools.partial(rest_kernel, picks),
+                jax.ShapeDtypeStruct((len(picks), tok, cols), F32),
+                lax.optimization_barrier((mixed_in, prior))[0],
+                mate_in,
+                ring_w,
+            )
         got = (across(sums[1], 1), across(sums[0], 0))
-    came = lax.optimization_barrier((got[1], prior))[0]
+    came = lax.optimization_barrier((got[0], prior))[0]
     total = small(functools.partial(add_kernel, 2 * half - 4), tokens, terms, came)
-    return small(last_kernel, sent, total, got[0])
+    return small(last_kernel, sent, total, got[1])
 
 
 def solution(mesh):

time: 103 us -> 108 us (1.049)
  blocking collectives: 15.9 us -> 0 us
  starting transfers between devices: 46.7 us -> 60.8 us
  waiting for transfers between devices: 21.3 us -> 23.8 us
  local copies, waits for them, and re-layouts: 0.02 us -> 2.09 us
  Pallas kernels: 18.6 us -> 19.9 us
    all_gather x1 -> x0, blocking collectives: 15.9 us -> none  [per_device(): gathered = lax.all_gather(maps, 'ctx_1')]
    ppermute x0 -> x2, starting transfers between devices: none -> 10.5 us  [swap_x(): return lax.ppermute(a, 'ctx_1', pairs + [(j, i) for i, j in pairs])]
    ppermute x0 -> x2, waiting for transfers between devices: none -> 8.41 us  [swap_x(): return lax.ppermute(a, 'ctx_1', pairs + [(j, i) for i, j in pairs])]
    ppermute x7 -> x8, waiting for transfers between devices: 17.6 us -> 12 us  [across(): lax.ppermute(a, 'head', [(2 * c + i, 2 * d + i) for c, d in both for i in...]
    ppermute x7 -> x8, starting transfers between devices: 22.3 us -> 26.8 us  [across(): lax.ppermute(a, 'head', [(2 * c + i, 2 * d + i) for c, d in both for i in...]
    pallas_call x0 -> x1, Pallas kernels: none -> 4.16 us  [token_parts(): pl.pallas_call(local_kernel, out_shape=(tokens, jax.ShapeDtypeStruct(big[...]
    pallas_call x16 -> x17, Pallas kernels: 7.21 us -> 4.57 us  [small(): pl.pallas_call(kernel, out_shape=outs, in_specs=specs or [VM] * len(args)...]
    unnamed x8 -> x12, local copies, waits for them, and re-layouts: 0.02 us -> 2.09 us
  transfers between devices with their start and end apart: 12 -> 15, of which waited for: 8 -> 10; matrix products, arithmetic and copies ran while one was open for 0% -> 0% of each run, Pallas kernels for 16% -> 17%
where the time goes in v7:
time: 108 us; the launch traced here: 107 us
  starting transfers between devices  60.8 us (56%)
  waiting for transfers between devices  23.8 us (22%)
  Pallas kernels  19.9 us (18%)
  local copies, waits for them, and re-layouts  2.09 us (2%)
    ppermute x8, starting transfers between devices, across(): lax.ppermute(a, 'head', [(2 * c + i, 2 * d + i) for c, d in both for i in...  26.8 us
    ppermute x3, starting transfers between devices, later_z(): return lax.ppermute(a, 'ctx_0', [(i, i + by) for i in range(groups - by)])  19.7 us
    ppermute x8, waiting for transfers between devices, across(): lax.ppermute(a, 'head', [(2 * c + i, 2 * d + i) for c, d in both for i in...  12 us
    ppermute x2, starting transfers between devices, swap_x(): return lax.ppermute(a, 'ctx_1', pairs + [(j, i) for i, j in pairs])  10.5 us
    pallas_call x1, Pallas kernels, local_maps(): pl.pallas_call(functools.partial(map_kernel, group), out_shape=(jax.Shape...  9.36 us
    ppermute x2, waiting for transfers between devices, swap_x(): return lax.ppermute(a, 'ctx_1', pairs + [(j, i) for i, j in pairs])  8.41 us
    pallas_call x17, Pallas kernels, small(): pl.pallas_call(kernel, out_shape=outs, in_specs=specs or [VM] * len(args)...  4.57 us
    pallas_call x1, Pallas kernels, token_parts(): pl.pallas_call(local_kernel, out_shape=(tokens, jax.ShapeDtypeStruct(big[...  4.16 us
  transfers between devices with their start and end apart: 15, of which 10 were waited for; matrix products, arithmetic and copies ran while one was open for 0% of the time, Pallas kernels for 17%

profile of v7, /device:TPU:6, one launch (start us, length us, event | category | flops | bytes accessed | tf_op | source)
XLA Modules:
  0.0 107.0 jit_solution(14148418949715779328)
XLA Ops:
  0.0 1.9 %collective-permute-start.4 = (bf16[256,4096]{1,0:T(8,128)(2,1)}, bf16[256,4096]{1,0:T(8,128)(2,1)}, u32[]{:S(2)}, u32[]{:S(2)}) collective-permute-start(bf16[256,4096]{1,0:T(8,128)(2,1)} %w_ref.1), channel_id=1, source_target_pairs={{0,1},{1,0},{2,3},{3,2},{4,5},{5,4},{6,7},{7,6},{8,9},{9,8},{10,11... | collective-permute-start | bytes 6291464 | tf_op jit(solution)/shard_map/ppermute | solution.py:437
  1.9 9.4 %shard_map.64 = (bf16[2,128,256]{2,1,0:T(8,128)(2,1)S(1)}, bf16[16,128,256]{2,1,0:T(8,128)(2,1)S(1)}, f32[16,2,128]{2,1,0:T(2,128)S(1)}, bf16[16,128,256]{2,1,0:T(8,128)(2,1)S(1)}, f32[16,128,128]{2,1,0:T(8,128)S(1)}) custom-call(bf16[2,512,256]{2,1,0:T(8,128)(2,1)} %k_hbm.3, bf16[2,512,256]{2,1,0:T(8,128)(2,1)} %v_hbm.3, f32[2,2,512]{2,1,0:T(2,128)} %b_hbm.1), custom_call_target="tpu_custom_call" | custom-call | tf_op jit(solution)/shard_map/pallas_call | solution.py:157
  11.3 2.7 %collective-permute-start = (bf16[2,128,256]{2,1,0:T(8,128)(2,1)S(1)}, bf16[2,128,256]{2,1,0:T(8,128)(2,1)S(1)}, u32[]{:S(2)}, u32[]{:S(2)}) collective-permute-start(bf16[2,128,256]{2,1,0:T(8,128)(2,1)S(1)} %get-tuple-element.30.own_ref), channel_id=1, source_target_pairs={{0,16},{32,48},{16,0},{48,32},{1,17},{33,49},{17,1},{49,33},{2,18}... | collective-permute-start | bytes 393224 | tf_op jit(solution)/shard_map/ppermute | solution.py:442
  14.0 5.0 %collective-permute-done.got_ref.mate_ref = bf16[2,128,256]{2,1,0:T(8,128)(2,1)S(1)} collective-permute-done((bf16[2,128,256]{2,1,0:T(8,128)(2,1)S(1)}, bf16[2,128,256]{2,1,0:T(8,128)(2,1)S(1)}, u32[]{:S(2)}, u32[]{:S(2)}) %collective-permute-start) | collective-permute-done | bytes 131104 | tf_op jit(solution)/shard_map/ppermute | solution.py:442
  19.1 0.2 shard_map.65.own_ref
  19.3 7.8 %collective-permute-start.1 = (bf16[2,128,256]{2,1,0:T(8,128)(2,1)S(1)}, bf16[2,128,256]{2,1,0:T(8,128)(2,1)S(1)}, u32[]{:S(2)}, u32[]{:S(2)}) collective-permute-start(bf16[2,128,256]{2,1,0:T(8,128)(2,1)S(1)} %shard_map.65.own_ref), channel_id=1, source_target_pairs={{16,32},{48,0},{32,16},{0,48},{17,33},{49,1},{33,17},{1,49},{18,34... | collective-permute-start | bytes 393224 | tf_op jit(solution)/shard_map/ppermute | solution.py:442
  27.0 3.4 %collective-permute-done.1.pair_ref.got_ref = bf16[2,128,256]{2,1,0:T(8,128)(2,1)S(1)} collective-permute-done((bf16[2,128,256]{2,1,0:T(8,128)(2,1)S(1)}, bf16[2,128,256]{2,1,0:T(8,128)(2,1)S(1)}, u32[]{:S(2)}, u32[]{:S(2)}) %collective-permute-start.1) | collective-permute-done | bytes 131104 | tf_op jit(solution)/shard_map/ppermute | solution.py:442
  30.4 0.2 shard_map.67
  30.6 1.4 %collective-permute-start.2 = (bf16[2,128,256]{2,1,0:T(8,128)(2,1)S(1)}, bf16[2,128,256]{2,1,0:T(8,128)(2,1)S(1)}, u32[]{:S(2)}, u32[]{:S(2)}) collective-permute-start(bf16[2,128,256]{2,1,0:T(8,128)(2,1)S(1)} %get-tuple-element.31), channel_id=1, source_target_pairs={{0,64},{64,128},{128,192},{192,256},{256,320},{320,384},{384,448},... | collective-permute-start | bytes 393224 | tf_op jit(solution)/shard_map/ppermute | solution.py:446
  32.0 4.2 %shard_map.68 = (f32[512,256]{1,0:T(8,128)S(1)}, bf16[512,256]{1,0:T(8,128)(2,1)S(1)}, f32[512,256]{1,0:T(8,128)S(1)}) custom-call(bf16[512,256]{1,0:T(8,128)(2,1)} %q_hbm.1, bf16[2,512,256]{2,1,0:T(8,128)(2,1)} %k_hbm.3, bf16[2,512,256]{2,1,0:T(8,128)(2,1)} %v_hbm.3, bf16[512,256]{1,0:T(8,128)(2,1)} %g_hbm.1, ...), custom_call_target="tpu_custom_call" | custom-call | tf_op jit(solution)/shard_map/pallas_call | solution.py:365
  36.1 0.0 copy-start
  36.1 0.8 copy-done
  36.9 0.0 copy-start.2
  36.9 0.8 copy-done.2
  37.7 0.0 copy-start.4
  37.7 0.0 collective-permute-done.2.earlier_ref.near_ref
  37.7 0.2 shard_map.69
  37.9 0.5 copy-done.4
  38.4 6.1 %collective-permute-start.3 = (bf16[2,128,256]{2,1,0:T(8,128)(2,1)S(1)}, bf16[2,128,256]{2,1,0:T(8,128)(2,1)S(1)}, u32[]{:S(2)}, u32[]{:S(2)}) collective-permute-start(bf16[2,128,256]{2,1,0:T(8,128)(2,1)S(1)} %get-tuple-element.40), channel_id=1, source_target_pairs={{0,128},{64,192},{128,256},{192,320},{256,384},{320,448},{1,129},{... | collective-permute-start | bytes 393224 | tf_op jit(solution)/shard_map/ppermute | solution.py:446
  44.5 0.0 collective-permute-done.4.x_ref
  44.5 0.0 copy-start.5
  44.5 1.8 %shard_map.70.w_ref = bf16[8,512,256]{2,1,0:T(8,128)(2,1)S(1)} custom-call(s32[1]{0:T(128)} %bitcast.1.me_ref, bf16[256,4096]{1,0:T(8,128)(2,1)} %w_ref.1, bf16[256,4096]{1,0:T(8,128)(2,1)} %collective-permute-done.4.x_ref), custom_call_target="tpu_custom_call" | custom-call | tf_op jit(solution)/shard_map/pallas_call | solution.py:377
  46.4 0.0 copy-start.1
  46.4 0.0 copy-start.3
  46.4 0.6 collective-permute-done.3.far_ref.earlier_ref
  47.0 0.2 shard_map.72
  47.2 12.2 %collective-permute-start.5 = (bf16[2,128,128]{2,1,0:T(8,128)(2,1)S(1)}, bf16[2,128,128]{2,1,0:T(8,128)(2,1)S(1)}, u32[]{:S(2)}, u32[]{:S(2)}) collective-permute-start(bf16[2,128,128]{2,1,0:T(8,128)(2,1)S(1)} %shard_map.72), channel_id=1, source_target_pairs={{0,256},{64,320},{128,384},{192,448},{1,257},{65,321},{129,385},{1... | collective-permute-start | bytes 196616 | tf_op jit(solution)/shard_map/ppermute | solution.py:446
  59.4 0.2 shard_map.66.in_ref
  59.6 0.4 shard_map.71.entry_ref
  60.0 1.3 %collective-permute-done.5.state_ref = bf16[2,128,128]{2,1,0:T(8,128)(2,1)S(1)} collective-permute-done((bf16[2,128,128]{2,1,0:T(8,128)(2,1)S(1)}, bf16[2,128,128]{2,1,0:T(8,128)(2,1)S(1)}, u32[]{:S(2)}, u32[]{:S(2)}) %collective-permute-start.5) | collective-permute-done | bytes 65568 | tf_op jit(solution)/shard_map/ppermute | solution.py:446
  61.3 0.0 copy-done.5
  61.3 0.0 copy-done.1
  61.3 0.0 copy-done.3
  61.3 0.5 shard_map.73.a_ref
  61.8 1.9 %collective-permute-start.6 = (bf16[512,256]{1,0:T(8,128)(2,1)S(1)}, bf16[512,256]{1,0:T(8,128)(2,1)S(1)}, u32[]{:S(2)}, u32[]{:S(2)}) collective-permute-start(bf16[512,256]{1,0:T(8,128)(2,1)S(1)} %shard_map.73.a_ref), channel_id=1, source_target_pairs={{0,1},{1,0},{2,3},{3,2},{4,5},{5,4},{6,7},{7,6},{8,9},{9,8},{10,11... | collective-permute-start | bytes 786440 | tf_op jit(solution)/shard_map/ppermute | solution.py:437
  63.8 1.5 %collective-permute-done.6.b_ref = bf16[512,256]{1,0:T(8,128)(2,1)S(1)} collective-permute-done((bf16[512,256]{1,0:T(8,128)(2,1)S(1)}, bf16[512,256]{1,0:T(8,128)(2,1)S(1)}, u32[]{:S(2)}, u32[]{:S(2)}) %collective-permute-start.6) | collective-permute-done | bytes 262176 | tf_op jit(solution)/shard_map/ppermute | solution.py:437
  65.3 0.3 shard_map.74
  65.6 3.5 %collective-permute-start.8 = (bf16[256,256]{1,0:T(8,128)(2,1)S(1)}, bf16[256,256]{1,0:T(8,128)(2,1)S(1)}, u32[]{:S(2)}, u32[]{:S(2)}) collective-permute-start(bf16[256,256]{1,0:T(8,128)(2,1)S(1)} %get-tuple-element.47), channel_id=1, source_target_pairs={{0,2},{1,3},{4,6},{5,7},{8,10},{9,11},{12,14},{13,15},{2,0},{3,1},... | collective-permute-start | bytes 393224 | tf_op jit(solution)/shard_map/ppermute | solution.py:434
  69.1 5.1 %collective-permute-start.7 = (bf16[256,256]{1,0:T(8,128)(2,1)S(1)}, bf16[256,256]{1,0:T(8,128)(2,1)S(1)}, u32[]{:S(2)}, u32[]{:S(2)}) collective-permute-start(bf16[256,256]{1,0:T(8,128)(2,1)S(1)} %get-tuple-element.46), channel_id=1, source_target_pairs={{2,4},{3,5},{6,8},{7,9},{10,12},{11,13},{14,0},{15,1},{4,2},{5,3},... | collective-permute-start | bytes 393224 | tf_op jit(solution)/shard_map/ppermute | solution.py:434
  74.2 0.0 collective-permute-done.8.got_ref
  74.2 0.3 shard_map.75
  74.5 4.1 %collective-permute-start.9 = (bf16[512,256]{1,0:T(8,128)(2,1)S(1)}, bf16[512,256]{1,0:T(8,128)(2,1)S(1)}, u32[]{:S(2)}, u32[]{:S(2)}) collective-permute-start(bf16[512,256]{1,0:T(8,128)(2,1)S(1)} %shard_map.75), channel_id=1, source_target_pairs={{2,4},{3,5},{6,8},{7,9},{10,12},{11,13},{14,0},{15,1},{4,2},{5,3},... | collective-permute-start | bytes 786440 | tf_op jit(solution)/shard_map/ppermute | solution.py:434
  78.7 0.0 collective-permute-done.7.got_ref
  78.7 0.3 shard_map.76
  79.0 1.9 %collective-permute-start.11 = (bf16[512,256]{1,0:T(8,128)(2,1)S(1)}, bf16[512,256]{1,0:T(8,128)(2,1)S(1)}, u32[]{:S(2)}, u32[]{:S(2)}) collective-permute-start(bf16[512,256]{1,0:T(8,128)(2,1)S(1)} %shard_map.76), channel_id=1, source_target_pairs={{0,2},{1,3},{4,6},{5,7},{8,10},{9,11},{12,14},{13,15},{2,0},{3,1},... | collective-permute-start | bytes 786440 | tf_op jit(solution)/shard_map/ppermute | solution.py:434
  80.9 0.9 shard_map.77.terms_ref
  81.8 3.6 %collective-permute-done.9.got_ref = bf16[512,256]{1,0:T(8,128)(2,1)S(1)} collective-permute-done((bf16[512,256]{1,0:T(8,128)(2,1)S(1)}, bf16[512,256]{1,0:T(8,128)(2,1)S(1)}, u32[]{:S(2)}, u32[]{:S(2)}) %collective-permute-start.9) | collective-permute-done | bytes 262176 | tf_op jit(solution)/shard_map/ppermute | solution.py:434
  85.4 0.1 shard_map.78
  85.5 1.9 %collective-permute-start.10 = (bf16[512,256]{1,0:T(8,128)(2,1)S(1)}, bf16[512,256]{1,0:T(8,128)(2,1)S(1)}, u32[]{:S(2)}, u32[]{:S(2)}) collective-permute-start(bf16[512,256]{1,0:T(8,128)(2,1)S(1)} %shard_map.78), channel_id=1, source_target_pairs={{0,2},{1,3},{4,6},{5,7},{8,10},{9,11},{12,14},{13,15},{2,0},{3,1},... | collective-permute-start | bytes 786440 | tf_op jit(solution)/shard_map/ppermute | solution.py:434
  87.4 0.7 collective-permute-done.11.got_ref
  88.1 0.1 shard_map.79
  88.2 3.8 %collective-permute-start.13 = (bf16[512,256]{1,0:T(8,128)(2,1)S(1)}, bf16[512,256]{1,0:T(8,128)(2,1)S(1)}, u32[]{:S(2)}, u32[]{:S(2)}) collective-permute-start(bf16[512,256]{1,0:T(8,128)(2,1)S(1)} %shard_map.79), channel_id=1, source_target_pairs={{2,4},{3,5},{6,8},{7,9},{10,12},{11,13},{14,0},{15,1},{4,2},{5,3},... | collective-permute-start | bytes 786440 | tf_op jit(solution)/shard_map/ppermute | solution.py:434
  92.0 2.2 %collective-permute-done.10.got_ref = bf16[512,256]{1,0:T(8,128)(2,1)S(1)} collective-permute-done((bf16[512,256]{1,0:T(8,128)(2,1)S(1)}, bf16[512,256]{1,0:T(8,128)(2,1)S(1)}, u32[]{:S(2)}, u32[]{:S(2)}) %collective-permute-start.10) | collective-permute-done | bytes 262176 | tf_op jit(solution)/shard_map/ppermute | solution.py:434
  94.3 3.6 %collective-permute-start.12 = (bf16[512,256]{1,0:T(8,128)(2,1)S(1)}, bf16[512,256]{1,0:T(8,128)(2,1)S(1)}, u32[]{:S(2)}, u32[]{:S(2)}) collective-permute-start(bf16[512,256]{1,0:T(8,128)(2,1)S(1)} %shard_map.80), channel_id=1, source_target_pairs={{2,4},{3,5},{6,8},{7,9},{10,12},{11,13},{14,0},{15,1},{4,2},{5,3},... | collective-permute-start | bytes 786440 | tf_op jit(solution)/shard_map/ppermute | solution.py:434
  97.9 0.0 collective-permute-done.13.got_ref
  98.0 2.8 %collective-permute-start.14 = (bf16[512,256]{1,0:T(8,128)(2,1)S(1)}, bf16[512,256]{1,0:T(8,128)(2,1)S(1)}, u32[]{:S(2)}, u32[]{:S(2)}) collective-permute-start(bf16[512,256]{1,0:T(8,128)(2,1)S(1)} %shard_map.81), channel_id=1, source_target_pairs={{0,2},{1,3},{4,6},{5,7},{8,10},{9,11},{12,14},{13,15},{2,0},{3,1},... | collective-permute-start | bytes 786440 | tf_op jit(solution)/shard_map/ppermute | solution.py:434
  100.8 3.0 %collective-permute-done.12.got_ref = bf16[512,256]{1,0:T(8,128)(2,1)S(1)} collective-permute-done((bf16[512,256]{1,0:T(8,128)(2,1)S(1)}, bf16[512,256]{1,0:T(8,128)(2,1)S(1)}, u32[]{:S(2)}, u32[]{:S(2)}) %collective-permute-start.12) | collective-permute-done | bytes 262176 | tf_op jit(solution)/shard_map/ppermute | solution.py:434
  103.8 2.4 %collective-permute-done.14.got_ref = bf16[512,256]{1,0:T(8,128)(2,1)S(1)} collective-permute-done((bf16[512,256]{1,0:T(8,128)(2,1)S(1)}, bf16[512,256]{1,0:T(8,128)(2,1)S(1)}, u32[]{:S(2)}, u32[]{:S(2)}) %collective-permute-start.14) | collective-permute-done | bytes 262176 | tf_op jit(solution)/shard_map/ppermute | solution.py:434
  106.2 0.7 shard_map.83
  (3 shorter events, 0.1 us)
Async XLA Ops:
  0.0 44.5 %collective-permute-start.4 = (bf16[256,4096]{1,0:T(8,128)(2,1)}, bf16[256,4096]{1,0:T(8,128)(2,1)}, u32[]{:S(2)}, u32[]{:S(2)}) collective-permute-start(bf16[256,4096]{1,0:T(8,128)(2,1)} %w_ref.1), channel_id=1, source_target_pairs={{0,1},{1,0},{2,3},{3,2},{4,5},{5,4},{6,7},{7,6},{8,9},{9,8},{10,11... | collective-permute-start | bytes 6291464 | tf_op jit(solution)/shard_map/ppermute | solution.py:437
  11.3 7.8 %collective-permute-start = (bf16[2,128,256]{2,1,0:T(8,128)(2,1)S(1)}, bf16[2,128,256]{2,1,0:T(8,128)(2,1)S(1)}, u32[]{:S(2)}, u32[]{:S(2)}) collective-permute-start(bf16[2,128,256]{2,1,0:T(8,128)(2,1)S(1)} %get-tuple-element.30.own_ref), channel_id=1, source_target_pairs={{0,16},{32,48},{16,0},{48,32},{1,17},{33,49},{17,1},{49,33},{2,18}... | collective-permute-start | bytes 393224 | tf_op jit(solution)/shard_map/ppermute | solution.py:442
  19.3 11.1 %collective-permute-start.1 = (bf16[2,128,256]{2,1,0:T(8,128)(2,1)S(1)}, bf16[2,128,256]{2,1,0:T(8,128)(2,1)S(1)}, u32[]{:S(2)}, u32[]{:S(2)}) collective-permute-start(bf16[2,128,256]{2,1,0:T(8,128)(2,1)S(1)} %shard_map.65.own_ref), channel_id=1, source_target_pairs={{16,32},{48,0},{32,16},{0,48},{17,33},{49,1},{33,17},{1,49},{18,34... | collective-permute-start | bytes 393224 | tf_op jit(solution)/shard_map/ppermute | solution.py:442
  30.6 7.1 %collective-permute-start.2 = (bf16[2,128,256]{2,1,0:T(8,128)(2,1)S(1)}, bf16[2,128,256]{2,1,0:T(8,128)(2,1)S(1)}, u32[]{:S(2)}, u32[]{:S(2)}) collective-permute-start(bf16[2,128,256]{2,1,0:T(8,128)(2,1)S(1)} %get-tuple-element.31), channel_id=1, source_target_pairs={{0,64},{64,128},{128,192},{192,256},{256,320},{320,384},{384,448},... | collective-permute-start | bytes 393224 | tf_op jit(solution)/shard_map/ppermute | solution.py:446
  36.1 0.8 copy-start
  36.9 0.8 copy-start.2
  37.7 0.7 copy-start.4
  38.4 8.6 %collective-permute-start.3 = (bf16[2,128,256]{2,1,0:T(8,128)(2,1)S(1)}, bf16[2,128,256]{2,1,0:T(8,128)(2,1)S(1)}, u32[]{:S(2)}, u32[]{:S(2)}) collective-permute-start(bf16[2,128,256]{2,1,0:T(8,128)(2,1)S(1)} %get-tuple-element.40), channel_id=1, source_target_pairs={{0,128},{64,192},{128,256},{192,320},{256,384},{320,448},{1,129},{... | collective-permute-start | bytes 393224 | tf_op jit(solution)/shard_map/ppermute | solution.py:446
  44.5 16.8 %copy-start.5 = (bf16[512,256]{1,0:T(8,128)(2,1)S(1)}, bf16[512,256]{1,0:T(8,128)(2,1)}, u32[]{:S(2)}) copy-start(bf16[512,256]{1,0:T(8,128)(2,1)} %copy-done.4) | copy-start | bytes 786436
  46.4 14.9 %copy-start.1 = (f32[512,256]{1,0:T(8,128)S(1)}, f32[512,256]{1,0:T(8,128)}, u32[]{:S(2)}) copy-start(f32[512,256]{1,0:T(8,128)} %copy-done) | copy-start | bytes 1572868
  46.4 14.9 %copy-start.3 = (f32[512,256]{1,0:T(8,128)S(1)}, f32[512,256]{1,0:T(8,128)}, u32[]{:S(2)}) copy-start(f32[512,256]{1,0:T(8,128)} %copy-done.2) | copy-start | bytes 1572868
  47.2 14.1 %collective-permute-start.5 = (bf16[2,128,128]{2,1,0:T(8,128)(2,1)S(1)}, bf16[2,128,128]{2,1,0:T(8,128)(2,1)S(1)}, u32[]{:S(2)}, u32[]{:S(2)}) collective-permute-start(bf16[2,128,128]{2,1,0:T(8,128)(2,1)S(1)} %shard_map.72), channel_id=1, source_target_pairs={{0,256},{64,320},{128,384},{192,448},{1,257},{65,321},{129,385},{1... | collective-permute-start | bytes 196616 | tf_op jit(solution)/shard_map/ppermute | solution.py:446
  61.8 3.4 %collective-permute-start.6 = (bf16[512,256]{1,0:T(8,128)(2,1)S(1)}, bf16[512,256]{1,0:T(8,128)(2,1)S(1)}, u32[]{:S(2)}, u32[]{:S(2)}) collective-permute-start(bf16[512,256]{1,0:T(8,128)(2,1)S(1)} %shard_map.73.a_ref), channel_id=1, source_target_pairs={{0,1},{1,0},{2,3},{3,2},{4,5},{5,4},{6,7},{7,6},{8,9},{9,8},{10,11... | collective-permute-start | bytes 786440 | tf_op jit(solution)/shard_map/ppermute | solution.py:437
  65.6 8.6 %collective-permute-start.8 = (bf16[256,256]{1,0:T(8,128)(2,1)S(1)}, bf16[256,256]{1,0:T(8,128)(2,1)S(1)}, u32[]{:S(2)}, u32[]{:S(2)}) collective-permute-start(bf16[256,256]{1,0:T(8,128)(2,1)S(1)} %get-tuple-element.47), channel_id=1, source_target_pairs={{0,2},{1,3},{4,6},{5,7},{8,10},{9,11},{12,14},{13,15},{2,0},{3,1},... | collective-permute-start | bytes 393224 | tf_op jit(solution)/shard_map/ppermute | solution.py:434
  69.1 9.6 %collective-permute-start.7 = (bf16[256,256]{1,0:T(8,128)(2,1)S(1)}, bf16[256,256]{1,0:T(8,128)(2,1)S(1)}, u32[]{:S(2)}, u32[]{:S(2)}) collective-permute-start(bf16[256,256]{1,0:T(8,128)(2,1)S(1)} %get-tuple-element.46), channel_id=1, source_target_pairs={{2,4},{3,5},{6,8},{7,9},{10,12},{11,13},{14,0},{15,1},{4,2},{5,3},... | collective-permute-start | bytes 393224 | tf_op jit(solution)/shard_map/ppermute | solution.py:434
  74.5 10.9 %collective-permute-start.9 = (bf16[512,256]{1,0:T(8,128)(2,1)S(1)}, bf16[512,256]{1,0:T(8,128)(2,1)S(1)}, u32[]{:S(2)}, u32[]{:S(2)}) collective-permute-start(bf16[512,256]{1,0:T(8,128)(2,1)S(1)} %shard_map.75), channel_id=1, source_target_pairs={{2,4},{3,5},{6,8},{7,9},{10,12},{11,13},{14,0},{15,1},{4,2},{5,3},... | collective-permute-start | bytes 786440 | tf_op jit(solution)/shard_map/ppermute | solution.py:434
  79.0 9.1 %collective-permute-start.11 = (bf16[512,256]{1,0:T(8,128)(2,1)S(1)}, bf16[512,256]{1,0:T(8,128)(2,1)S(1)}, u32[]{:S(2)}, u32[]{:S(2)}) collective-permute-start(bf16[512,256]{1,0:T(8,128)(2,1)S(1)} %shard_map.76), channel_id=1, source_target_pairs={{0,2},{1,3},{4,6},{5,7},{8,10},{9,11},{12,14},{13,15},{2,0},{3,1},... | collective-permute-start | bytes 786440 | tf_op jit(solution)/shard_map/ppermute | solution.py:434
  85.5 8.8 %collective-permute-start.10 = (bf16[512,256]{1,0:T(8,128)(2,1)S(1)}, bf16[512,256]{1,0:T(8,128)(2,1)S(1)}, u32[]{:S(2)}, u32[]{:S(2)}) collective-permute-start(bf16[512,256]{1,0:T(8,128)(2,1)S(1)} %shard_map.78), channel_id=1, source_target_pairs={{0,2},{1,3},{4,6},{5,7},{8,10},{9,11},{12,14},{13,15},{2,0},{3,1},... | collective-permute-start | bytes 786440 | tf_op jit(solution)/shard_map/ppermute | solution.py:434
  88.2 9.7 %collective-permute-start.13 = (bf16[512,256]{1,0:T(8,128)(2,1)S(1)}, bf16[512,256]{1,0:T(8,128)(2,1)S(1)}, u32[]{:S(2)}, u32[]{:S(2)}) collective-permute-start(bf16[512,256]{1,0:T(8,128)(2,1)S(1)} %shard_map.79), channel_id=1, source_target_pairs={{2,4},{3,5},{6,8},{7,9},{10,12},{11,13},{14,0},{15,1},{4,2},{5,3},... | collective-permute-start | bytes 786440 | tf_op jit(solution)/shard_map/ppermute | solution.py:434
  94.3 9.5 %collective-permute-start.12 = (bf16[512,256]{1,0:T(8,128)(2,1)S(1)}, bf16[512,256]{1,0:T(8,128)(2,1)S(1)}, u32[]{:S(2)}, u32[]{:S(2)}) collective-permute-start(bf16[512,256]{1,0:T(8,128)(2,1)S(1)} %shard_map.80), channel_id=1, source_target_pairs={{2,4},{3,5},{6,8},{7,9},{10,12},{11,13},{14,0},{15,1},{4,2},{5,3},... | collective-permute-start | bytes 786440 | tf_op jit(solution)/shard_map/ppermute | solution.py:434
  98.0 8.3 %collective-permute-start.14 = (bf16[512,256]{1,0:T(8,128)(2,1)S(1)}, bf16[512,256]{1,0:T(8,128)(2,1)S(1)}, u32[]{:S(2)}, u32[]{:S(2)}) collective-permute-start(bf16[512,256]{1,0:T(8,128)(2,1)S(1)} %shard_map.81), channel_id=1, source_target_pairs={{0,2},{1,3},{4,6},{5,7},{8,10},{9,11},{12,14},{13,15},{2,0},{3,1},... | collective-permute-start | bytes 786440 | tf_op jit(solution)/shard_map/ppermute | solution.py:434

commit v8 on v6

--- a/solution.py
+++ b/solution.py
@@ -79,7 +79,7 @@
         level = level + (apart >= 2**bit).astype(jnp.int32)
     lev_ref[...] = jnp.where(s_r > s_c, level, -1)
     eye = (place_r == place_c).astype(F32)
-    for copy in copies:
+    for copy in copies[: len(copies) // 2 + 1]:
         copy.wait()
 
     blocks_of = [[] for _ in range(heads)]
@@ -114,6 +114,9 @@
                 Z.append(halves(dot(wide(C), square(xw[i]))))
             for i in num:
                 X[i] = X[i] - halves(dot(xw[i], square(wide(Z[i]))))
+        if step == 0:
+            for copy in copies[len(copies) // 2 + 1 :]:
+                copy.wait()
         A, B = [], []
         for i in num:
             blk, h = probs[i]
@@ -333,13 +336,22 @@
     return dot(a, w[:rows]) + dot(b, w[rows:])
 
 
-def term_kernel(at, a_ref, b_ref, w_ref, o_ref):
-    o_ref[...] = term(a_ref[...], b_ref[...], w_ref[at]).astype(BF16)
-
-
-def hop_kernel(at, a_ref, b_ref, w_ref, got_ref, o_ref):
+def far_kernel(me_ref, a_ref, b_ref, w_ref, ahead_ref, back_ref):
+    odd = (me_ref[0] // 2) % 2 != 0
+    out = term(a_ref[...], b_ref[...], w_ref[0]).astype(BF16)
+    cut = ahead_ref.shape[0]
+    ahead_ref[...] = jnp.where(odd, out[cut:], out[:cut])
+    back_ref[...] = jnp.where(odd, out[:cut], out[cut:])
+
+
+def hop_kernel(at, side, me_ref, a_ref, b_ref, w_ref, got_ref, o_ref):
+    odd = (me_ref[0] // 2) % 2
     out = term(a_ref[...], b_ref[...], w_ref[at])
-    o_ref[...] = (out + got_ref[...].astype(F32)).astype(BF16)
+    cut = got_ref.shape[0]
+    for i in range(2):
+        rows = slice(i * cut, (i + 1) * cut)
+        got = jnp.where((odd + side) % 2 == i, got_ref[...].astype(F32), 0.0)
+        o_ref[rows] = (out[rows] + got).astype(BF16)
 
 
 def rest_kernel(picks, a_ref, b_ref, w_ref, o_ref):
@@ -422,32 +434,36 @@
 
     half = chips // 2
     sent = jax.ShapeDtypeStruct((tok, cols), BF16)
+    part = jax.ShapeDtypeStruct((tok // 2, cols), BF16)
     both = (mixed_in, mate_in, ring_w)
-    far = small(functools.partial(term_kernel, 0), sent, *both)
-    came = across(far, 0)
-    late_in = lax.optimization_barrier((mixed_in, far))[0]
-    third = small(functools.partial(term_kernel, 1), sent, late_in, mate_in, ring_w)
-    came = lax.optimization_barrier((came, third))[0]
-    prior = small(functools.partial(hop_kernel, half), sent, *both, came)
-    got = (across(prior, 1), across(third, 0))
-    picks = [j + i * (half - 1) for j in range(2, half) for i in range(2)] + [chips - 1]
-    terms = small(
-        functools.partial(rest_kernel, picks),
-        jax.ShapeDtypeStruct((len(picks), tok, cols), F32),
-        lax.optimization_barrier((mixed_in, prior))[0],
-        mate_in,
-        ring_w,
-    )
-    for k in range(half - 2, 0, -1):
+    ahead, back = small(far_kernel, (part, part), place, *both, specs=[SM] + [VM] * 3)
+    got, prior, terms = (across(back, 1), across(ahead, 0)), None, None
+    for k in range(half - 1, 0, -1):
         sums = [None, None]
-        for i in (0, 1) if k % 2 else (1, 0):
-            came = lax.optimization_barrier((got[i], prior))[0]
-            body = functools.partial(add_kernel, 2 * (half - 2 - k) + i)
-            sums[i] = prior = small(body, sent, terms, came)
+        for i in (1, 0) if k % 2 else (0, 1):
+            came = got[i]
+            if prior is not None:
+                came = lax.optimization_barrier((came, prior))[0]
+            if k == half - 1:
+                body = functools.partial(hop_kernel, 1 + i * (half - 1), i)
+                sums[i] = small(body, sent, place, *both, came, specs=[SM] + [VM] * 4)
+            else:
+                body = functools.partial(add_kernel, 2 * (half - 2 - k) + i)
+                sums[i] = small(body, sent, terms, came)
+            prior = sums[i]
+        if k == half - 1:
+            picks = [j + i * (half - 1) for j in range(2, half) for i in range(2)] + [chips - 1]
+            terms = small(
+                functools.partial(rest_kernel, picks),
+                jax.ShapeDtypeStruct((len(picks), tok, cols), F32),
+                lax.optimization_barrier((mixed_in, prior))[0],
+                mate_in,
+                ring_w,
+            )
         got = (across(sums[1], 1), across(sums[0], 0))
-    came = lax.optimization_barrier((got[1], prior))[0]
+    came = lax.optimization_barrier((got[0], prior))[0]
     total = small(functools.partial(add_kernel, 2 * half - 4), tokens, terms, came)
-    return small(last_kernel, sent, total, got[0])
+    return small(last_kernel, sent, total, got[1])
 
 
 def solution(mesh):

time: 103 us -> 102 us (level)
  waiting for transfers between devices: 21.3 us -> 15.7 us
  starting transfers between devices: 46.7 us -> 51.2 us
    ppermute x7 -> x8, waiting for transfers between devices: 17.6 us -> 12 us  [across(): lax.ppermute(a, 'head', [(2 * c + i, 2 * d + i) for c, d in both for i in...]
    ppermute x7 -> x8, starting transfers between devices: 22.3 us -> 26.9 us  [across(): lax.ppermute(a, 'head', [(2 * c + i, 2 * d + i) for c, d in both for i in...]
  transfers between devices with their start and end apart: 12 -> 13, of which waited for: 8 -> 8; matrix products, arithmetic and copies ran while one was open for 0% -> 0% of each run, Pallas kernels for 16% -> 16%
where the time goes in v8:
time: 102 us
  starting transfers between devices  51.2 us (50%)
  Pallas kernels  18.4 us (18%)
  blocking collectives  15.9 us (16%)
  waiting for transfers between devices  15.7 us (15%)
    ppermute x8, starting transfers between devices, across(): lax.ppermute(a, 'head', [(2 * c + i, 2 * d + i) for c, d in both for i in...  26.9 us
    ppermute x3, starting transfers between devices, later_z(): return lax.ppermute(a, 'ctx_0', [(i, i + by) for i in range(groups - by)])  20.4 us
    all_gather x1, blocking collectives, per_device(): gathered = lax.all_gather(maps, 'ctx_1')  15.9 us
    ppermute x8, waiting for transfers between devices, across(): lax.ppermute(a, 'head', [(2 * c + i, 2 * d + i) for c, d in both for i in...  12 us
    pallas_call x1, Pallas kernels, local_maps(): pl.pallas_call(functools.partial(map_kernel, group), out_shape=(jax.Shape...  9.36 us
    pallas_call x16, Pallas kernels, small(): pl.pallas_call(kernel, out_shape=outs, in_specs=specs or [VM] * len(args)...  7.27 us
    ppermute x2, starting transfers between devices, mate(): return lax.ppermute(a, 'head', [(i, i ^ 1) for i in range(devices)])  3.98 us
    ppermute x3, waiting for transfers between devices, later_z(): return lax.ppermute(a, 'ctx_0', [(i, i + by) for i in range(groups - by)])  2.18 us
  transfers between devices with their start and end apart: 13, of which 8 were waited for; matrix products, arithmetic and copies ran while one was open for 0% of the time, Pallas kernels for 16%

profile of v8, /device:TPU:6, one launch (start us, length us, event | category | flops | bytes accessed | tf_op | source)
XLA Modules:
  0.0 101.6 jit_solution(18044284723493851924)
XLA Ops:
  0.0 0.0 copy-start
  0.0 0.0 copy-start.1
  0.0 0.0 copy-start.2
  0.0 0.0 copy-start.3
  0.0 2.1 %collective-permute-start.2 = (bf16[256,4096]{1,0:T(8,128)(2,1)}, bf16[256,4096]{1,0:T(8,128)(2,1)}, u32[]{:S(2)}, u32[]{:S(2)}) collective-permute-start(bf16[256,4096]{1,0:T(8,128)(2,1)} %w_ref.1), channel_id=1, source_target_pairs={{0,1},{1,0},{2,3},{3,2},{4,5},{5,4},{6,7},{7,6},{8,9},{9,8},{10,11... | collective-permute-start | bytes 6291464 | tf_op jit(solution)/shard_map/ppermute | solution.py:384
  2.1 9.4 %shard_map.64 = (bf16[2,128,256]{2,1,0:T(8,128)(2,1)S(1)}, bf16[16,128,256]{2,1,0:T(8,128)(2,1)S(1)}, f32[16,2,128]{2,1,0:T(2,128)S(1)}, bf16[16,128,256]{2,1,0:T(8,128)(2,1)S(1)}, f32[16,128,128]{2,1,0:T(8,128)S(1)}) custom-call(bf16[2,512,256]{2,1,0:T(8,128)(2,1)} %k_ref.1, bf16[2,512,256]{2,1,0:T(8,128)(2,1)} %v_ref.1, f32[2,2,512]{2,1,0:T(2,128)} %b_hbm.1), custom_call_target="tpu_custom_call" | custom-call | tf_op jit(solution)/shard_map/pallas_call | solution.py:157
  11.5 15.9 %all-gather = bf16[8,128,256]{2,1,0:T(8,128)(2,1)S(1)} all-gather(bf16[2,128,256]{2,1,0:T(8,128)(2,1)S(1)} %get-tuple-element.31), channel_id=2, replica_groups=mesh['ctx_0'=8,'ctx_1'=4,'head'=16] {'ctx_1'}, dimensions={0}, use_global_device_ids=true | all-gather | bytes 655360 | tf_op jit(solution)/shard_map/all_gather | solution.py:397
  27.4 0.6 shard_map.65
  28.0 1.8 %collective-permute-start = (bf16[2,128,256]{2,1,0:T(8,128)(2,1)S(1)}, bf16[2,128,256]{2,1,0:T(8,128)(2,1)S(1)}, u32[]{:S(2)}, u32[]{:S(2)}) collective-permute-start(bf16[2,128,256]{2,1,0:T(8,128)(2,1)S(1)} %get-tuple-element.33), channel_id=1, source_target_pairs={{0,64},{64,128},{128,192},{192,256},{256,320},{320,384},{384,448},... | collective-permute-start | bytes 393224 | tf_op jit(solution)/shard_map/ppermute | solution.py:388
  29.8 0.0 copy-done
  29.8 0.0 copy-done.1
  29.8 0.0 copy-done.2
  29.9 0.0 copy-done.3
  29.9 2.6 %shard_map.66 = (f32[512,256]{1,0:T(8,128)S(1)}, bf16[512,256]{1,0:T(8,128)(2,1)S(1)}, f32[512,256]{1,0:T(8,128)S(1)}) custom-call(bf16[512,256]{1,0:T(8,128)(2,1)S(1)} %copy-done.2, bf16[2,512,256]{2,1,0:T(8,128)(2,1)S(1)} %copy-done, bf16[2,512,256]{2,1,0:T(8,128)(2,1)S(1)} %copy-done.1, bf16[512,256]{1,0:T(8,128)(2,1)S(1)} %copy-done.3, ...), custom_call_target="tpu_custom_call" | custom-call | tf_op jit(solution)/shard_map/pallas_call | solution.py:295
  32.5 0.0 collective-permute-done.earlier_ref.near_ref
  32.5 0.2 shard_map.67
  32.7 6.1 %collective-permute-start.1 = (bf16[2,128,256]{2,1,0:T(8,128)(2,1)S(1)}, bf16[2,128,256]{2,1,0:T(8,128)(2,1)S(1)}, u32[]{:S(2)}, u32[]{:S(2)}) collective-permute-start(bf16[2,128,256]{2,1,0:T(8,128)(2,1)S(1)} %get-tuple-element.42), channel_id=1, source_target_pairs={{0,128},{64,192},{128,256},{192,320},{256,384},{320,448},{1,129},{... | collective-permute-start | bytes 393224 | tf_op jit(solution)/shard_map/ppermute | solution.py:388
  38.8 0.0 collective-permute-done.2.x_ref
  38.8 1.8 %shard_map.68.w_ref = bf16[8,512,256]{2,1,0:T(8,128)(2,1)S(1)} custom-call(s32[1]{0:T(128)} %bitcast.2.me_ref, bf16[256,4096]{1,0:T(8,128)(2,1)} %w_ref.1, bf16[256,4096]{1,0:T(8,128)(2,1)} %collective-permute-done.2.x_ref), custom_call_target="tpu_custom_call" | custom-call | tf_op jit(solution)/shard_map/pallas_call | solution.py:324
  40.6 0.7 collective-permute-done.1.far_ref.earlier_ref
  41.3 0.2 shard_map.70
  41.4 12.5 %collective-permute-start.3 = (bf16[2,128,128]{2,1,0:T(8,128)(2,1)S(1)}, bf16[2,128,128]{2,1,0:T(8,128)(2,1)S(1)}, u32[]{:S(2)}, u32[]{:S(2)}) collective-permute-start(bf16[2,128,128]{2,1,0:T(8,128)(2,1)S(1)} %shard_map.70), channel_id=1, source_target_pairs={{0,256},{64,320},{128,384},{192,448},{1,257},{65,321},{129,385},{1... | collective-permute-start | bytes 196616 | tf_op jit(solution)/shard_map/ppermute | solution.py:388
  54.0 0.4 shard_map.69.entry_ref
  54.4 1.5 %collective-permute-done.3.state_ref = bf16[2,128,128]{2,1,0:T(8,128)(2,1)S(1)} collective-permute-done((bf16[2,128,128]{2,1,0:T(8,128)(2,1)S(1)}, bf16[2,128,128]{2,1,0:T(8,128)(2,1)S(1)}, u32[]{:S(2)}, u32[]{:S(2)}) %collective-permute-start.3) | collective-permute-done | bytes 65568 | tf_op jit(solution)/shard_map/ppermute | solution.py:388
  55.9 0.5 shard_map.71.a_ref
  56.4 1.9 %collective-permute-start.4 = (bf16[512,256]{1,0:T(8,128)(2,1)S(1)}, bf16[512,256]{1,0:T(8,128)(2,1)S(1)}, u32[]{:S(2)}, u32[]{:S(2)}) collective-permute-start(bf16[512,256]{1,0:T(8,128)(2,1)S(1)} %shard_map.71.a_ref), channel_id=1, source_target_pairs={{0,1},{1,0},{2,3},{3,2},{4,5},{5,4},{6,7},{7,6},{8,9},{9,8},{10,11... | collective-permute-start | bytes 786440 | tf_op jit(solution)/shard_map/ppermute | solution.py:384
  58.3 1.5 %collective-permute-done.4.b_ref = bf16[512,256]{1,0:T(8,128)(2,1)S(1)} collective-permute-done((bf16[512,256]{1,0:T(8,128)(2,1)S(1)}, bf16[512,256]{1,0:T(8,128)(2,1)S(1)}, u32[]{:S(2)}, u32[]{:S(2)}) %collective-permute-start.4) | collective-permute-done | bytes 262176 | tf_op jit(solution)/shard_map/ppermute | solution.py:384
  59.8 0.3 shard_map.72
  60.1 3.5 %collective-permute-start.6 = (bf16[256,256]{1,0:T(8,128)(2,1)S(1)}, bf16[256,256]{1,0:T(8,128)(2,1)S(1)}, u32[]{:S(2)}, u32[]{:S(2)}) collective-permute-start(bf16[256,256]{1,0:T(8,128)(2,1)S(1)} %get-tuple-element.49), channel_id=1, source_target_pairs={{0,2},{1,3},{4,6},{5,7},{8,10},{9,11},{12,14},{13,15},{2,0},{3,1},... | collective-permute-start | bytes 393224 | tf_op jit(solution)/shard_map/ppermute | solution.py:381
  63.6 5.2 %collective-permute-start.5 = (bf16[256,256]{1,0:T(8,128)(2,1)S(1)}, bf16[256,256]{1,0:T(8,128)(2,1)S(1)}, u32[]{:S(2)}, u32[]{:S(2)}) collective-permute-start(bf16[256,256]{1,0:T(8,128)(2,1)S(1)} %get-tuple-element.48), channel_id=1, source_target_pairs={{2,4},{3,5},{6,8},{7,9},{10,12},{11,13},{14,0},{15,1},{4,2},{5,3},... | collective-permute-start | bytes 393224 | tf_op jit(solution)/shard_map/ppermute | solution.py:381
  68.8 0.0 collective-permute-done.6.got_ref
  68.8 0.3 shard_map.73
  69.1 4.2 %collective-permute-start.7 = (bf16[512,256]{1,0:T(8,128)(2,1)S(1)}, bf16[512,256]{1,0:T(8,128)(2,1)S(1)}, u32[]{:S(2)}, u32[]{:S(2)}) collective-permute-start(bf16[512,256]{1,0:T(8,128)(2,1)S(1)} %shard_map.73), channel_id=1, source_target_pairs={{2,4},{3,5},{6,8},{7,9},{10,12},{11,13},{14,0},{15,1},{4,2},{5,3},... | collective-permute-start | bytes 786440 | tf_op jit(solution)/shard_map/ppermute | solution.py:381
  73.3 0.0 collective-permute-done.5.got_ref
  73.3 0.3 shard_map.74
  73.6 1.9 %collective-permute-start.9 = (bf16[512,256]{1,0:T(8,128)(2,1)S(1)}, bf16[512,256]{1,0:T(8,128)(2,1)S(1)}, u32[]{:S(2)}, u32[]{:S(2)}) collective-permute-start(bf16[512,256]{1,0:T(8,128)(2,1)S(1)} %shard_map.74), channel_id=1, source_target_pairs={{0,2},{1,3},{4,6},{5,7},{8,10},{9,11},{12,14},{13,15},{2,0},{3,1},... | collective-permute-start | bytes 786440 | tf_op jit(solution)/shard_map/ppermute | solution.py:381
  75.5 0.9 shard_map.75.terms_ref
  76.4 3.6 %collective-permute-done.7.got_ref = bf16[512,256]{1,0:T(8,128)(2,1)S(1)} collective-permute-done((bf16[512,256]{1,0:T(8,128)(2,1)S(1)}, bf16[512,256]{1,0:T(8,128)(2,1)S(1)}, u32[]{:S(2)}, u32[]{:S(2)}) %collective-permute-start.7) | collective-permute-done | bytes 262176 | tf_op jit(solution)/shard_map/ppermute | solution.py:381
  80.0 0.1 shard_map.76
  80.1 1.9 %collective-permute-start.8 = (bf16[512,256]{1,0:T(8,128)(2,1)S(1)}, bf16[512,256]{1,0:T(8,128)(2,1)S(1)}, u32[]{:S(2)}, u32[]{:S(2)}) collective-permute-start(bf16[512,256]{1,0:T(8,128)(2,1)S(1)} %shard_map.76), channel_id=1, source_target_pairs={{0,2},{1,3},{4,6},{5,7},{8,10},{9,11},{12,14},{13,15},{2,0},{3,1},... | collective-permute-start | bytes 786440 | tf_op jit(solution)/shard_map/ppermute | solution.py:381
  82.0 0.7 collective-permute-done.9.got_ref
  82.7 0.1 shard_map.77
  82.8 3.8 %collective-permute-start.11 = (bf16[512,256]{1,0:T(8,128)(2,1)S(1)}, bf16[512,256]{1,0:T(8,128)(2,1)S(1)}, u32[]{:S(2)}, u32[]{:S(2)}) collective-permute-start(bf16[512,256]{1,0:T(8,128)(2,1)S(1)} %shard_map.77), channel_id=1, source_target_pairs={{2,4},{3,5},{6,8},{7,9},{10,12},{11,13},{14,0},{15,1},{4,2},{5,3},... | collective-permute-start | bytes 786440 | tf_op jit(solution)/shard_map/ppermute | solution.py:381
  86.6 2.2 %collective-permute-done.8.got_ref = bf16[512,256]{1,0:T(8,128)(2,1)S(1)} collective-permute-done((bf16[512,256]{1,0:T(8,128)(2,1)S(1)}, bf16[512,256]{1,0:T(8,128)(2,1)S(1)}, u32[]{:S(2)}, u32[]{:S(2)}) %collective-permute-start.8) | collective-permute-done | bytes 262176 | tf_op jit(solution)/shard_map/ppermute | solution.py:381
  88.9 3.6 %collective-permute-start.10 = (bf16[512,256]{1,0:T(8,128)(2,1)S(1)}, bf16[512,256]{1,0:T(8,128)(2,1)S(1)}, u32[]{:S(2)}, u32[]{:S(2)}) collective-permute-start(bf16[512,256]{1,0:T(8,128)(2,1)S(1)} %shard_map.78), channel_id=1, source_target_pairs={{2,4},{3,5},{6,8},{7,9},{10,12},{11,13},{14,0},{15,1},{4,2},{5,3},... | collective-permute-start | bytes 786440 | tf_op jit(solution)/shard_map/ppermute | solution.py:381
  92.5 0.0 collective-permute-done.11.got_ref
  92.6 2.8 %collective-permute-start.12 = (bf16[512,256]{1,0:T(8,128)(2,1)S(1)}, bf16[512,256]{1,0:T(8,128)(2,1)S(1)}, u32[]{:S(2)}, u32[]{:S(2)}) collective-permute-start(bf16[512,256]{1,0:T(8,128)(2,1)S(1)} %shard_map.79), channel_id=1, source_target_pairs={{0,2},{1,3},{4,6},{5,7},{8,10},{9,11},{12,14},{13,15},{2,0},{3,1},... | collective-permute-start | bytes 786440 | tf_op jit(solution)/shard_map/ppermute | solution.py:381
  95.4 3.0 %collective-permute-done.10.got_ref = bf16[512,256]{1,0:T(8,128)(2,1)S(1)} collective-permute-done((bf16[512,256]{1,0:T(8,128)(2,1)S(1)}, bf16[512,256]{1,0:T(8,128)(2,1)S(1)}, u32[]{:S(2)}, u32[]{:S(2)}) %collective-permute-start.10) | collective-permute-done | bytes 262176 | tf_op jit(solution)/shard_map/ppermute | solution.py:381
  98.4 2.4 %collective-permute-done.12.got_ref = bf16[512,256]{1,0:T(8,128)(2,1)S(1)} collective-permute-done((bf16[512,256]{1,0:T(8,128)(2,1)S(1)}, bf16[512,256]{1,0:T(8,128)(2,1)S(1)}, u32[]{:S(2)}, u32[]{:S(2)}) %collective-permute-start.12) | collective-permute-done | bytes 262176 | tf_op jit(solution)/shard_map/ppermute | solution.py:381
  100.8 0.7 shard_map.81
  (3 shorter events, 0.1 us)
Async XLA Ops:
  0.0 29.8 %copy-start = (bf16[2,512,256]{2,1,0:T(8,128)(2,1)S(1)}, bf16[2,512,256]{2,1,0:T(8,128)(2,1)}, u32[]{:S(2)}) copy-start(bf16[2,512,256]{2,1,0:T(8,128)(2,1)} %k_ref.1) | copy-start | bytes 1572868
  0.0 29.8 %copy-start.1 = (bf16[2,512,256]{2,1,0:T(8,128)(2,1)S(1)}, bf16[2,512,256]{2,1,0:T(8,128)(2,1)}, u32[]{:S(2)}) copy-start(bf16[2,512,256]{2,1,0:T(8,128)(2,1)} %v_ref.1) | copy-start | bytes 1572868
  0.0 29.8 %copy-start.2 = (bf16[512,256]{1,0:T(8,128)(2,1)S(1)}, bf16[512,256]{1,0:T(8,128)(2,1)}, u32[]{:S(2)}) copy-start(bf16[512,256]{1,0:T(8,128)(2,1)} %q_ref.1) | copy-start | bytes 786436
  0.0 29.8 %copy-start.3 = (bf16[512,256]{1,0:T(8,128)(2,1)S(1)}, bf16[512,256]{1,0:T(8,128)(2,1)}, u32[]{:S(2)}) copy-start(bf16[512,256]{1,0:T(8,128)(2,1)} %g_ref.1) | copy-start | bytes 786436
  0.0 38.8 %collective-permute-start.2 = (bf16[256,4096]{1,0:T(8,128)(2,1)}, bf16[256,4096]{1,0:T(8,128)(2,1)}, u32[]{:S(2)}, u32[]{:S(2)}) collective-permute-start(bf16[256,4096]{1,0:T(8,128)(2,1)} %w_ref.1), channel_id=1, source_target_pairs={{0,1},{1,0},{2,3},{3,2},{4,5},{5,4},{6,7},{7,6},{8,9},{9,8},{10,11... | collective-permute-start | bytes 6291464 | tf_op jit(solution)/shard_map/ppermute | solution.py:384
  28.0 4.5 %collective-permute-start = (bf16[2,128,256]{2,1,0:T(8,128)(2,1)S(1)}, bf16[2,128,256]{2,1,0:T(8,128)(2,1)S(1)}, u32[]{:S(2)}, u32[]{:S(2)}) collective-permute-start(bf16[2,128,256]{2,1,0:T(8,128)(2,1)S(1)} %get-tuple-element.33), channel_id=1, source_target_pairs={{0,64},{64,128},{128,192},{192,256},{256,320},{320,384},{384,448},... | collective-permute-start | bytes 393224 | tf_op jit(solution)/shard_map/ppermute | solution.py:388
  32.7 8.6 %collective-permute-start.1 = (bf16[2,128,256]{2,1,0:T(8,128)(2,1)S(1)}, bf16[2,128,256]{2,1,0:T(8,128)(2,1)S(1)}, u32[]{:S(2)}, u32[]{:S(2)}) collective-permute-start(bf16[2,128,256]{2,1,0:T(8,128)(2,1)S(1)} %get-tuple-element.42), channel_id=1, source_target_pairs={{0,128},{64,192},{128,256},{192,320},{256,384},{320,448},{1,129},{... | collective-permute-start | bytes 393224 | tf_op jit(solution)/shard_map/ppermute | solution.py:388
  41.4 14.4 %collective-permute-start.3 = (bf16[2,128,128]{2,1,0:T(8,128)(2,1)S(1)}, bf16[2,128,128]{2,1,0:T(8,128)(2,1)S(1)}, u32[]{:S(2)}, u32[]{:S(2)}) collective-permute-start(bf16[2,128,128]{2,1,0:T(8,128)(2,1)S(1)} %shard_map.70), channel_id=1, source_target_pairs={{0,256},{64,320},{128,384},{192,448},{1,257},{65,321},{129,385},{1... | collective-permute-start | bytes 196616 | tf_op jit(solution)/shard_map/ppermute | solution.py:388
  56.4 3.4 %collective-permute-start.4 = (bf16[512,256]{1,0:T(8,128)(2,1)S(1)}, bf16[512,256]{1,0:T(8,128)(2,1)S(1)}, u32[]{:S(2)}, u32[]{:S(2)}) collective-permute-start(bf16[512,256]{1,0:T(8,128)(2,1)S(1)} %shard_map.71.a_ref), channel_id=1, source_target_pairs={{0,1},{1,0},{2,3},{3,2},{4,5},{5,4},{6,7},{7,6},{8,9},{9,8},{10,11... | collective-permute-start | bytes 786440 | tf_op jit(solution)/shard_map/ppermute | solution.py:384
  60.1 8.7 %collective-permute-start.6 = (bf16[256,256]{1,0:T(8,128)(2,1)S(1)}, bf16[256,256]{1,0:T(8,128)(2,1)S(1)}, u32[]{:S(2)}, u32[]{:S(2)}) collective-permute-start(bf16[256,256]{1,0:T(8,128)(2,1)S(1)} %get-tuple-element.49), channel_id=1, source_target_pairs={{0,2},{1,3},{4,6},{5,7},{8,10},{9,11},{12,14},{13,15},{2,0},{3,1},... | collective-permute-start | bytes 393224 | tf_op jit(solution)/shard_map/ppermute | solution.py:381
  63.6 9.6 %collective-permute-start.5 = (bf16[256,256]{1,0:T(8,128)(2,1)S(1)}, bf16[256,256]{1,0:T(8,128)(2,1)S(1)}, u32[]{:S(2)}, u32[]{:S(2)}) collective-permute-start(bf16[256,256]{1,0:T(8,128)(2,1)S(1)} %get-tuple-element.48), channel_id=1, source_target_pairs={{2,4},{3,5},{6,8},{7,9},{10,12},{11,13},{14,0},{15,1},{4,2},{5,3},... | collective-permute-start | bytes 393224 | tf_op jit(solution)/shard_map/ppermute | solution.py:381
  69.1 10.9 %collective-permute-start.7 = (bf16[512,256]{1,0:T(8,128)(2,1)S(1)}, bf16[512,256]{1,0:T(8,128)(2,1)S(1)}, u32[]{:S(2)}, u32[]{:S(2)}) collective-permute-start(bf16[512,256]{1,0:T(8,128)(2,1)S(1)} %shard_map.73), channel_id=1, source_target_pairs={{2,4},{3,5},{6,8},{7,9},{10,12},{11,13},{14,0},{15,1},{4,2},{5,3},... | collective-permute-start | bytes 786440 | tf_op jit(solution)/shard_map/ppermute | solution.py:381
  73.6 9.1 %collective-permute-start.9 = (bf16[512,256]{1,0:T(8,128)(2,1)S(1)}, bf16[512,256]{1,0:T(8,128)(2,1)S(1)}, u32[]{:S(2)}, u32[]{:S(2)}) collective-permute-start(bf16[512,256]{1,0:T(8,128)(2,1)S(1)} %shard_map.74), channel_id=1, source_target_pairs={{0,2},{1,3},{4,6},{5,7},{8,10},{9,11},{12,14},{13,15},{2,0},{3,1},... | collective-permute-start | bytes 786440 | tf_op jit(solution)/shard_map/ppermute | solution.py:381
  80.1 8.8 %collective-permute-start.8 = (bf16[512,256]{1,0:T(8,128)(2,1)S(1)}, bf16[512,256]{1,0:T(8,128)(2,1)S(1)}, u32[]{:S(2)}, u32[]{:S(2)}) collective-permute-start(bf16[512,256]{1,0:T(8,128)(2,1)S(1)} %shard_map.76), channel_id=1, source_target_pairs={{0,2},{1,3},{4,6},{5,7},{8,10},{9,11},{12,14},{13,15},{2,0},{3,1},... | collective-permute-start | bytes 786440 | tf_op jit(solution)/shard_map/ppermute | solution.py:381
  82.8 9.7 %collective-permute-start.11 = (bf16[512,256]{1,0:T(8,128)(2,1)S(1)}, bf16[512,256]{1,0:T(8,128)(2,1)S(1)}, u32[]{:S(2)}, u32[]{:S(2)}) collective-permute-start(bf16[512,256]{1,0:T(8,128)(2,1)S(1)} %shard_map.77), channel_id=1, source_target_pairs={{2,4},{3,5},{6,8},{7,9},{10,12},{11,13},{14,0},{15,1},{4,2},{5,3},... | collective-permute-start | bytes 786440 | tf_op jit(solution)/shard_map/ppermute | solution.py:381
  88.9 9.5 %collective-permute-start.10 = (bf16[512,256]{1,0:T(8,128)(2,1)S(1)}, bf16[512,256]{1,0:T(8,128)(2,1)S(1)}, u32[]{:S(2)}, u32[]{:S(2)}) collective-permute-start(bf16[512,256]{1,0:T(8,128)(2,1)S(1)} %shard_map.78), channel_id=1, source_target_pairs={{2,4},{3,5},{6,8},{7,9},{10,12},{11,13},{14,0},{15,1},{4,2},{5,3},... | collective-permute-start | bytes 786440 | tf_op jit(solution)/shard_map/ppermute | solution.py:381
  92.6 8.3 %collective-permute-start.12 = (bf16[512,256]{1,0:T(8,128)(2,1)S(1)}, bf16[512,256]{1,0:T(8,128)(2,1)S(1)}, u32[]{:S(2)}, u32[]{:S(2)}) collective-permute-start(bf16[512,256]{1,0:T(8,128)(2,1)S(1)} %shard_map.79), channel_id=1, source_target_pairs={{0,2},{1,3},{4,6},{5,7},{8,10},{9,11},{12,14},{13,15},{2,0},{3,1},... | collective-permute-start | bytes 786440 | tf_op jit(solution)/shard_map/ppermute | solution.py:381
